TPU v7x, 512 devices: a whole 4x8x8 slice. The times are simulated.
512 devices in a mesh: tile: 128 (over y, z, core), mem: 4 (over x).
Axes of the slice: x: 4, y: 8, z: 8, core: 2. Of those that a mesh axis runs over, the one named last changes fastest.
Arguments:
- radiance: bfloat16 [3072, 80, 4352], P('tile', 'mem'), may hold values from -6 to 6
- observed: bfloat16 [3072, 4352], P('tile', 'mem'), may hold values from -6 to 6
- basis: bfloat16 [4352, 300], P('mem'), may hold values from -0.09375 to 0.09375
- precision_pc: float32 [300], replicated, may hold values from 0.002 to 0.02
- tile_lists: int32 [3072, 3], P('tile'), may hold values from 0 to 127, all different within a row; in each aligned block of 24 rows (0 to 23, 24 to 47, ...) at most 2 rows name the same one
- radius_bins: int32 [3072, 3], P('tile'), may hold values from 0 to 7
Outputs:
- analysis: bfloat16 [3072, 80, 300], P('tile', 'mem')
Inputs may be any that keep to these rules, and one draw needn't show every extreme that they name: `tile_lists`: each row names 3 different tiles; within the rows of one swath no tile is named more than 2 times.
All inputs are finite; a program needn't handle non-finite values. Where the computation divides by a largest or mean magnitude, that divisor is 1e-20 or more.
Results may differ from a plain program's by a relative error of at most 0.0011.
The roundings to bfloat16 on the way count: a program that leaves them out, or rounds other values in their place, can miss the bound.
Values may be sent and summed in bfloat16 or wider, within the bound.
No kernel may reach another device: no remote copies, remote signals or barrier semaphores. Data moves between devices by JAX's collectives and lax.ppermute only.
A program may use at most 128 MiB of HBM per device.

v0:
```python
import jax
import jax.numpy as jnp
from jax import lax
from jax.sharding import PartitionSpec as P

NS_ITERS = 4


bin_spread = 3.0


def localization(radius_bins):
    scaled = radius_bins.astype(jnp.float32) / bin_spread
    return jnp.exp(-0.5 * scaled * scaled)


def square_root_weights(gram, pull):
    highest = lax.Precision.HIGHEST
    order = gram.shape[0]
    identity = jnp.eye(order, dtype=jnp.float32)
    symmetric = 0.5 * (gram + gram.T)
    scaled = identity + symmetric / (order - 1.0)
    bound = jnp.max(jnp.sum(jnp.abs(scaled), axis=1))
    root_iter = scaled / bound
    inverse_iter = identity
    for sweep in range(NS_ITERS):
        factor = 1.5 * identity - 0.5 * jnp.dot(inverse_iter, root_iter, precision=highest)
        root_iter = jnp.dot(root_iter, factor, precision=highest)
        inverse_iter = jnp.dot(factor, inverse_iter, precision=highest)
    spread = inverse_iter / jnp.sqrt(bound)
    inverse = jnp.dot(inverse_iter, inverse_iter, precision=highest) / (bound * (order - 1.0))
    offset = jnp.dot(inverse, pull, precision=highest)
    return spread + offset[:, None]


def body(radiance, observed, basis, precision_pc, tile_lists, radius_bins):
    highest = lax.Precision.HIGHEST
    obs_count, member_count, channels = radiance.shape
    components = basis.shape[1]
    tiles = lax.axis_size("tile")
    groups = lax.axis_size("mem")
    members = member_count * groups
    fanout = tile_lists.shape[1]
    capacity = max(2, (2 * obs_count * fanout + tiles - 1) // tiles)
    slot_total = tiles * capacity
    pair_total = obs_count * fanout
    flat_rad = radiance.reshape(obs_count * member_count, channels)
    scores = jnp.dot(
        flat_rad,
        lax.all_gather(basis, "mem", axis=0, tiled=True),
        preferred_element_type=jnp.float32,
    )
    scores = scores.reshape(obs_count, member_count, components)
    obs_partial = jnp.dot(observed, basis, preferred_element_type=jnp.float32)
    member_sum, obs_score = lax.psum((jnp.sum(scores, axis=1), obs_partial), "mem")
    member_mean = member_sum / members
    innovation = (obs_score - member_mean).astype(jnp.bfloat16)
    perturbed = (scores - member_mean[:, None, :]).astype(jnp.bfloat16)
    everyone = lax.all_gather(perturbed, "mem", axis=1, tiled=True)
    targets = tile_lists.reshape(pair_total)
    tile_ids = jnp.arange(tiles, dtype=jnp.int32)
    matches = (targets[:, None] == tile_ids[None, :]).astype(jnp.int32)
    earlier = jnp.cumsum(matches, axis=0) - matches
    position = jnp.sum(earlier * matches, axis=1)
    slot_of = targets * capacity + position
    placed = (jnp.arange(slot_total, dtype=jnp.int32)[:, None] == slot_of[None, :]).astype(
        jnp.float32
    )
    weights_loc = localization(radius_bins)
    rounded_loc = weights_loc.astype(jnp.bfloat16)
    member_index = lax.axis_index("mem")
    by_footprint = jnp.sum(placed.reshape(slot_total, obs_count, fanout), axis=2).astype(
        jnp.bfloat16
    )
    send_pert = jnp.dot(
        by_footprint,
        perturbed.reshape(obs_count, member_count * components),
        preferred_element_type=jnp.float32,
    ).astype(jnp.bfloat16)
    send_innov = jnp.dot(by_footprint, innovation, preferred_element_type=jnp.float32).astype(
        jnp.bfloat16
    )
    send_loc = jnp.dot(
        placed, rounded_loc.reshape(pair_total).astype(jnp.float32), precision=highest
    ).astype(jnp.bfloat16)
    got_pert, got_innov, got_loc = (
        lax.all_to_all(
            send_pert.reshape(tiles, capacity, member_count, components),
            "tile",
            split_axis=0,
            concat_axis=0,
            tiled=True,
        ),
        lax.all_to_all(
            send_innov.reshape(tiles, capacity, components),
            "tile",
            split_axis=0,
            concat_axis=0,
            tiled=True,
        ),
        lax.all_to_all(
            send_loc.reshape(tiles, capacity), "tile", split_axis=0, concat_axis=0, tiled=True
        ),
    )
    got_pert = got_pert.reshape(slot_total, member_count, components)
    got_innov = got_innov.reshape(slot_total, components)
    got_loc = got_loc.reshape(slot_total).astype(jnp.float32)
    pc_share = components // groups
    by_member = lax.all_to_all(got_pert, "mem", split_axis=2, concat_axis=1, tiled=True)
    precision_part = lax.dynamic_slice_in_dim(precision_pc, member_index * pc_share, pc_share, 0)
    innov_part = lax.dynamic_slice_in_dim(got_innov, member_index * pc_share, pc_share, 1)
    factor = got_loc[:, None] * precision_part[None, :]
    weighted = (by_member.astype(jnp.float32) * factor[:, None, :]).astype(jnp.bfloat16)
    gram_part = jnp.einsum("skp,smp->km", weighted, by_member, preferred_element_type=jnp.float32)
    pull_part = jnp.einsum("skp,sp->k", weighted, innov_part, preferred_element_type=jnp.float32)
    gram, pull = lax.psum((gram_part, pull_part), "mem")
    whole_weights = square_root_weights(gram, pull)
    own_columns = lax.dynamic_slice_in_dim(
        whole_weights, member_index * member_count, member_count, 1
    )
    coef = (weights_loc / jnp.sum(weights_loc, axis=1, keepdims=True)).reshape(pair_total)
    outgoing = jnp.broadcast_to(
        own_columns.reshape(1, 1, members * member_count), (tiles, capacity, members * member_count)
    )
    returned = lax.all_to_all(outgoing, "tile", split_axis=0, concat_axis=0, tiled=True).reshape(
        slot_total, members * member_count
    )
    blend_matrix = jnp.sum(
        (placed * coef[None, :]).reshape(slot_total, obs_count, fanout), axis=2
    ).T
    blended = jnp.dot(blend_matrix, returned, precision=highest).reshape(
        obs_count, members, member_count
    )
    mixed = jnp.einsum("omp,omk->okp", everyone.astype(jnp.float32), blended, precision=highest)
    return (member_mean[:, None, :] + mixed).astype(jnp.bfloat16)


def solution(mesh):
    placed = (
        P("tile", "mem", None),
        P("tile", "mem"),
        P("mem", None),
        P(),
        P("tile", None),
        P("tile", None),
    )
    return jax.shard_map(
        body, mesh=mesh, in_specs=placed, out_specs=P("tile", "mem", None), check_vma=False
    )
```

profile of v0, /device:TPU:1, one launch (start us, length us, event | category | flops | bytes accessed | tf_op | source)
XLA Modules:
  0.0 403.2 jit_solution(4526454749362081001)
XLA Ops:
  11.1 18.4 %all-to-all-start.2 = ((bf16[128,1,2]{2,1,0:T(2,128)(2,1)}), bf16[128,1,2]{2,1,0:T(2,128)(2,1)S(1)}, u32[]{:S(2)}, u32[]{:S(2)}) async-start(bf16[128,1,2]{2,1,0:T(2,128)(2,1)} %all_to_all.37), calls=%async_computation.2 | async-start | bytes 131072 | tf_op jit(solution)/shard_map/all_to_all | solution.py:101
  30.5 1.4 fusion.45
  31.9 25.2 %all-gather.6.cloned.1.call-done = bf16[4,1088,300]{1,2,0:T(8,128)(2,1)} async-done(((bf16[1,1088,300]{1,2,0:T(8,128)(2,1)}), bf16[4,1088,300]{1,2,0:T(8,128)(2,1)}) %all-gather.6.cloned.1.call-update) | async-done | bytes 2611216 | tf_op jit(solution)/shard_map/all_gather | solution.py:50
  57.1 2.9 copy.83
  59.9 3.9 reshape.113
  63.9 5.4 %fusion.39 = (f32[24,300]{1,0:T(8,128)S(1)}, f32[24,20,300]{2,0,1:T(8,128)S(1)}) fusion(bf16[24,20,4352]{2,0,1:T(8,128)(2,1)} %param.6, bf16[4352,300,1]{0,1,2:T(8,128)(2,1)} %reshape.113), kind=kOutput, calls=%fused_computation.62 | convolution fusion | flops 1253512832 | bytes 7393920 | tf_op jit(solution)/shard_map/dot_general | solution.py:48
  69.2 13.0 %all-reduce.1 = (f32[24,300]{1,0:T(8,128)S(1)}, f32[24,300]{1,0:T(8,128)S(1)}) all-reduce(f32[24,300]{1,0:T(8,128)S(1)} %get-tuple-element.13, f32[24,300]{1,0:T(8,128)S(1)} %fusion.45), channel_id=1, replica_groups=mesh['tile'=128,'mem'=4] {'mem'}, use_global_device_ids=true, to_apply=%region_1.0 | all-reduce | flops 14400 | bytes 115200 | tf_op jit(solution)/shard_map/psum | solution.py:55
  83.1 2.6 convolution_convert_fusion
  85.7 3.4 copy.87
  89.2 6.0 %reshape.104 = bf16[128,2,20,300]{3,2,1,0:T(8,128)(2,1)} reshape(bf16[256,6000]{1,0:T(8,128)(2,1)S(1)} %copy.87) | data formatting | bytes 6144000 | tf_op jit(solution)/shard_map/reshape | solution.py:88
  95.2 7.3 %copy.88 = bf16[128,2,20,300]{3,1,2,0:T(2,128)(2,1)} copy(bf16[128,2,20,300]{3,2,1,0:T(8,128)(2,1)} %reshape.104) | data formatting | bytes 6144000 | tf_op jit(solution)/shard_map/reshape | solution.py:88
  102.5 18.3 %all-to-all-start = ((bf16[128,2,20,300]{3,1,2,0:T(2,128)(2,1)}), bf16[128,2,20,300]{3,1,2,0:T(2,128)(2,1)}, u32[]{:S(2)}, u32[]{:S(2)}) async-start(bf16[128,2,20,300]{3,1,2,0:T(2,128)(2,1)} %copy.88), calls=%async_computation | async-start | bytes 7864320 | tf_op jit(solution)/shard_map/all_to_all | solution.py:87
  122.1 89.1 %all-to-all-done = bf16[128,2,20,300]{3,1,2,0:T(2,128)(2,1)} async-done(((bf16[128,2,20,300]{3,1,2,0:T(2,128)(2,1)}), bf16[128,2,20,300]{3,1,2,0:T(2,128)(2,1)}, u32[]{:S(2)}, u32[]{:S(2)}) %all-to-all-start) | async-done | bytes 3072032 | tf_op jit(solution)/shard_map/all_to_all | solution.py:87
  211.1 13.8 %all-to-all-start.3 = ((bf16[128,2,300]{2,1,0:T(2,128)(2,1)}), bf16[128,2,300]{2,1,0:T(2,128)(2,1)S(1)}, u32[]{:S(2)}, u32[]{:S(2)}) async-start(bf16[128,2,300]{2,1,0:T(2,128)(2,1)} %reshape.107), calls=%async_computation.3 | async-start | bytes 393216 | tf_op jit(solution)/shard_map/all_to_all | solution.py:94
  224.9 7.9 %copy.89 = bf16[128,2,20,300]{3,1,0,2:T(2,128)(2,1)} copy(bf16[128,2,20,300]{3,1,2,0:T(2,128)(2,1)} %all-to-all-done) | data formatting | bytes 6144000 | tf_op jit(solution)/shard_map/all_to_all | solution.py:87
  232.8 9.1 %reshape.105 = bf16[256,20,300]{2,0,1:T(8,128)(2,1)} reshape(bf16[128,2,20,300]{3,1,0,2:T(2,128)(2,1)} %copy.89) | data formatting | bytes 6144000 | tf_op jit(solution)/shard_map/reshape | solution.py:105
  241.9 6.6 %copy.90 = bf16[256,20,300]{0,1,2:T(8,128)(2,1)} copy(bf16[256,20,300]{2,0,1:T(8,128)(2,1)} %reshape.105) | data formatting | bytes 6144000 | tf_op jit(solution)/shard_map/reshape | solution.py:105
  248.4 4.8 %all-to-all-start.1 = ((bf16[256,20,300]{0,1,2:T(8,128)(2,1)}), bf16[256,20,300]{0,1,2:T(8,128)(2,1)}, u32[]{:S(2)}, u32[]{:S(2)}) async-start(bf16[256,20,300]{0,1,2:T(8,128)(2,1)} %copy.90), calls=%async_computation.1 | async-start | bytes 7372800 | tf_op jit(solution)/shard_map/all_to_all | solution.py:109
  254.8 41.1 %all-to-all-done.1 = bf16[256,20,300]{0,1,2:T(8,128)(2,1)} async-done(((bf16[256,20,300]{0,1,2:T(8,128)(2,1)}), bf16[256,20,300]{0,1,2:T(8,128)(2,1)}, u32[]{:S(2)}, u32[]{:S(2)}) %all-to-all-start.1) | async-done | bytes 3072032 | tf_op jit(solution)/shard_map/all_to_all | solution.py:109
  295.9 2.7 copy.92
  298.6 0.9 multiply_convert_fusion
  299.5 1.0 fusion.18
  300.5 3.3 fusion.9
  303.8 12.2 %all-reduce = (f32[80,80]{1,0:T(8,128)S(1)}, f32[80]{0:T(128)S(1)}) all-reduce(f32[80,80]{1,0:T(8,128)S(1)} %fusion.9, f32[80]{0:T(128)S(1)} %fusion.18), channel_id=1, replica_groups=mesh['tile'=128,'mem'=4] {'mem'}, use_global_device_ids=true, to_apply=%region_7.8 | all-reduce | flops 6480 | bytes 51840 | tf_op jit(solution)/shard_map/psum | solution.py:116
  322.4 1.6 broadcast_in_dim.5
  324.0 18.8 %all-to-all-start.4 = ((f32[128,2,1600]{2,1,0:T(2,128)}), f32[128,2,1600]{2,1,0:T(2,128)S(1)}, u32[]{:S(2)}, u32[]{:S(2)}) async-start(f32[128,2,1600]{2,1,0:T(2,128)} %broadcast_in_dim.5), calls=%async_computation.4 | async-start | bytes 3407872 | tf_op jit(solution)/shard_map/all_to_all | solution.py:125
  343.6 43.0 %all-to-all-done.4 = f32[128,2,1600]{2,1,0:T(2,128)S(1)} async-done(((f32[128,2,1600]{2,1,0:T(2,128)}), f32[128,2,1600]{2,1,0:T(2,128)S(1)}, u32[]{:S(2)}, u32[]{:S(2)}) %all-to-all-start.4) | async-done | bytes 1638432 | tf_op jit(solution)/shard_map/all_to_all | solution.py:125
  386.6 1.2 reshape.109
  387.7 1.6 copy.100
  389.4 1.5 dot_general.91
  390.8 2.1 fusion.5
  393.0 2.3 fusion.7
  (64 shorter events, 15.5 us)
Async XLA Ops:
  6.5 23.9 %copy-start = (bf16[24,1088]{1,0:T(8,128)(2,1)S(1)}, bf16[24,1088]{1,0:T(8,128)(2,1)}, u32[]{:S(2)}) copy-start(bf16[24,1088]{1,0:T(8,128)(2,1)} %param.7) | copy-start | bytes 156676
  6.5 50.5 %all-gather.6.cloned.1.call-start = ((), (), s32[]{:S(2)}) async-start(), calls=%async_computation.6 | async-start | bytes 3502080 | tf_op jit(solution)/shard_map/all_gather | solution.py:50
  11.1 91.5 %all-to-all-start.2 = ((bf16[128,1,2]{2,1,0:T(2,128)(2,1)}), bf16[128,1,2]{2,1,0:T(2,128)(2,1)S(1)}, u32[]{:S(2)}, u32[]{:S(2)}) async-start(bf16[128,1,2]{2,1,0:T(2,128)(2,1)} %all_to_all.37), calls=%async_computation.2 | async-start | bytes 131072 | tf_op jit(solution)/shard_map/all_to_all | solution.py:101
  82.4 0.7 copy-start.2
  102.5 108.6 %all-to-all-start = ((bf16[128,2,20,300]{3,1,2,0:T(2,128)(2,1)}), bf16[128,2,20,300]{3,1,2,0:T(2,128)(2,1)}, u32[]{:S(2)}, u32[]{:S(2)}) async-start(bf16[128,2,20,300]{3,1,2,0:T(2,128)(2,1)} %copy.88), calls=%async_computation | async-start | bytes 7864320 | tf_op jit(solution)/shard_map/all_to_all | solution.py:87
  211.1 37.3 %all-to-all-start.3 = ((bf16[128,2,300]{2,1,0:T(2,128)(2,1)}), bf16[128,2,300]{2,1,0:T(2,128)(2,1)S(1)}, u32[]{:S(2)}, u32[]{:S(2)}) async-start(bf16[128,2,300]{2,1,0:T(2,128)(2,1)} %reshape.107), calls=%async_computation.3 | async-start | bytes 393216 | tf_op jit(solution)/shard_map/all_to_all | solution.py:94
  248.4 47.5 %all-to-all-start.1 = ((bf16[256,20,300]{0,1,2:T(8,128)(2,1)}), bf16[256,20,300]{0,1,2:T(8,128)(2,1)}, u32[]{:S(2)}, u32[]{:S(2)}) async-start(bf16[256,20,300]{0,1,2:T(8,128)(2,1)} %copy.90), calls=%async_computation.1 | async-start | bytes 7372800 | tf_op jit(solution)/shard_map/all_to_all | solution.py:109
  324.0 62.5 %all-to-all-start.4 = ((f32[128,2,1600]{2,1,0:T(2,128)}), f32[128,2,1600]{2,1,0:T(2,128)S(1)}, u32[]{:S(2)}, u32[]{:S(2)}) async-start(f32[128,2,1600]{2,1,0:T(2,128)} %broadcast_in_dim.5), calls=%async_computation.4 | async-start | bytes 3407872 | tf_op jit(solution)/shard_map/all_to_all | solution.py:125
  342.8 50.1 %all-gather.4.cloned.1.call-start = ((), (), s32[]{:S(2)}) async-start(), calls=%async_computation.5 | async-start | bytes 1843200 | tf_op jit(solution)/shard_map/all_gather | solution.py:59
  389.4 6.8 %copy-start.1 = (bf16[24,1088]{1,0:T(8,128)(2,1)S(1)}, bf16[24,1088]{1,0:T(8,128)(2,1)}, u32[]{:S(2)}) copy-start(bf16[24,1088]{1,0:T(8,128)(2,1)} %param.7) | copy-start | bytes 156676
Sparse Core Ops, SparseCore 0:
  9.5 47.5 all-gather.5
  345.8 30.1 all-gather.3
where the time goes:
time: 410 us; the launch traced here: 403 us
  waiting for transfers between devices  200 us (49%)
  starting transfers between devices  74.1 us (18%)
  local copies, waits for them, and re-layouts  60.9 us (15%)
  blocking collectives  25.3 us (6%)
  matrix products  22.2 us (5%)
  between operations  15.4 us (4%)
  other arithmetic  5.52 us (1%)
    all_to_all x1, waiting for transfers between devices, body(): lax.all_to_all(send_pert.reshape(tiles, capacity, member_count, component...  89.1 us
    all_to_all x1, waiting for transfers between devices, body(): lax.all_to_all(outgoing, 'tile', split_axis=0, concat_axis=0, tiled=True)  43 us
    all_to_all x1, waiting for transfers between devices, body(): lax.all_to_all(got_pert, 'mem', split_axis=2, concat_axis=1, tiled=True)  41.1 us
    all_gather x1, waiting for transfers between devices, body(): lax.all_gather(basis, 'mem', axis=0, tiled=True)  25.2 us
    all_to_all x1, starting transfers between devices, body(): lax.all_to_all(outgoing, 'tile', split_axis=0, concat_axis=0, tiled=True)  18.8 us
    all_to_all x1, starting transfers between devices, body(): lax.all_to_all(send_loc.reshape(tiles, capacity), 'tile', split_axis=0, c...  18.4 us
    all_to_all x1, starting transfers between devices, body(): lax.all_to_all(send_pert.reshape(tiles, capacity, member_count, component...  18.3 us
    reshape x2, local copies, waits for them, and re-layouts, body(): got_pert = got_pert.reshape(slot_total, member_count, components)  15.6 us
  transfers between devices with their start and end apart: 7, of which 4 were waited for; matrix products, arithmetic and copies ran while one was open for 17% of the time, Pallas kernels for 0%

commit v1 on v0

v1 whole, which is shorter than its diff:
```python
import jax
import jax.numpy as jnp
from jax import lax
from jax.experimental import pallas as pl
from jax.experimental.pallas import tpu as pltpu
from jax.sharding import Mesh, PartitionSpec as P

NS_ITERS = 4
bin_spread = 3.0

GROUPS = 4
MEM = 20
OBS = 24
TOP = 3
COMPS = 300
WIDE = 384
ROWS = 304
HALF = 160
SPAN = 96
BLOCK = 1088
FRAME = 1152
CHIPS = 64

F32 = jnp.float32
BF16 = jnp.bfloat16
HIGHEST = lax.Precision.HIGHEST
NT = (((1,), (1,)), ((), ()))
VMEM = pl.BlockSpec(memory_space=pltpu.VMEM)
SMEM = pl.BlockSpec(memory_space=pltpu.SMEM)
ANY = pl.BlockSpec(memory_space=pl.ANY)


def params():
    return pltpu.CompilerParams(vmem_limit_bytes=32 * 1024 * 1024)


def localization(radius_bins):
    scaled = radius_bins.astype(F32) / bin_spread
    return jnp.exp(-0.5 * scaled * scaled)


def frame_of(block):
    return pl.multiple_of(1024 * block + 128 * lax.div(block, 2), 128)


def own_kernel(place, rad, own, out):
    columns = pl.ds(frame_of(place[0]), FRAME)
    out[...] = lax.dot_general(rad[:, columns], own[...], NT, preferred_element_type=F32)


def own_call(place, rad, own):
    return pl.pallas_call(
        own_kernel,
        out_shape=jax.ShapeDtypeStruct((MEM * OBS, ROWS), F32),
        in_specs=[SMEM, VMEM, VMEM],
        out_specs=VMEM,
        compiler_params=params(),
        name="scores_own",
    )(place, rad, own)


def scores_kernel(place, rad, first, beside1, beside2, far1, far2, out, total, far):
    group, core = place[0], place[1]
    near = pl.ds(pl.multiple_of(core * (ROWS - HALF), 16), HALF)
    far[near, :] = far1[...]
    rest = ROWS - HALF
    source = pl.ds(pl.multiple_of((1 - core) * (HALF - rest), 16), rest)
    target = pl.ds(pl.multiple_of((1 - core) * HALF, 16), rest)
    far[target, :] = far2[source, :]
    step = 2 * core - 1
    blocks = (
        (beside1, lax.rem(group + step + GROUPS, GROUPS)),
        (beside2, lax.rem(group - step + GROUPS, GROUPS)),
        (far, lax.rem(group + 2, GROUPS)),
    )
    members = 10
    rows = members * OBS
    sums = jnp.zeros((OBS, ROWS), F32)
    for part in range(MEM // members):
        span = slice(part * rows, (part + 1) * rows)
        acc = first[span, :]
        for block, index in blocks:
            acc = acc + lax.dot_general(
                rad[span, pl.ds(frame_of(index), FRAME)],
                block[...],
                NT,
                preferred_element_type=F32,
            )
        block = acc.reshape(members, OBS, ROWS)
        out[part * members : (part + 1) * members, :, :] = block
        sums = sums + jnp.sum(block, axis=0)
    total[...] = sums


def scores_call(place, rad, first, beside1, beside2, far1, far2):
    return pl.pallas_call(
        scores_kernel,
        out_shape=(
            jax.ShapeDtypeStruct((MEM, OBS, ROWS), F32),
            jax.ShapeDtypeStruct((OBS, ROWS), F32),
        ),
        in_specs=[SMEM] + [VMEM] * 6,
        out_specs=(VMEM, VMEM),
        scratch_shapes=[pltpu.VMEM((ROWS, FRAME), BF16)],
        compiler_params=params(),
        name="scores",
    )(place, rad, first, beside1, beside2, far1, far2)


def widen(value):
    return jnp.concatenate([value, jnp.zeros(value.shape[:-1] + (WIDE - ROWS,), F32)], axis=-1)


def perturb_kernel(scores, totals1, totals2, out, innovation, mean):
    totals = totals1[...] + totals2[...]
    average = totals[0] / (GROUPS * MEM)
    mean[...] = widen(average)
    innovation[...] = widen(totals[1] - average).astype(BF16)
    for m in range(MEM):
        out[m, :, :] = widen(scores[m] - average).astype(BF16)


def perturb_call(scores, totals1, totals2):
    return pl.pallas_call(
        perturb_kernel,
        out_shape=(
            jax.ShapeDtypeStruct((MEM, OBS, WIDE), BF16),
            jax.ShapeDtypeStruct((OBS, WIDE), BF16),
            jax.ShapeDtypeStruct((OBS, WIDE), F32),
        ),
        in_specs=[VMEM] * 3,
        out_specs=(VMEM,) * 3,
        compiler_params=params(),
        name="perturb",
    )(scores, totals1, totals2)


def gram_kernel(place, targets, loc, precision, innov, own, p1, p2, p3, keep, send, every, rows, acc):
    core = place[1]
    rows[...] = jnp.zeros_like(rows)
    acc[...] = jnp.zeros_like(acc)
    for at, block in ((0, own), (MEM, p1), (2 * MEM, p2), (3 * MEM + 1, p3)):
        for m in range(MEM):
            wide = block[m].astype(F32)
            for g in range(OBS // 8):
                for lane in range(WIDE // 128):
                    rows[lane, pl.ds(g * 8 * SPAN + at + m, 8, stride=SPAN), :] = wide[
                        g * 8 : g * 8 + 8, lane * 128 : lane * 128 + 128
                    ]
    wide = innov[...].astype(F32)
    for g in range(OBS // 8):
        for lane in range(WIDE // 128):
            rows[lane, pl.ds(g * 8 * SPAN + 3 * MEM, 8, stride=SPAN), :] = wide[
                g * 8 : g * 8 + 8, lane * 128 : lane * 128 + 128
            ]
    live = lax.broadcasted_iota(jnp.int32, (24, 128), 0) < MEM
    fade = [
        jnp.where(live, precision[0:1, lane * 128 : lane * 128 + 128], 0.0)
        for lane in range(WIDE // 128)
    ]

    def footprint(o, carry):
        start = pl.multiple_of(o * SPAN, SPAN)
        result = None
        for lane in range(WIDE // 128):
            whole = rows[lane, pl.ds(start, SPAN), :]
            every[o, :, lane * 128 : lane * 128 + 128] = whole.astype(BF16)
            mine = whole[:24]
            weighted = jnp.concatenate(
                [mine * (loc[o * TOP + r] * fade[lane]) for r in range(TOP)], axis=0
            ).astype(BF16)
            right = jnp.concatenate([whole[:64], jnp.zeros((64, 128), F32)], axis=0).astype(BF16)
            term = lax.dot_general(weighted, right, NT, preferred_element_type=F32)
            result = term if result is None else result + term
        for r in range(TOP):
            target = targets[o * TOP + r]
            bit = lax.rem(target, 2)
            side = bit + core - 2 * bit * core
            index = side * CHIPS + lax.div(target, 2)
            part = result[24 * r : 24 * r + 24]
            acc[index, 0:8, :] += part[0:8] + pltpu.roll(part[16:24], 64, 1)
            acc[index, 8:16, :] += part[8:16]
        return carry

    lax.fori_loop(0, OBS, footprint, 0, unroll=4)
    keep[...] = acc[:CHIPS]
    send[...] = acc[CHIPS:]


def gram_call(place, targets, loc, precision, innov, own, p1, p2, p3):
    half = jax.ShapeDtypeStruct((CHIPS, 16, 128), F32)
    return pl.pallas_call(
        gram_kernel,
        out_shape=(half, half, jax.ShapeDtypeStruct((OBS, SPAN, WIDE), BF16)),
        in_specs=[SMEM] * 3 + [VMEM] * 6,
        out_specs=(VMEM,) * 3,
        scratch_shapes=[
            pltpu.VMEM((WIDE // 128, OBS * SPAN, 128), F32),
            pltpu.VMEM((2 * CHIPS, 16, 128), F32),
        ],
        compiler_params=params(),
        name="gram",
    )(place, targets, loc, precision, innov, own, p1, p2, p3)


def root_kernel(place, gathered, out, upper):
    group = place[0]
    order = GROUPS * MEM
    lane20 = lax.broadcasted_iota(jnp.int32, (MEM, 128), 1)
    share = jnp.where(lane20 < 20, 0.5, jnp.where(lane20 < 40, 1.0, jnp.where(lane20 < 60, 0.5, 0.0)))
    upper[...] = jnp.zeros_like(upper)
    for d in range(GROUPS):
        block = gathered[lax.rem(group + d, GROUPS)]
        full = jnp.concatenate([block, pltpu.roll(block[0:8], 64, 1)[0:4]], axis=0)
        scaled = full * share
        shift = MEM * d
        placed = scaled if d == 0 else pltpu.roll(scaled, shift, 1)
        placed = jnp.where(lane20 < order, placed, 0.0)
        if d >= 2:
            wrapped = pltpu.roll(scaled, (shift - order) % 128, 1)
            placed = placed + jnp.where(lane20 < shift - 20, wrapped, 0.0)
        placed = placed + jnp.where(lane20 == order, pltpu.roll(full, 20, 1), 0.0)
        upper[shift : shift + MEM, :] = placed
    half = upper[...]
    flipped = half.T
    row = lax.broadcasted_iota(jnp.int32, (128, 128), 0)
    lane = lax.broadcasted_iota(jnp.int32, (128, 128), 1)
    inside = (row < order) & (lane < order)
    identity = jnp.where(inside & (row == lane), 1.0, 0.0)
    symmetric = jnp.where(inside, half + flipped, 0.0)
    matrix = identity + symmetric / (order - 1.0)
    bound = jnp.max(jnp.sum(jnp.abs(matrix), axis=1, keepdims=True), axis=0, keepdims=True)
    pull = flipped[order : order + 8]
    pull = jnp.where(
        (lax.broadcasted_iota(jnp.int32, (8, 128), 1) < order)
        & (lax.broadcasted_iota(jnp.int32, (8, 128), 0) == 0),
        pull,
        0.0,
    )

    def times(a, b):
        return jnp.dot(a, b, precision=HIGHEST, preferred_element_type=F32)

    root = matrix / bound
    inverse = None
    for sweep in range(NS_ITERS):
        product = root if inverse is None else times(inverse, root)
        factor = 1.5 * identity - 0.5 * product
        if sweep < NS_ITERS - 1:
            root = times(root, factor)
        inverse = factor if inverse is None else times(factor, inverse)
    offset = times(times(pull, inverse), inverse) / (bound * (order - 1.0))
    weights = inverse[0:24] / jnp.sqrt(bound) + offset[0:1]
    lane8 = lax.broadcasted_iota(jnp.int32, (8, 128), 1)
    row8 = lax.broadcasted_iota(jnp.int32, (8, 128), 0)
    tail = jnp.where(row8 < 4, weights[16:24], 0.0)
    first = jnp.where(lane8 >= 80, pltpu.roll(tail, 80, 1), 0.0)
    second = jnp.where((lane8 >= 80) & (lane8 < 112), pltpu.roll(tail, 32, 1), 0.0)
    out[0:8, :] = weights[0:8] + first + pltpu.roll(second, 4, 0)
    out[8:16, :] = weights[8:16]


def root_call(place, gathered):
    return pl.pallas_call(
        root_kernel,
        out_shape=jax.ShapeDtypeStruct((16, 128), F32),
        in_specs=[SMEM, VMEM],
        out_specs=VMEM,
        scratch_shapes=[pltpu.VMEM((128, 128), F32)],
        compiler_params=params(),
        name="root",
    )(place, gathered)


def mix_kernel(place, targets, coef, mine, other, every, mean, out, rows):
    core = place[1]
    lane8 = lax.broadcasted_iota(jnp.int32, (8, 128), 1)
    row8 = lax.broadcasted_iota(jnp.int32, (8, 128), 0)

    def footprint(o, carry):
        blend = jnp.zeros((16, 128), F32)
        for r in range(TOP):
            target = targets[o * TOP + r]
            index = lax.div(target, 2)
            local = lax.rem(target, 2) == core
            piece = jnp.where(local, mine[index], other[index])
            blend = blend + coef[o * TOP + r] * piece
        top, middle = blend[0:8], blend[8:16]
        first = jnp.where(lane8 < 48, pltpu.roll(top, 48, 1), 0.0)
        second = jnp.where((lane8 >= 48) & (lane8 < 80), pltpu.roll(top, 96, 1), 0.0)
        tail = jnp.where(row8 < 4, first + pltpu.roll(second, 4, 0), 0.0)
        whole = jnp.concatenate(
            [jnp.where(lane8 < 80, top, 0.0), jnp.where(lane8 < 80, middle, 0.0), tail], axis=0
        )
        lane24 = lax.broadcasted_iota(jnp.int32, (24, 128), 1)
        moved = jnp.where((lane24 > 60) & (lane24 < 81), pltpu.roll(whole, 1, 1), 0.0)
        whole = jnp.where(lane24 < 60, whole, moved)
        high = whole.astype(BF16).astype(F32)
        both = jnp.concatenate([high, whole - high], axis=0).astype(BF16)
        pert = jnp.concatenate([every[o], jnp.zeros((128 - SPAN, WIDE), BF16)], axis=0)
        mixed = jnp.dot(both, pert, preferred_element_type=F32)
        mixed = mixed[0:24] + mixed[24:48] + mean[pl.ds(o, 1), :]
        for g in range(3):
            for lane in range(WIDE // 128):
                rows[lane, pl.ds(g * 8 * OBS + o, 8, stride=OBS), :] = mixed[
                    g * 8 : g * 8 + 8, lane * 128 : lane * 128 + 128
                ]
        return carry

    lax.fori_loop(0, OBS, footprint, 0, unroll=4)
    for m in range(MEM):
        wide = jnp.concatenate(
            [rows[lane, m * OBS : (m + 1) * OBS, :] for lane in range(WIDE // 128)], axis=1
        )
        out[m, :, :] = wide[:, :COMPS].astype(BF16)


def mix_call(place, targets, coef, mine, other, every, mean):
    return pl.pallas_call(
        mix_kernel,
        out_shape=jax.ShapeDtypeStruct((MEM, OBS, COMPS), BF16),
        in_specs=[SMEM] * 3 + [VMEM] * 4,
        out_specs=VMEM,
        scratch_shapes=[pltpu.VMEM((WIDE // 128, 24 * OBS, 128), F32)],
        compiler_params=params(),
        name="mix",
    )(place, targets, coef, mine, other, every, mean)


def shift(value, steps):
    return lax.ppermute(value, "mem", [(i, (i + steps) % GROUPS) for i in range(GROUPS)])


def swap(value):
    return lax.ppermute(value, "core", [(0, 1), (1, 0)])


def turn(value):
    pairs = [(i, (i + 1) % GROUPS) for i in range(GROUPS)]
    pairs += [(GROUPS + i, GROUPS + (i - 1) % GROUPS) for i in range(GROUPS)]
    return lax.ppermute(value, ("core", "mem"), pairs)


def pad_lanes(value, width):
    return jnp.pad(value, [(0, 0)] * (value.ndim - 1) + [(0, width - value.shape[-1])])


def body(radiance, observed, basis, precision_pc, tile_lists, radius_bins):
    group = lax.axis_index("mem")
    core = lax.axis_index("core")
    place = jnp.stack([group, core]).astype(jnp.int32)
    rad = jnp.transpose(radiance, (1, 0, 2)).reshape(MEM * OBS, GROUPS * BLOCK)

    turned = basis.T
    spare = ROWS - COMPS
    own = jnp.where(
        lax.rem(group, 2) == 1,
        jnp.pad(turned, ((0, spare), (FRAME - BLOCK, 0))),
        jnp.pad(turned, ((0, spare), (0, FRAME - BLOCK))),
    )
    beside1 = turn(own)
    first = own_call(place, rad, own)
    obs_partial = pad_lanes(jnp.dot(observed, basis, preferred_element_type=F32), ROWS)
    beside1, first, obs_partial = lax.optimization_barrier((beside1, first, obs_partial))
    far1 = turn(lax.dynamic_slice_in_dim(beside1, core * (ROWS - HALF), HALF, 0))
    beside2 = swap(beside1)
    far2 = swap(far1)
    scores, member_sum = scores_call(place, rad, first, beside1, beside2, far1, far2)
    totals = jnp.stack([member_sum, obs_partial])
    totals = totals + lax.ppermute(totals, "mem", [(0, 1), (1, 0), (2, 3), (3, 2)])
    across = lax.ppermute(totals, "mem", [(0, 3), (3, 0), (1, 2), (2, 1)])
    perturbed, innovation, mean = perturb_call(scores, totals, across)
    after1 = shift(perturbed, 3)
    after3 = shift(perturbed, 1)
    after2 = turn(jnp.where(core == 0, after3, after1))

    weights_loc = localization(radius_bins)
    rounded_loc = lax.reduce_precision(weights_loc, 8, 7).reshape(OBS * TOP)
    coef = (weights_loc / jnp.sum(weights_loc, axis=1, keepdims=True)).reshape(OBS * TOP)
    targets = tile_lists.reshape(OBS * TOP)
    keep, send, every = gram_call(
        place,
        targets,
        rounded_loc,
        pad_lanes(precision_pc[None], WIDE),
        innovation,
        perturbed,
        after1,
        after2,
        after3,
    )
    chip_sum = keep + swap(send)
    arrived = lax.all_to_all(chip_sum, ("y", "z"), split_axis=0, concat_axis=0, tiled=True)
    gathered = lax.all_gather(jnp.sum(arrived, axis=0), "mem", axis=0)
    weights = root_call(place, gathered)
    mine = lax.all_to_all(
        jnp.broadcast_to(weights[None], (CHIPS, 16, 128)),
        ("y", "z"),
        split_axis=0,
        concat_axis=0,
        tiled=True,
    )
    other = swap(mine)
    analysis = mix_call(place, targets, coef, mine, other, every, mean)
    return jnp.transpose(analysis, (1, 0, 2))


def solution(mesh):
    fine = Mesh(mesh.devices.reshape(8, 8, 2, GROUPS), ("y", "z", "core", "mem"))
    tile = ("y", "z", "core")
    placed = (
        P(tile, "mem", None),
        P(tile, "mem"),
        P("mem", None),
        P(),
        P(tile, None),
        P(tile, None),
    )
    return jax.shard_map(
        body, mesh=fine, in_specs=placed, out_specs=P(tile, "mem", None), check_vma=False
    )
```

time: 410 us -> 162 us (0.40); the launches traced: 403 us -> 162 us
  waiting for transfers between devices: 200 us -> 23.5 us
  local copies, waits for them, and re-layouts: 60.9 us -> 2.85 us
  blocking collectives: 25.3 us -> 58.7 us
  matrix products: 22.2 us -> 1.4 us
  starting transfers between devices: 74.1 us -> 56.3 us
  Pallas kernels: 0 us -> 16.5 us
  between operations: 15.4 us -> 0.27 us
    all_to_all x5 -> x0, waiting for transfers between devices: 173 us -> none  [the longest x1 89.1 us: body(): lax.all_to_all(send_pert.reshape(tiles, capacity, member_count, component...]
    all_to_all x5 -> x0, starting transfers between devices: 74.1 us -> none  [the longest x1 18.8 us: body(): lax.all_to_all(outgoing, 'tile', split_axis=0, concat_axis=0, tiled=True)]
    ppermute x0 -> x11, starting transfers between devices: none -> 56.3 us  [the longest x4 30.3 us: swap(): return lax.ppermute(value, 'core', [(0, 1), (1, 0)])]
    all_to_all x0 -> x2, blocking collectives: none -> 49.7 us  [the longest x1 27.4 us: body(): lax.all_to_all(chip_sum, ('y', 'z'), split_axis=0, concat_axis=0, tiled=T...]
    reshape x9 -> x3, local copies, waits for them, and re-layouts: 31.5 us -> 0.29 us  [the longest x1 0.1 us: body(): rounded_loc = lax.reduce_precision(weights_loc, 8, 7).reshape(OBS * TOP)]
    psum x2 -> x0, blocking collectives: 25.3 us -> none  [the longest x1 13 us: body(): lax.psum((jnp.sum(scores, axis=1), obs_partial), 'mem')]
    all_gather x2 -> x0, waiting for transfers between devices: 25.2 us -> none  [the longest x1 25.2 us: body(): lax.all_gather(basis, 'mem', axis=0, tiled=True)]
    ppermute x0 -> x11, waiting for transfers between devices: none -> 23.5 us  [the longest x3 6.94 us: turn(): return lax.ppermute(value, ('core', 'mem'), pairs)]
  transfers between devices with their start and end apart: 7 -> 11, of which waited for: 4 -> 9; matrix products, arithmetic and copies ran while one was open for 17% -> 1% of each run, Pallas kernels for 0% -> 1%
where the time goes in v1:
time: 162 us
  blocking collectives  58.7 us (36%)
  starting transfers between devices  56.3 us (35%)
  waiting for transfers between devices  23.5 us (15%)
  Pallas kernels  16.5 us (10%)
  local copies, waits for them, and re-layouts  2.85 us (2%)
  other arithmetic  2.07 us (1%)
    ppermute x4, starting transfers between devices, swap(): return lax.ppermute(value, 'core', [(0, 1), (1, 0)])  30.3 us
    all_to_all x1, blocking collectives, body(): lax.all_to_all(chip_sum, ('y', 'z'), split_axis=0, concat_axis=0, tiled=T...  27.4 us
    all_to_all x1, blocking collectives, body(): lax.all_to_all(jnp.broadcast_to(weights[None], (CHIPS, 16, 128)), ('y', '...  22.2 us
    ppermute x3, starting transfers between devices, turn(): return lax.ppermute(value, ('core', 'mem'), pairs)  15.7 us
    all_gather x1, blocking collectives, body(): gathered = lax.all_gather(jnp.sum(arrived, axis=0), 'mem', axis=0)  9.02 us
    ppermute x3, waiting for transfers between devices, turn(): return lax.ppermute(value, ('core', 'mem'), pairs)  6.94 us
    ppermute x2, starting transfers between devices, shift(): lax.ppermute(value, 'mem', [(i, (i + steps) % GROUPS) for i in range(GROU...  6.49 us
    pallas_call x1, Pallas kernels, gram_call(): pl.pallas_call(gram_kernel, out_shape=(half, half, jax.ShapeDtypeStruct((...  6.13 us
  transfers between devices with their start and end apart: 11, of which 9 were waited for; matrix products, arithmetic and copies ran while one was open for 1% of the time, Pallas kernels for 1%

profile of v1, /device:TPU:1, one launch (start us, length us, event | category | flops | bytes accessed | tf_op | source)
XLA Modules:
  0.0 161.6 jit_solution(14130452667169593776)
XLA Ops:
  0.0 1.8 %pad_select_fusion.own = bf16[304,1152]{1,0:T(8,128)(2,1)S(1)} fusion(bf16[300,1088]{1,0:T(8,128)(2,1)} %bitcast.17, pred[]{:T(512)S(6)} %eq.6), kind=kLoop, calls=%fused_computation | loop fusion | flops 350208 | bytes 1353217 | tf_op jit(solution)/shard_map/jit(_where)/select_n | solution.py:356
  1.8 5.2 %collective-permute-start = (bf16[304,1152]{1,0:T(8,128)(2,1)S(1)}, bf16[304,1152]{1,0:T(8,128)(2,1)S(1)}, u32[]{:S(2)}, u32[]{:S(2)}) collective-permute-start(bf16[304,1152]{1,0:T(8,128)(2,1)S(1)} %pad_select_fusion.own), channel_id=1, source_target_pairs={{0,1},{1,2},{2,3},{3,0},{4,7},{5,4},{6,5},{7,6},{8,9},{9,10},{10,1... | collective-permute-start | bytes 2101256 | tf_op jit(solution)/shard_map/ppermute | solution.py:341
  7.0 1.4 fusion.3
  8.5 2.2 %copy-done.1 = bf16[24,20,4352]{2,0,1:T(8,128)(2,1)S(1)} copy-done((bf16[24,20,4352]{2,0,1:T(8,128)(2,1)S(1)}, bf16[24,20,4352]{2,0,1:T(8,128)(2,1)}, u32[]{:S(2)}) %copy-start.1) | copy-done | bytes 4177944
  10.7 1.3 scores_own.1.first
  12.0 3.0 %collective-permute-done.beside1 = bf16[304,1152]{1,0:T(8,128)(2,1)S(1)} collective-permute-done((bf16[304,1152]{1,0:T(8,128)(2,1)S(1)}, bf16[304,1152]{1,0:T(8,128)(2,1)S(1)}, u32[]{:S(2)}, u32[]{:S(2)}) %collective-permute-start) | collective-permute-done | bytes 700448 | tf_op jit(solution)/shard_map/ppermute | solution.py:341
  15.0 5.2 %collective-permute-start.2 = (bf16[160,1152]{1,0:T(8,128)(2,1)S(1)}, bf16[160,1152]{1,0:T(8,128)(2,1)S(1)}, u32[]{:S(2)}, u32[]{:S(2)}) collective-permute-start(bf16[160,1152]{1,0:T(8,128)(2,1)S(1)} %constant_dynamic-slice_fusion), channel_id=1, source_target_pairs={{0,1},{1,2},{2,3},{3,0},{4,7},{5,4},{6,5},{7,6},{8,9},{9,10},{10,1... | collective-permute-start | bytes 1105928 | tf_op jit(solution)/shard_map/ppermute | solution.py:341
  20.2 6.6 %collective-permute-start.1 = (bf16[304,1152]{1,0:T(8,128)(2,1)S(1)}, bf16[304,1152]{1,0:T(8,128)(2,1)S(1)}, u32[]{:S(2)}, u32[]{:S(2)}) collective-permute-start(bf16[304,1152]{1,0:T(8,128)(2,1)S(1)} %collective-permute-done.beside1), channel_id=1, source_target_pairs={{0,4},{4,0},{1,5},{5,1},{2,6},{6,2},{3,7},{7,3},{8,12},{12,8},{9,1... | collective-permute-start | bytes 2101256 | tf_op jit(solution)/shard_map/ppermute | solution.py:335
  26.9 8.7 %collective-permute-start.3 = (bf16[160,1152]{1,0:T(8,128)(2,1)S(1)}, bf16[160,1152]{1,0:T(8,128)(2,1)S(1)}, u32[]{:S(2)}, u32[]{:S(2)}) collective-permute-start(bf16[160,1152]{1,0:T(8,128)(2,1)S(1)} %collective-permute-done.2.far1), channel_id=1, source_target_pairs={{0,4},{4,0},{1,5},{5,1},{2,6},{6,2},{3,7},{7,3},{8,12},{12,8},{9,1... | collective-permute-start | bytes 1105928 | tf_op jit(solution)/shard_map/ppermute | solution.py:335
  35.5 1.3 collective-permute-done.3.far2
  36.8 2.7 %scores.1 = (f32[20,24,304]{2,1,0:T(8,128)S(1)}, f32[24,304]{1,0:T(8,128)S(1)}) custom-call(s32[2]{0:T(128)S(1)} %pad_add_fusion.place, bf16[480,4352]{1,0:T(8,128)(2,1)S(1)} %bitcast.13, f32[480,304]{1,0:T(8,128)S(1)} %scores_own.1.first, bf16[304,1152]{1,0:T(8,128)(2,1)S(1)} %collective-permute-done.beside1, ...), custom_call_target="tpu_custom_call" | custom-call | tf_op jit(solution)/shard_map/scores/pallas_call | solution.py:96
  39.5 1.9 %collective-permute-start.4 = (f32[2,24,304]{2,1,0:T(8,128)S(1)}, f32[2,24,304]{2,1,0:T(8,128)S(1)}, u32[]{:S(2)}, u32[]{:S(2)}) collective-permute-start(f32[2,24,304]{2,1,0:T(8,128)S(1)} %pad_maximum_fusion), channel_id=1, source_target_pairs={{0,1},{1,0},{2,3},{3,2},{4,5},{5,4},{6,7},{7,6},{8,9},{9,8},{10,11... | collective-permute-start | bytes 175112 | tf_op jit(solution)/shard_map/ppermute | solution.py:370
  41.4 3.2 %collective-permute-done.4 = f32[2,24,304]{2,1,0:T(8,128)S(1)} collective-permute-done((f32[2,24,304]{2,1,0:T(8,128)S(1)}, f32[2,24,304]{2,1,0:T(8,128)S(1)}, u32[]{:S(2)}, u32[]{:S(2)}) %collective-permute-start.4) | collective-permute-done | bytes 58400 | tf_op jit(solution)/shard_map/ppermute | solution.py:370
  44.6 1.9 %collective-permute-start.5 = (f32[2,24,304]{2,1,0:T(8,128)S(1)}, f32[2,24,304]{2,1,0:T(8,128)S(1)}, u32[]{:S(2)}, u32[]{:S(2)}) collective-permute-start(f32[2,24,304]{2,1,0:T(8,128)S(1)} %fusion.2.totals1), channel_id=1, source_target_pairs={{0,3},{3,0},{1,2},{2,1},{4,7},{7,4},{5,6},{6,5},{8,11},{11,8},{9,1... | collective-permute-start | bytes 175112 | tf_op jit(solution)/shard_map/ppermute | solution.py:371
  46.6 4.4 %collective-permute-done.5.totals2 = f32[2,24,304]{2,1,0:T(8,128)S(1)} collective-permute-done((f32[2,24,304]{2,1,0:T(8,128)S(1)}, f32[2,24,304]{2,1,0:T(8,128)S(1)}, u32[]{:S(2)}, u32[]{:S(2)}) %collective-permute-start.5) | collective-permute-done | bytes 58400 | tf_op jit(solution)/shard_map/ppermute | solution.py:371
  51.0 1.9 %collective-permute-start.7 = (bf16[20,24,384]{2,1,0:T(8,128)(2,1)S(1)}, bf16[20,24,384]{2,1,0:T(8,128)(2,1)S(1)}, u32[]{:S(2)}, u32[]{:S(2)}) collective-permute-start(bf16[20,24,384]{2,1,0:T(8,128)(2,1)S(1)} %get-tuple-element.22.own), channel_id=1, source_target_pairs={{0,1},{1,2},{2,3},{3,0},{4,5},{5,6},{6,7},{7,4},{8,9},{9,10},{10,1... | collective-permute-start | bytes 1105928 | tf_op jit(solution)/shard_map/ppermute | solution.py:331
  52.9 4.6 %collective-permute-start.6 = (bf16[20,24,384]{2,1,0:T(8,128)(2,1)S(1)}, bf16[20,24,384]{2,1,0:T(8,128)(2,1)S(1)}, u32[]{:S(2)}, u32[]{:S(2)}) collective-permute-start(bf16[20,24,384]{2,1,0:T(8,128)(2,1)S(1)} %get-tuple-element.22.own), channel_id=1, source_target_pairs={{0,3},{1,0},{2,1},{3,2},{4,7},{5,4},{6,5},{7,6},{8,11},{9,8},{10,9... | collective-permute-start | bytes 1105928 | tf_op jit(solution)/shard_map/ppermute | solution.py:331
  57.5 4.0 %collective-permute-done.7.p3 = bf16[20,24,384]{2,1,0:T(8,128)(2,1)S(1)} collective-permute-done((bf16[20,24,384]{2,1,0:T(8,128)(2,1)S(1)}, bf16[20,24,384]{2,1,0:T(8,128)(2,1)S(1)}, u32[]{:S(2)}, u32[]{:S(2)}) %collective-permute-start.7) | collective-permute-done | bytes 368672 | tf_op jit(solution)/shard_map/ppermute | solution.py:331
  61.5 0.9 collective-permute-done.6.p1
  62.5 5.3 %collective-permute-start.8 = (bf16[20,24,384]{2,1,0:T(8,128)(2,1)S(1)}, bf16[20,24,384]{2,1,0:T(8,128)(2,1)S(1)}, u32[]{:S(2)}, u32[]{:S(2)}) collective-permute-start(bf16[20,24,384]{2,1,0:T(8,128)(2,1)S(1)} %broadcast_select_fusion), channel_id=1, source_target_pairs={{0,1},{1,2},{2,3},{3,0},{4,7},{5,4},{6,5},{7,6},{8,9},{9,10},{10,1... | collective-permute-start | bytes 1105928 | tf_op jit(solution)/shard_map/ppermute | solution.py:341
  68.0 0.1 reshape.16.loc
  68.3 4.0 %collective-permute-done.8.p2 = bf16[20,24,384]{2,1,0:T(8,128)(2,1)S(1)} collective-permute-done((bf16[20,24,384]{2,1,0:T(8,128)(2,1)S(1)}, bf16[20,24,384]{2,1,0:T(8,128)(2,1)S(1)}, u32[]{:S(2)}, u32[]{:S(2)}) %collective-permute-start.8) | collective-permute-done | bytes 368672 | tf_op jit(solution)/shard_map/ppermute | solution.py:341
  72.2 6.1 %gram.1 = (f32[64,16,128]{2,1,0:T(8,128)S(1)}, f32[64,16,128]{2,1,0:T(8,128)S(1)}, bf16[24,96,384]{2,1,0:T(8,128)(2,1)S(1)}) custom-call(s32[2]{0:T(128)S(1)} %pad_add_fusion.place, s32[72]{0:T(128)S(1)} %reshape.14.targets, f32[72]{0:T(128)S(1)} %reshape.16.loc, f32[1,384]{1,0:T(1,128)S(1)} %pad.16.precision, bf16[24,384]{1,0:T(8,128)(2,1)S(1)} %get-tuple-element.21.innov, ...), custom_call_target="tpu_custom_call" | custom-call | tf_op jit(solution)/shard_map/gram/pallas_call | solution.py:192
  78.4 7.1 %collective-permute-start.9 = (f32[64,16,128]{2,1,0:T(8,128)S(1)}, f32[64,16,128]{2,1,0:T(8,128)S(1)}, u32[]{:S(2)}, u32[]{:S(2)}) collective-permute-start(f32[64,16,128]{2,1,0:T(8,128)S(1)} %get-tuple-element.24), channel_id=1, source_target_pairs={{0,4},{4,0},{1,5},{5,1},{2,6},{6,2},{3,7},{7,3},{8,12},{12,8},{9,1... | collective-permute-start | bytes 1572872 | tf_op jit(solution)/shard_map/ppermute | solution.py:335
  85.5 1.5 collective-permute-done.9
  87.1 27.4 %all_to_all.10 = f32[64,16,128]{2,1,0:T(8,128)S(1)} all-to-all(f32[64,16,128]{2,1,0:T(8,128)S(1)} %add.19), channel_id=1, replica_groups=mesh['y'=8,'z'=8,'core'=2,'mem'=4] {'y','z'}, dimensions={0} | all-to-all | bytes 1048576 | tf_op jit(solution)/shard_map/all_to_all | solution.py:393
  114.6 9.0 %all-gather = f32[64,128]{1,0:T(8,128)S(1)} all-gather(f32[16,128]{1,0:T(8,128)S(1)} %reduce_sum.19), channel_id=2, replica_groups=mesh['y'=8,'z'=8,'core'=2,'mem'=4] {'mem'}, dimensions={0}, use_global_device_ids=true | all-gather | bytes 40960 | tf_op jit(solution)/shard_map/all_gather | solution.py:394
  123.6 2.9 %root.1 = f32[16,128]{1,0:T(8,128)S(1)} custom-call(s32[2]{0:T(128)S(1)} %pad_add_fusion.place, f32[4,16,128]{2,1,0:T(8,128)S(1)} %bitcast.16), custom_call_target="tpu_custom_call" | custom-call | tf_op jit(solution)/shard_map/root/pallas_call | solution.py:264
  126.5 22.2 %all_to_all.11.mine = f32[64,16,128]{2,1,0:T(8,128)S(1)} all-to-all(f32[64,16,128]{2,1,0:T(8,128)S(1)} %broadcast_in_dim.5), channel_id=1, replica_groups=mesh['y'=8,'z'=8,'core'=2,'mem'=4] {'y','z'}, dimensions={0} | all-to-all | bytes 1048576 | tf_op jit(solution)/shard_map/all_to_all | solution.py:396
  148.8 7.9 %collective-permute-start.10 = (f32[64,16,128]{2,1,0:T(8,128)S(1)}, f32[64,16,128]{2,1,0:T(8,128)S(1)}, u32[]{:S(2)}, u32[]{:S(2)}) collective-permute-start(f32[64,16,128]{2,1,0:T(8,128)S(1)} %all_to_all.11.mine), channel_id=1, source_target_pairs={{0,4},{4,0},{1,5},{5,1},{2,6},{6,2},{3,7},{7,3},{8,12},{12,8},{9,1... | collective-permute-start | bytes 1572872 | tf_op jit(solution)/shard_map/ppermute | solution.py:335
  156.8 1.3 collective-permute-done.10.other
  158.2 3.5 %mix.1 = bf16[20,24,300]{2,1,0:T(8,128)(2,1)} custom-call(s32[2]{0:T(128)S(1)} %pad_add_fusion.place, s32[72]{0:T(128)S(1)} %reshape.14.targets, f32[72]{0:T(128)S(1)} %reshape.15.coef, f32[64,16,128]{2,1,0:T(8,128)S(1)} %all_to_all.11.mine, f32[64,16,128]{2,1,0:T(8,128)S(1)} %collective-permute-done.10.other, ...), custom_call_target="tpu_custom_call" | custom-call | tf_op jit(solution)/shard_map/mix/pallas_call | solution.py:319
  (30 shorter events, 1.0 us)
Async XLA Ops:
  0.0 7.0 %copy-start = (bf16[24,1088]{1,0:T(8,128)(2,1)S(1)}, bf16[24,1088]{1,0:T(8,128)(2,1)}, u32[]{:S(2)}) copy-start(bf16[24,1088]{1,0:T(8,128)(2,1)} %param.7) | copy-start | bytes 156676
  1.8 13.2 %collective-permute-start = (bf16[304,1152]{1,0:T(8,128)(2,1)S(1)}, bf16[304,1152]{1,0:T(8,128)(2,1)S(1)}, u32[]{:S(2)}, u32[]{:S(2)}) collective-permute-start(bf16[304,1152]{1,0:T(8,128)(2,1)S(1)} %pad_select_fusion.own), channel_id=1, source_target_pairs={{0,1},{1,2},{2,3},{3,0},{4,7},{5,4},{6,5},{7,6},{8,9},{9,10},{10,1... | collective-permute-start | bytes 2101256 | tf_op jit(solution)/shard_map/ppermute | solution.py:341
  8.5 2.2 %copy-start.1 = (bf16[24,20,4352]{2,0,1:T(8,128)(2,1)S(1)}, bf16[24,20,4352]{2,0,1:T(8,128)(2,1)}, u32[]{:S(2)}) copy-start(bf16[24,20,4352]{2,0,1:T(8,128)(2,1)} %param.6) | copy-start | bytes 12533764
  15.0 52.8 %copy-start.4 = (f32[300]{0:T(512)S(1)}, f32[300]{0:T(512)}, u32[]{:S(2)}) copy-start(f32[300]{0:T(512)} %param.9) | copy-start | bytes 3604
  15.0 52.8 %copy-start.2 = (s32[24,3]{0,1:T(4,128)S(1)}, s32[24,3]{0,1:T(4,128)}, u32[]{:S(2)}) copy-start(s32[24,3]{0,1:T(4,128)} %param.11) | copy-start | bytes 868
  15.0 53.0 %copy-start.3 = (s32[24,3]{0,1:T(4,128)S(1)}, s32[24,3]{0,1:T(4,128)}, u32[]{:S(2)}) copy-start(s32[24,3]{0,1:T(4,128)} %param.10) | copy-start | bytes 868
  15.0 11.8 %collective-permute-start.2 = (bf16[160,1152]{1,0:T(8,128)(2,1)S(1)}, bf16[160,1152]{1,0:T(8,128)(2,1)S(1)}, u32[]{:S(2)}, u32[]{:S(2)}) collective-permute-start(bf16[160,1152]{1,0:T(8,128)(2,1)S(1)} %constant_dynamic-slice_fusion), channel_id=1, source_target_pairs={{0,1},{1,2},{2,3},{3,0},{4,7},{5,4},{6,5},{7,6},{8,9},{9,10},{10,1... | collective-permute-start | bytes 1105928 | tf_op jit(solution)/shard_map/ppermute | solution.py:341
  20.2 15.3 %collective-permute-start.1 = (bf16[304,1152]{1,0:T(8,128)(2,1)S(1)}, bf16[304,1152]{1,0:T(8,128)(2,1)S(1)}, u32[]{:S(2)}, u32[]{:S(2)}) collective-permute-start(bf16[304,1152]{1,0:T(8,128)(2,1)S(1)} %collective-permute-done.beside1), channel_id=1, source_target_pairs={{0,4},{4,0},{1,5},{5,1},{2,6},{6,2},{3,7},{7,3},{8,12},{12,8},{9,1... | collective-permute-start | bytes 2101256 | tf_op jit(solution)/shard_map/ppermute | solution.py:335
  26.9 10.0 %collective-permute-start.3 = (bf16[160,1152]{1,0:T(8,128)(2,1)S(1)}, bf16[160,1152]{1,0:T(8,128)(2,1)S(1)}, u32[]{:S(2)}, u32[]{:S(2)}) collective-permute-start(bf16[160,1152]{1,0:T(8,128)(2,1)S(1)} %collective-permute-done.2.far1), channel_id=1, source_target_pairs={{0,4},{4,0},{1,5},{5,1},{2,6},{6,2},{3,7},{7,3},{8,12},{12,8},{9,1... | collective-permute-start | bytes 1105928 | tf_op jit(solution)/shard_map/ppermute | solution.py:335
  39.5 5.1 %collective-permute-start.4 = (f32[2,24,304]{2,1,0:T(8,128)S(1)}, f32[2,24,304]{2,1,0:T(8,128)S(1)}, u32[]{:S(2)}, u32[]{:S(2)}) collective-permute-start(f32[2,24,304]{2,1,0:T(8,128)S(1)} %pad_maximum_fusion), channel_id=1, source_target_pairs={{0,1},{1,0},{2,3},{3,2},{4,5},{5,4},{6,7},{7,6},{8,9},{9,8},{10,11... | collective-permute-start | bytes 175112 | tf_op jit(solution)/shard_map/ppermute | solution.py:370
  44.6 6.3 %collective-permute-start.5 = (f32[2,24,304]{2,1,0:T(8,128)S(1)}, f32[2,24,304]{2,1,0:T(8,128)S(1)}, u32[]{:S(2)}, u32[]{:S(2)}) collective-permute-start(f32[2,24,304]{2,1,0:T(8,128)S(1)} %fusion.2.totals1), channel_id=1, source_target_pairs={{0,3},{3,0},{1,2},{2,1},{4,7},{7,4},{5,6},{6,5},{8,11},{11,8},{9,1... | collective-permute-start | bytes 175112 | tf_op jit(solution)/shard_map/ppermute | solution.py:371
  51.0 10.5 %collective-permute-start.7 = (bf16[20,24,384]{2,1,0:T(8,128)(2,1)S(1)}, bf16[20,24,384]{2,1,0:T(8,128)(2,1)S(1)}, u32[]{:S(2)}, u32[]{:S(2)}) collective-permute-start(bf16[20,24,384]{2,1,0:T(8,128)(2,1)S(1)} %get-tuple-element.22.own), channel_id=1, source_target_pairs={{0,1},{1,2},{2,3},{3,0},{4,5},{5,6},{6,7},{7,4},{8,9},{9,10},{10,1... | collective-permute-start | bytes 1105928 | tf_op jit(solution)/shard_map/ppermute | solution.py:331
  52.9 9.5 %collective-permute-start.6 = (bf16[20,24,384]{2,1,0:T(8,128)(2,1)S(1)}, bf16[20,24,384]{2,1,0:T(8,128)(2,1)S(1)}, u32[]{:S(2)}, u32[]{:S(2)}) collective-permute-start(bf16[20,24,384]{2,1,0:T(8,128)(2,1)S(1)} %get-tuple-element.22.own), channel_id=1, source_target_pairs={{0,3},{1,0},{2,1},{3,2},{4,7},{5,4},{6,5},{7,6},{8,11},{9,8},{10,9... | collective-permute-start | bytes 1105928 | tf_op jit(solution)/shard_map/ppermute | solution.py:331
  62.5 9.8 %collective-permute-start.8 = (bf16[20,24,384]{2,1,0:T(8,128)(2,1)S(1)}, bf16[20,24,384]{2,1,0:T(8,128)(2,1)S(1)}, u32[]{:S(2)}, u32[]{:S(2)}) collective-permute-start(bf16[20,24,384]{2,1,0:T(8,128)(2,1)S(1)} %broadcast_select_fusion), channel_id=1, source_target_pairs={{0,1},{1,2},{2,3},{3,0},{4,7},{5,4},{6,5},{7,6},{8,9},{9,10},{10,1... | collective-permute-start | bytes 1105928 | tf_op jit(solution)/shard_map/ppermute | solution.py:341
  78.4 8.6 %collective-permute-start.9 = (f32[64,16,128]{2,1,0:T(8,128)S(1)}, f32[64,16,128]{2,1,0:T(8,128)S(1)}, u32[]{:S(2)}, u32[]{:S(2)}) collective-permute-start(f32[64,16,128]{2,1,0:T(8,128)S(1)} %get-tuple-element.24), channel_id=1, source_target_pairs={{0,4},{4,0},{1,5},{5,1},{2,6},{6,2},{3,7},{7,3},{8,12},{12,8},{9,1... | collective-permute-start | bytes 1572872 | tf_op jit(solution)/shard_map/ppermute | solution.py:335
  148.8 9.4 %collective-permute-start.10 = (f32[64,16,128]{2,1,0:T(8,128)S(1)}, f32[64,16,128]{2,1,0:T(8,128)S(1)}, u32[]{:S(2)}, u32[]{:S(2)}) collective-permute-start(f32[64,16,128]{2,1,0:T(8,128)S(1)} %all_to_all.11.mine), channel_id=1, source_target_pairs={{0,4},{4,0},{1,5},{5,1},{2,6},{6,2},{3,7},{7,3},{8,12},{12,8},{9,1... | collective-permute-start | bytes 1572872 | tf_op jit(solution)/shard_map/ppermute | solution.py:335

commit v2 on v1

--- a/solution.py
+++ b/solution.py
@@ -16,6 +16,7 @@
 WIDE = 384
 ROWS = 304
 HALF = 160
+SIDE = 51
 SPAN = 96
 BLOCK = 1088
 FRAME = 1152
@@ -92,7 +93,7 @@
     total[...] = sums
 
 
-def scores_call(place, rad, first, beside1, beside2, far1, far2):
+def scores_call(place, rad, first, *pieces):
     return pl.pallas_call(
         scores_kernel,
         out_shape=(
@@ -104,15 +105,15 @@
         scratch_shapes=[pltpu.VMEM((ROWS, FRAME), BF16)],
         compiler_params=params(),
         name="scores",
-    )(place, rad, first, beside1, beside2, far1, far2)
+    )(place, rad, first, *pieces)
 
 
 def widen(value):
     return jnp.concatenate([value, jnp.zeros(value.shape[:-1] + (WIDE - ROWS,), F32)], axis=-1)
 
 
-def perturb_kernel(scores, totals1, totals2, out, innovation, mean):
-    totals = totals1[...] + totals2[...]
+def perturb_kernel(scores, parts, out, innovation, mean):
+    totals = (parts[0] + parts[1]) + (parts[2] + parts[3])
     average = totals[0] / (GROUPS * MEM)
     mean[...] = widen(average)
     innovation[...] = widen(totals[1] - average).astype(BF16)
@@ -120,7 +121,7 @@
         out[m, :, :] = widen(scores[m] - average).astype(BF16)
 
 
-def perturb_call(scores, totals1, totals2):
+def perturb_call(scores, parts):
     return pl.pallas_call(
         perturb_kernel,
         out_shape=(
@@ -128,18 +129,23 @@
             jax.ShapeDtypeStruct((OBS, WIDE), BF16),
             jax.ShapeDtypeStruct((OBS, WIDE), F32),
         ),
-        in_specs=[VMEM] * 3,
+        in_specs=[VMEM] * 2,
         out_specs=(VMEM,) * 3,
         compiler_params=params(),
         name="perturb",
-    )(scores, totals1, totals2)
-
-
-def gram_kernel(place, targets, loc, precision, innov, own, p1, p2, p3, keep, send, every, rows, acc):
-    core = place[1]
-    rows[...] = jnp.zeros_like(rows)
+    )(scores, parts)
+
+
+def gram_kernel(place, targets, loc, precision, innov, own, n1, n2, p2, out, every, rows, acc):
+    group, core = place[0], place[1]
+    for o in range(OBS):
+        for lane in range(WIDE // 128):
+            rows[lane, o * SPAN + 80 : (o + 1) * SPAN, :] = jnp.zeros((SPAN - 80, 128), F32)
     acc[...] = jnp.zeros_like(acc)
-    for at, block in ((0, own), (MEM, p1), (2 * MEM, p2), (3 * MEM + 1, p3)):
+    after, before = MEM, 3 * MEM + 1
+    at1 = before + core * (after - before)
+    at2 = after + core * (before - after)
+    for at, block in ((0, own), (at1, n1), (at2, n2), (2 * MEM, p2)):
         for m in range(MEM):
             wide = block[m].astype(F32)
             for g in range(OBS // 8):
@@ -173,53 +179,90 @@
             term = lax.dot_general(weighted, right, NT, preferred_element_type=F32)
             result = term if result is None else result + term
         for r in range(TOP):
-            target = targets[o * TOP + r]
-            bit = lax.rem(target, 2)
-            side = bit + core - 2 * bit * core
-            index = side * CHIPS + lax.div(target, 2)
+            index = targets[o * TOP + r]
             part = result[24 * r : 24 * r + 24]
             acc[index, 0:8, :] += part[0:8] + pltpu.roll(part[16:24], 64, 1)
             acc[index, 8:16, :] += part[8:16]
         return carry
 
     lax.fori_loop(0, OBS, footprint, 0, unroll=4)
-    keep[...] = acc[:CHIPS]
-    send[...] = acc[CHIPS:]
-
-
-def gram_call(place, targets, loc, precision, innov, own, p1, p2, p3):
-    half = jax.ShapeDtypeStruct((CHIPS, 16, 128), F32)
+    lane = lax.broadcasted_iota(jnp.int32, (8, 128), 1)
+    row = lax.broadcasted_iota(jnp.int32, (8, 128), 0)
+    column = lane % 64
+    second = jnp.where(lane < 64, row * 0, 1)
+    as_is = []
+    for half in (second, jnp.where(row + 8 >= MEM // 2, 1, 0)):
+        near = half == jnp.where(group >= GROUPS // 2, 1, 0)
+        as_is.append((column < 40) | ((column < 50) & near))
+
+    def pack(t, carry):
+        top, middle = acc[t, 0:8, :], acc[t, 8:16, :]
+        top = jnp.where(as_is[0], top, pltpu.roll(top, 118, 1))
+        middle = jnp.where(as_is[1], middle, pltpu.roll(middle, 118, 1))
+        low = top - top.astype(BF16).astype(F32)
+        top = jnp.where(lane == 19, pltpu.roll(low, 97, 1), top)
+        top = jnp.where(lane == 115, pltpu.roll(low, 1, 1), top)
+        low = middle - middle.astype(BF16).astype(F32)
+        middle = jnp.where(lane == 19, pltpu.roll(low, 97, 1), middle)
+        tail = jnp.where(row < 4, pltpu.roll(top, 38, 1), pltpu.roll(pltpu.roll(top, 12, 1), 4, 0))
+        out[t, :, :] = jnp.where(
+            lane < SIDE, top, jnp.where(lane < 2 * SIDE, pltpu.roll(middle, SIDE, 1), tail)
+        )
+        return carry
+
+    lax.fori_loop(0, 2 * CHIPS, pack, 0, unroll=8)
+
+
+def gram_call(place, targets, loc, precision, innov, own, n1, n2, p2):
+    packed = jax.ShapeDtypeStruct((2 * CHIPS, 8, 128), F32)
     return pl.pallas_call(
         gram_kernel,
-        out_shape=(half, half, jax.ShapeDtypeStruct((OBS, SPAN, WIDE), BF16)),
+        out_shape=(packed, jax.ShapeDtypeStruct((OBS, SPAN, WIDE), BF16)),
         in_specs=[SMEM] * 3 + [VMEM] * 6,
-        out_specs=(VMEM,) * 3,
+        out_specs=(VMEM,) * 2,
         scratch_shapes=[
             pltpu.VMEM((WIDE // 128, OBS * SPAN, 128), F32),
             pltpu.VMEM((2 * CHIPS, 16, 128), F32),
         ],
         compiler_params=params(),
         name="gram",
-    )(place, targets, loc, precision, innov, own, p1, p2, p3)
+    )(place, targets, loc, precision, innov, own, n1, n2, p2)
 
 
 def root_kernel(place, gathered, out, upper):
     group = place[0]
     order = GROUPS * MEM
     lane20 = lax.broadcasted_iota(jnp.int32, (MEM, 128), 1)
-    share = jnp.where(lane20 < 20, 0.5, jnp.where(lane20 < 40, 1.0, jnp.where(lane20 < 60, 0.5, 0.0)))
+    row20 = lax.broadcasted_iota(jnp.int32, (MEM, 128), 0)
+    lower = jnp.where(row20 >= MEM // 2, 1, 0)
+    own = jnp.where((row20 < 16) & (lane20 == 19), 0.0, 0.5)
+    own = jnp.where((row20 == 19) & (lane20 < 16), 1.0, own)
+    lane8 = lax.broadcasted_iota(jnp.int32, (8, 128), 1)
+    row8 = lax.broadcasted_iota(jnp.int32, (8, 128), 0)
     upper[...] = jnp.zeros_like(upper)
     for d in range(GROUPS):
-        block = gathered[lax.rem(group + d, GROUPS)]
-        full = jnp.concatenate([block, pltpu.roll(block[0:8], 64, 1)[0:4]], axis=0)
-        scaled = full * share
+        source = lax.rem(group + d, GROUPS)
+        block = gathered[source]
+        tail = jnp.where(
+            lane8 < 26, pltpu.roll(block, 26, 1), pltpu.roll(pltpu.roll(block, 52, 1), 4, 0)
+        )
+        full = jnp.concatenate([block, pltpu.roll(block, 128 - SIDE, 1), tail[0:4]], axis=0)
+        near = lower == jnp.where(source >= GROUPS // 2, 1, 0)
+        scaled = jnp.where(lane20 < 20, own * full, full)
+        scaled = jnp.where((lane20 < 40) | ((lane20 < 50) & near), scaled, 0.0)
+        moved = jnp.where((lane20 >= 50) & (lane20 < 60) & ~near, pltpu.roll(full, 10, 1), 0.0)
+        scaled = scaled + moved
         shift = MEM * d
         placed = scaled if d == 0 else pltpu.roll(scaled, shift, 1)
         placed = jnp.where(lane20 < order, placed, 0.0)
         if d >= 2:
             wrapped = pltpu.roll(scaled, (shift - order) % 128, 1)
             placed = placed + jnp.where(lane20 < shift - 20, wrapped, 0.0)
-        placed = placed + jnp.where(lane20 == order, pltpu.roll(full, 20, 1), 0.0)
+        low = jnp.where(
+            row20 < 16, pltpu.roll(full, order - 19, 1), pltpu.roll(full, order - SIDE, 1)
+        )
+        pull = pltpu.roll(full, order - 50, 1) + low
+        placed = placed + jnp.where(lane20 == order, pull, 0.0)
         upper[shift : shift + MEM, :] = placed
     half = upper[...]
     flipped = half.T
@@ -250,20 +293,28 @@
             root = times(root, factor)
         inverse = factor if inverse is None else times(factor, inverse)
     offset = times(times(pull, inverse), inverse) / (bound * (order - 1.0))
-    weights = inverse[0:24] / jnp.sqrt(bound) + offset[0:1]
-    lane8 = lax.broadcasted_iota(jnp.int32, (8, 128), 1)
-    row8 = lax.broadcasted_iota(jnp.int32, (8, 128), 0)
+    weights = inverse[0:24] / jnp.sqrt(bound)
+    offset = offset[0:1]
+    own = (row[0:24] == lane[0:24]) & (row[0:24] < MEM)
+    diagonal = jnp.sum(jnp.where(own, weights, 0.0), axis=0, keepdims=True)
+    low = diagonal - diagonal.astype(BF16).astype(F32)
+    offset_high = offset.astype(BF16).astype(F32)
+    offset_low = offset - offset_high
+    pair = [jnp.where(row8 == 1 + at, offset_low, 0.0) + jnp.where(row8 == 3 + at, offset_high, 0.0) for at in (0, 1)]
+    low = jnp.where(row8 == 0, low, 0.0) + pair[0]
+    low = jnp.where(lane8 >= 80, pltpu.roll(low, 80, 1), 0.0)
+    low = low + jnp.where((lane8 >= 80) & (lane8 < 112), pltpu.roll(pair[1], 32, 1), 0.0)
     tail = jnp.where(row8 < 4, weights[16:24], 0.0)
     first = jnp.where(lane8 >= 80, pltpu.roll(tail, 80, 1), 0.0)
     second = jnp.where((lane8 >= 80) & (lane8 < 112), pltpu.roll(tail, 32, 1), 0.0)
-    out[0:8, :] = weights[0:8] + first + pltpu.roll(second, 4, 0)
-    out[8:16, :] = weights[8:16]
+    top = weights[0:8] + first + pltpu.roll(second, 4, 0)
+    out[...] = jnp.concatenate([top, weights[8:16] + low], axis=0).astype(BF16)
 
 
 def root_call(place, gathered):
     return pl.pallas_call(
         root_kernel,
-        out_shape=jax.ShapeDtypeStruct((16, 128), F32),
+        out_shape=jax.ShapeDtypeStruct((16, 128), BF16),
         in_specs=[SMEM, VMEM],
         out_specs=VMEM,
         scratch_shapes=[pltpu.VMEM((128, 128), F32)],
@@ -283,7 +334,7 @@
             target = targets[o * TOP + r]
             index = lax.div(target, 2)
             local = lax.rem(target, 2) == core
-            piece = jnp.where(local, mine[index], other[index])
+            piece = jnp.where(local, mine[index].astype(F32), other[index].astype(F32))
             blend = blend + coef[o * TOP + r] * piece
         top, middle = blend[0:8], blend[8:16]
         first = jnp.where(lane8 < 48, pltpu.roll(top, 48, 1), 0.0)
@@ -293,6 +344,14 @@
             [jnp.where(lane8 < 80, top, 0.0), jnp.where(lane8 < 80, middle, 0.0), tail], axis=0
         )
         lane24 = lax.broadcasted_iota(jnp.int32, (24, 128), 1)
+        own = lax.broadcasted_iota(jnp.int32, (24, 128), 0) == lane24
+        left, right = pltpu.roll(middle, 48, 1), pltpu.roll(middle, 96, 1)
+        offset = jnp.where(
+            lane8[0:1] < 48,
+            left[1:2] + left[3:4],
+            jnp.where(lane8[0:1] < 80, right[2:3] + right[4:5], 0.0),
+        )
+        whole = whole + offset + jnp.where(own & (lane24 < MEM), left[0:1], 0.0)
         moved = jnp.where((lane24 > 60) & (lane24 < 81), pltpu.roll(whole, 1, 1), 0.0)
         whole = jnp.where(lane24 < 60, whole, moved)
         high = whole.astype(BF16).astype(F32)
@@ -327,18 +386,19 @@
     )(place, targets, coef, mine, other, every, mean)
 
 
-def shift(value, steps):
-    return lax.ppermute(value, "mem", [(i, (i + steps) % GROUPS) for i in range(GROUPS)])
-
-
 def swap(value):
     return lax.ppermute(value, "core", [(0, 1), (1, 0)])
 
 
-def turn(value):
-    pairs = [(i, (i + 1) % GROUPS) for i in range(GROUPS)]
-    pairs += [(GROUPS + i, GROUPS + (i - 1) % GROUPS) for i in range(GROUPS)]
+def turn(value, step=1):
+    pairs = [(i, (i + step) % GROUPS) for i in range(GROUPS)]
+    pairs += [(GROUPS + i, GROUPS + (i - step) % GROUPS) for i in range(GROUPS)]
     return lax.ppermute(value, ("core", "mem"), pairs)
+
+
+def to_groups(value):
+    copies = jnp.broadcast_to(value[None], (GROUPS,) + value.shape)
+    return lax.all_to_all(copies, "mem", split_axis=0, concat_axis=0, tiled=True)
 
 
 def pad_lanes(value, width):
@@ -363,35 +423,34 @@
     obs_partial = pad_lanes(jnp.dot(observed, basis, preferred_element_type=F32), ROWS)
     beside1, first, obs_partial = lax.optimization_barrier((beside1, first, obs_partial))
     far1 = turn(lax.dynamic_slice_in_dim(beside1, core * (ROWS - HALF), HALF, 0))
-    beside2 = swap(beside1)
-    far2 = swap(far1)
-    scores, member_sum = scores_call(place, rad, first, beside1, beside2, far1, far2)
-    totals = jnp.stack([member_sum, obs_partial])
-    totals = totals + lax.ppermute(totals, "mem", [(0, 1), (1, 0), (2, 3), (3, 2)])
-    across = lax.ppermute(totals, "mem", [(0, 3), (3, 0), (1, 2), (2, 1)])
-    perturbed, innovation, mean = perturb_call(scores, totals, across)
-    after1 = shift(perturbed, 3)
-    after3 = shift(perturbed, 1)
-    after2 = turn(jnp.where(core == 0, after3, after1))
+    scores, member_sum = scores_call(
+        place, rad, first, beside1, swap(beside1), far1, swap(far1)
+    )
+    parts = to_groups(jnp.stack([member_sum, obs_partial]))
+    perturbed, innovation, mean = perturb_call(scores, parts)
+    next1 = turn(perturbed)
+    next2 = turn(perturbed, -1)
+    across = turn(next1)
 
     weights_loc = localization(radius_bins)
     rounded_loc = lax.reduce_precision(weights_loc, 8, 7).reshape(OBS * TOP)
     coef = (weights_loc / jnp.sum(weights_loc, axis=1, keepdims=True)).reshape(OBS * TOP)
     targets = tile_lists.reshape(OBS * TOP)
-    keep, send, every = gram_call(
+    packed, every = gram_call(
         place,
         targets,
         rounded_loc,
         pad_lanes(precision_pc[None], WIDE),
         innovation,
         perturbed,
-        after1,
-        after2,
-        after3,
-    )
-    chip_sum = keep + swap(send)
-    arrived = lax.all_to_all(chip_sum, ("y", "z"), split_axis=0, concat_axis=0, tiled=True)
-    gathered = lax.all_gather(jnp.sum(arrived, axis=0), "mem", axis=0)
+        next1,
+        next2,
+        across,
+    )
+    arrived = lax.all_to_all(
+        packed.astype(BF16), ("y", "z", "core"), split_axis=0, concat_axis=0, tiled=True
+    )
+    gathered = to_groups(jnp.sum(arrived.astype(F32), axis=0))
     weights = root_call(place, gathered)
     mine = lax.all_to_all(
         jnp.broadcast_to(weights[None], (CHIPS, 16, 128)),

time: 162 us -> 147 us (0.907)
  starting transfers between devices: 56.3 us -> 40.1 us
  waiting for transfers between devices: 23.5 us -> 12.7 us
  blocking collectives: 58.7 us -> 66.9 us
  Pallas kernels: 16.5 us -> 20.4 us
    all_to_all x1 -> x3, blocking collectives: 27.4 us -> 49.7 us  [the longest x1 34.2 us: body(): lax.all_to_all(packed.astype(BF16), ('y', 'z', 'core'), split_axis=0, con...]
    ppermute x4 -> x0, waiting for transfers between devices: 12.4 us -> none  [the longest x2 4.9 us: shift(): lax.ppermute(value, 'mem', [(i, (i + steps) % GROUPS) for i in range(GROU...]
    ppermute x4 -> x0, starting transfers between devices: 10.3 us -> none  [the longest x2 6.49 us: shift(): lax.ppermute(value, 'mem', [(i, (i + steps) % GROUPS) for i in range(GROU...]
    ppermute x4 -> x3, starting transfers between devices: 30.3 us -> 20.8 us  [swap(): return lax.ppermute(value, 'core', [(0, 1), (1, 0)])]
    all_gather x1 -> x0, blocking collectives: 9.02 us -> none  [body(): gathered = lax.all_gather(jnp.sum(arrived, axis=0), 'mem', axis=0)]
    all_to_all x1, blocking collectives: 22.2 us -> 17.2 us  [body(): lax.all_to_all(jnp.broadcast_to(weights[None], (CHIPS, 16, 128)), ('y', '...]
    pallas_call x2, Pallas kernels: 9 us -> 12.8 us  [the longest x1 9.86 us: gram_call(): pl.pallas_call(gram_kernel, out_shape=(packed, jax.ShapeDtypeStruct((OBS,...]
    ppermute x3 -> x5, starting transfers between devices: 15.7 us -> 19.4 us  [turn(): return lax.ppermute(value, ('core', 'mem'), pairs)]
  transfers between devices with their start and end apart: 11 -> 8, of which waited for: 9 -> 6; matrix products, arithmetic and copies ran while one was open for 1% -> 1% of each run, Pallas kernels for 1% -> 1%
where the time goes in v2:
time: 147 us
  blocking collectives  66.9 us (46%)
  starting transfers between devices  40.1 us (27%)
  Pallas kernels  20.4 us (14%)
  waiting for transfers between devices  12.7 us (9%)
  local copies, waits for them, and re-layouts  2.88 us (2%)
  other arithmetic  2.04 us (1%)
    all_to_all x1, blocking collectives, body(): lax.all_to_all(packed.astype(BF16), ('y', 'z', 'core'), split_axis=0, con...  34.2 us
    ppermute x3, starting transfers between devices, swap(): return lax.ppermute(value, 'core', [(0, 1), (1, 0)])  20.8 us
    ppermute x5, starting transfers between devices, turn(): return lax.ppermute(value, ('core', 'mem'), pairs)  19.4 us
    all_to_all x1, blocking collectives, body(): lax.all_to_all(jnp.broadcast_to(weights[None], (CHIPS, 16, 128)), ('y', '...  17.2 us
    all_to_all x2, blocking collectives, to_groups(): lax.all_to_all(copies, 'mem', split_axis=0, concat_axis=0, tiled=True)  15.6 us
    ppermute x5, waiting for transfers between devices, turn(): return lax.ppermute(value, ('core', 'mem'), pairs)  10.5 us
    pallas_call x1, Pallas kernels, gram_call(): pl.pallas_call(gram_kernel, out_shape=(packed, jax.ShapeDtypeStruct((OBS,...  9.86 us
    pallas_call x1, Pallas kernels, mix_call(): pl.pallas_call(mix_kernel, out_shape=jax.ShapeDtypeStruct((MEM, OBS, COMP...  3.51 us
  transfers between devices with their start and end apart: 8, of which 6 were waited for; matrix products, arithmetic and copies ran while one was open for 1% of the time, Pallas kernels for 1%

profile of v2, /device:TPU:1, one launch (start us, length us, event | category | flops | bytes accessed | tf_op | source)
XLA Modules:
  0.0 146.7 jit_solution(13067040921821307053)
XLA Ops:
  0.0 1.8 %pad_select_fusion.own = bf16[304,1152]{1,0:T(8,128)(2,1)S(1)} fusion(bf16[300,1088]{1,0:T(8,128)(2,1)} %bitcast.14, pred[]{:T(512)S(6)} %eq.3), kind=kLoop, calls=%fused_computation | loop fusion | flops 350208 | bytes 1353217 | tf_op jit(solution)/shard_map/jit(_where)/select_n | solution.py:416
  1.8 5.2 %collective-permute-start = (bf16[304,1152]{1,0:T(8,128)(2,1)S(1)}, bf16[304,1152]{1,0:T(8,128)(2,1)S(1)}, u32[]{:S(2)}, u32[]{:S(2)}) collective-permute-start(bf16[304,1152]{1,0:T(8,128)(2,1)S(1)} %pad_select_fusion.own), channel_id=1, source_target_pairs={{0,1},{1,2},{2,3},{3,0},{4,7},{5,4},{6,5},{7,6},{8,9},{9,10},{10,1... | collective-permute-start | bytes 2101256 | tf_op jit(solution)/shard_map/ppermute | solution.py:396
  7.0 1.4 fusion.2
  8.5 2.2 %copy-done.1 = bf16[24,20,4352]{2,0,1:T(8,128)(2,1)S(1)} copy-done((bf16[24,20,4352]{2,0,1:T(8,128)(2,1)S(1)}, bf16[24,20,4352]{2,0,1:T(8,128)(2,1)}, u32[]{:S(2)}) %copy-start.1) | copy-done | bytes 4177944
  10.7 1.3 scores_own.1.first
  12.0 3.0 %collective-permute-done.beside1 = bf16[304,1152]{1,0:T(8,128)(2,1)S(1)} collective-permute-done((bf16[304,1152]{1,0:T(8,128)(2,1)S(1)}, bf16[304,1152]{1,0:T(8,128)(2,1)S(1)}, u32[]{:S(2)}, u32[]{:S(2)}) %collective-permute-start) | collective-permute-done | bytes 700448 | tf_op jit(solution)/shard_map/ppermute | solution.py:396
  15.0 5.2 %collective-permute-start.2 = (bf16[160,1152]{1,0:T(8,128)(2,1)S(1)}, bf16[160,1152]{1,0:T(8,128)(2,1)S(1)}, u32[]{:S(2)}, u32[]{:S(2)}) collective-permute-start(bf16[160,1152]{1,0:T(8,128)(2,1)S(1)} %constant_dynamic-slice_fusion), channel_id=1, source_target_pairs={{0,1},{1,2},{2,3},{3,0},{4,7},{5,4},{6,5},{7,6},{8,9},{9,10},{10,1... | collective-permute-start | bytes 1105928 | tf_op jit(solution)/shard_map/ppermute | solution.py:396
  20.2 6.6 %collective-permute-start.1 = (bf16[304,1152]{1,0:T(8,128)(2,1)S(1)}, bf16[304,1152]{1,0:T(8,128)(2,1)S(1)}, u32[]{:S(2)}, u32[]{:S(2)}) collective-permute-start(bf16[304,1152]{1,0:T(8,128)(2,1)S(1)} %collective-permute-done.beside1), channel_id=1, source_target_pairs={{0,4},{4,0},{1,5},{5,1},{2,6},{6,2},{3,7},{7,3},{8,12},{12,8},{9,1... | collective-permute-start | bytes 2101256 | tf_op jit(solution)/shard_map/ppermute | solution.py:390
  26.9 8.7 %collective-permute-start.3 = (bf16[160,1152]{1,0:T(8,128)(2,1)S(1)}, bf16[160,1152]{1,0:T(8,128)(2,1)S(1)}, u32[]{:S(2)}, u32[]{:S(2)}) collective-permute-start(bf16[160,1152]{1,0:T(8,128)(2,1)S(1)} %collective-permute-done.2.far1), channel_id=1, source_target_pairs={{0,4},{4,0},{1,5},{5,1},{2,6},{6,2},{3,7},{7,3},{8,12},{12,8},{9,1... | collective-permute-start | bytes 1105928 | tf_op jit(solution)/shard_map/ppermute | solution.py:390
  35.5 1.3 collective-permute-done.3.far2
  36.8 2.7 %scores.1 = (f32[20,24,304]{2,1,0:T(8,128)S(1)}, f32[24,304]{1,0:T(8,128)S(1)}) custom-call(s32[2]{0:T(128)S(1)} %pad_add_fusion.place, bf16[480,4352]{1,0:T(8,128)(2,1)S(1)} %bitcast.12, f32[480,304]{1,0:T(8,128)S(1)} %scores_own.1.first, bf16[304,1152]{1,0:T(8,128)(2,1)S(1)} %collective-permute-done.beside1, ...), custom_call_target="tpu_custom_call" | custom-call | tf_op jit(solution)/shard_map/scores/pallas_call | solution.py:97
  39.5 9.0 %all_to_all.20.parts = f32[4,2,24,304]{3,2,1,0:T(8,128)S(1)} all-to-all(f32[4,2,24,304]{3,2,1,0:T(8,128)S(1)} %broadcast_in_dim.9), channel_id=1, replica_groups=mesh['y'=8,'z'=8,'core'=2,'mem'=4] {'mem'}, dimensions={0} | all-to-all | bytes 466944 | tf_op jit(solution)/shard_map/all_to_all | solution.py:401
  48.6 2.8 %collective-permute-start.4 = (bf16[20,24,384]{2,1,0:T(8,128)(2,1)S(1)}, bf16[20,24,384]{2,1,0:T(8,128)(2,1)S(1)}, u32[]{:S(2)}, u32[]{:S(2)}) collective-permute-start(bf16[20,24,384]{2,1,0:T(8,128)(2,1)S(1)} %get-tuple-element.21.own), channel_id=1, source_target_pairs={{0,1},{1,2},{2,3},{3,0},{4,7},{5,4},{6,5},{7,6},{8,9},{9,10},{10,1... | collective-permute-start | bytes 1105928 | tf_op jit(solution)/shard_map/ppermute | solution.py:396
  51.4 2.5 %collective-permute-start.5 = (bf16[20,24,384]{2,1,0:T(8,128)(2,1)S(1)}, bf16[20,24,384]{2,1,0:T(8,128)(2,1)S(1)}, u32[]{:S(2)}, u32[]{:S(2)}) collective-permute-start(bf16[20,24,384]{2,1,0:T(8,128)(2,1)S(1)} %get-tuple-element.21.own), channel_id=1, source_target_pairs={{0,3},{1,0},{2,1},{3,2},{4,5},{5,6},{6,7},{7,4},{8,11},{9,8},{10,9... | collective-permute-start | bytes 1105928 | tf_op jit(solution)/shard_map/ppermute | solution.py:396
  53.9 3.3 %collective-permute-done.4.n1 = bf16[20,24,384]{2,1,0:T(8,128)(2,1)S(1)} collective-permute-done((bf16[20,24,384]{2,1,0:T(8,128)(2,1)S(1)}, bf16[20,24,384]{2,1,0:T(8,128)(2,1)S(1)}, u32[]{:S(2)}, u32[]{:S(2)}) %collective-permute-start.4) | collective-permute-done | bytes 368672 | tf_op jit(solution)/shard_map/ppermute | solution.py:396
  57.2 3.7 %collective-permute-start.6 = (bf16[20,24,384]{2,1,0:T(8,128)(2,1)S(1)}, bf16[20,24,384]{2,1,0:T(8,128)(2,1)S(1)}, u32[]{:S(2)}, u32[]{:S(2)}) collective-permute-start(bf16[20,24,384]{2,1,0:T(8,128)(2,1)S(1)} %collective-permute-done.4.n1), channel_id=1, source_target_pairs={{0,1},{1,2},{2,3},{3,0},{4,7},{5,4},{6,5},{7,6},{8,9},{9,10},{10,1... | collective-permute-start | bytes 1105928 | tf_op jit(solution)/shard_map/ppermute | solution.py:396
  60.9 0.1 copy.12
  61.0 0.1 reshape.18.loc
  61.2 0.1 copy.10
  61.2 0.1 reshape.16.targets
  61.3 2.5 %collective-permute-done.5.n2 = bf16[20,24,384]{2,1,0:T(8,128)(2,1)S(1)} collective-permute-done((bf16[20,24,384]{2,1,0:T(8,128)(2,1)S(1)}, bf16[20,24,384]{2,1,0:T(8,128)(2,1)S(1)}, u32[]{:S(2)}, u32[]{:S(2)}) %collective-permute-start.5) | collective-permute-done | bytes 368672 | tf_op jit(solution)/shard_map/ppermute | solution.py:396
  63.8 1.8 %collective-permute-done.6.p2 = bf16[20,24,384]{2,1,0:T(8,128)(2,1)S(1)} collective-permute-done((bf16[20,24,384]{2,1,0:T(8,128)(2,1)S(1)}, bf16[20,24,384]{2,1,0:T(8,128)(2,1)S(1)}, u32[]{:S(2)}, u32[]{:S(2)}) %collective-permute-start.6) | collective-permute-done | bytes 368672 | tf_op jit(solution)/shard_map/ppermute | solution.py:396
  65.6 9.9 %gram.1 = (f32[128,8,128]{2,1,0:T(8,128)S(1)}, bf16[24,96,384]{2,1,0:T(8,128)(2,1)S(1)}) custom-call(s32[2]{0:T(128)S(1)} %pad_add_fusion.place, s32[72]{0:T(128)S(1)} %reshape.16.targets, f32[72]{0:T(128)S(1)} %reshape.18.loc, f32[1,384]{1,0:T(1,128)S(1)} %pad.16.precision, bf16[24,384]{1,0:T(8,128)(2,1)S(1)} %get-tuple-element.20.innov, ...), custom_call_target="tpu_custom_call" | custom-call | tf_op jit(solution)/shard_map/gram/pallas_call | solution.py:218
  75.5 34.2 %all_to_all.21 = bf16[128,8,128]{2,1,0:T(8,128)(2,1)S(1)} all-to-all(bf16[128,8,128]{2,1,0:T(8,128)(2,1)S(1)} %convert_element_type.18), channel_id=1, replica_groups=mesh['y'=8,'z'=8,'core'=2,'mem'=4] {'y','z','core'}, dimensions={0} | all-to-all | bytes 524288 | tf_op jit(solution)/shard_map/all_to_all | solution.py:450
  109.7 0.1 convert_reduce_fusion
  109.8 6.6 %all_to_all.22.gathered = f32[4,8,128]{2,1,0:T(8,128)S(1)} all-to-all(f32[4,8,128]{2,1,0:T(8,128)S(1)} %broadcast_in_dim.10), channel_id=1, replica_groups=mesh['y'=8,'z'=8,'core'=2,'mem'=4] {'mem'}, dimensions={0} | all-to-all | bytes 32768 | tf_op jit(solution)/shard_map/all_to_all | solution.py:401
  116.4 3.0 %root.1 = bf16[16,128]{1,0:T(8,128)(2,1)S(1)} custom-call(s32[2]{0:T(128)S(1)} %pad_add_fusion.place, f32[4,8,128]{2,1,0:T(8,128)S(1)} %all_to_all.22.gathered), custom_call_target="tpu_custom_call" | custom-call | tf_op jit(solution)/shard_map/root/pallas_call | solution.py:315
  119.4 17.2 %all_to_all.23.mine = bf16[64,16,128]{2,1,0:T(8,128)(2,1)S(1)} all-to-all(bf16[64,16,128]{2,1,0:T(8,128)(2,1)S(1)} %broadcast_in_dim.11), channel_id=1, replica_groups=mesh['y'=8,'z'=8,'core'=2,'mem'=4] {'y','z'}, dimensions={0} | all-to-all | bytes 524288 | tf_op jit(solution)/shard_map/all_to_all | solution.py:455
  136.6 5.5 %collective-permute-start.7 = (bf16[64,16,128]{2,1,0:T(8,128)(2,1)S(1)}, bf16[64,16,128]{2,1,0:T(8,128)(2,1)S(1)}, u32[]{:S(2)}, u32[]{:S(2)}) collective-permute-start(bf16[64,16,128]{2,1,0:T(8,128)(2,1)S(1)} %all_to_all.23.mine), channel_id=1, source_target_pairs={{0,4},{4,0},{1,5},{5,1},{2,6},{6,2},{3,7},{7,3},{8,12},{12,8},{9,1... | collective-permute-start | bytes 786440 | tf_op jit(solution)/shard_map/ppermute | solution.py:390
  142.2 0.1 reshape.17.coef
  142.2 1.0 collective-permute-done.7.other
  143.2 3.5 %mix.1 = bf16[20,24,300]{2,1,0:T(8,128)(2,1)} custom-call(s32[2]{0:T(128)S(1)} %pad_add_fusion.place, s32[72]{0:T(128)S(1)} %reshape.16.targets, f32[72]{0:T(128)S(1)} %reshape.17.coef, bf16[64,16,128]{2,1,0:T(8,128)(2,1)S(1)} %all_to_all.23.mine, bf16[64,16,128]{2,1,0:T(8,128)(2,1)S(1)} %collective-permute-done.7.other, ...), custom_call_target="tpu_custom_call" | custom-call | tf_op jit(solution)/shard_map/mix/pallas_call | solution.py:378
  (25 shorter events, 0.5 us)
Async XLA Ops:
  0.0 7.0 %copy-start = (bf16[24,1088]{1,0:T(8,128)(2,1)S(1)}, bf16[24,1088]{1,0:T(8,128)(2,1)}, u32[]{:S(2)}) copy-start(bf16[24,1088]{1,0:T(8,128)(2,1)} %param.7) | copy-start | bytes 156676
  1.8 13.2 %collective-permute-start = (bf16[304,1152]{1,0:T(8,128)(2,1)S(1)}, bf16[304,1152]{1,0:T(8,128)(2,1)S(1)}, u32[]{:S(2)}, u32[]{:S(2)}) collective-permute-start(bf16[304,1152]{1,0:T(8,128)(2,1)S(1)} %pad_select_fusion.own), channel_id=1, source_target_pairs={{0,1},{1,2},{2,3},{3,0},{4,7},{5,4},{6,5},{7,6},{8,9},{9,10},{10,1... | collective-permute-start | bytes 2101256 | tf_op jit(solution)/shard_map/ppermute | solution.py:396
  8.5 2.2 %copy-start.1 = (bf16[24,20,4352]{2,0,1:T(8,128)(2,1)S(1)}, bf16[24,20,4352]{2,0,1:T(8,128)(2,1)}, u32[]{:S(2)}) copy-start(bf16[24,20,4352]{2,0,1:T(8,128)(2,1)} %param.6) | copy-start | bytes 12533764
  15.0 45.9 %copy-start.4 = (f32[300]{0:T(512)S(1)}, f32[300]{0:T(512)}, u32[]{:S(2)}) copy-start(f32[300]{0:T(512)} %param.9) | copy-start | bytes 3604
  15.0 45.9 %copy-start.2 = (s32[24,3]{0,1:T(4,128)S(1)}, s32[24,3]{0,1:T(4,128)}, u32[]{:S(2)}) copy-start(s32[24,3]{0,1:T(4,128)} %param.11) | copy-start | bytes 868
  15.0 46.1 %copy-start.3 = (s32[24,3]{0,1:T(4,128)S(1)}, s32[24,3]{0,1:T(4,128)}, u32[]{:S(2)}) copy-start(s32[24,3]{0,1:T(4,128)} %param.10) | copy-start | bytes 868
  15.0 11.8 %collective-permute-start.2 = (bf16[160,1152]{1,0:T(8,128)(2,1)S(1)}, bf16[160,1152]{1,0:T(8,128)(2,1)S(1)}, u32[]{:S(2)}, u32[]{:S(2)}) collective-permute-start(bf16[160,1152]{1,0:T(8,128)(2,1)S(1)} %constant_dynamic-slice_fusion), channel_id=1, source_target_pairs={{0,1},{1,2},{2,3},{3,0},{4,7},{5,4},{6,5},{7,6},{8,9},{9,10},{10,1... | collective-permute-start | bytes 1105928 | tf_op jit(solution)/shard_map/ppermute | solution.py:396
  20.2 15.3 %collective-permute-start.1 = (bf16[304,1152]{1,0:T(8,128)(2,1)S(1)}, bf16[304,1152]{1,0:T(8,128)(2,1)S(1)}, u32[]{:S(2)}, u32[]{:S(2)}) collective-permute-start(bf16[304,1152]{1,0:T(8,128)(2,1)S(1)} %collective-permute-done.beside1), channel_id=1, source_target_pairs={{0,4},{4,0},{1,5},{5,1},{2,6},{6,2},{3,7},{7,3},{8,12},{12,8},{9,1... | collective-permute-start | bytes 2101256 | tf_op jit(solution)/shard_map/ppermute | solution.py:390
  26.9 10.0 %collective-permute-start.3 = (bf16[160,1152]{1,0:T(8,128)(2,1)S(1)}, bf16[160,1152]{1,0:T(8,128)(2,1)S(1)}, u32[]{:S(2)}, u32[]{:S(2)}) collective-permute-start(bf16[160,1152]{1,0:T(8,128)(2,1)S(1)} %collective-permute-done.2.far1), channel_id=1, source_target_pairs={{0,4},{4,0},{1,5},{5,1},{2,6},{6,2},{3,7},{7,3},{8,12},{12,8},{9,1... | collective-permute-start | bytes 1105928 | tf_op jit(solution)/shard_map/ppermute | solution.py:390
  48.6 8.6 %collective-permute-start.4 = (bf16[20,24,384]{2,1,0:T(8,128)(2,1)S(1)}, bf16[20,24,384]{2,1,0:T(8,128)(2,1)S(1)}, u32[]{:S(2)}, u32[]{:S(2)}) collective-permute-start(bf16[20,24,384]{2,1,0:T(8,128)(2,1)S(1)} %get-tuple-element.21.own), channel_id=1, source_target_pairs={{0,1},{1,2},{2,3},{3,0},{4,7},{5,4},{6,5},{7,6},{8,9},{9,10},{10,1... | collective-permute-start | bytes 1105928 | tf_op jit(solution)/shard_map/ppermute | solution.py:396
  51.4 12.4 %collective-permute-start.5 = (bf16[20,24,384]{2,1,0:T(8,128)(2,1)S(1)}, bf16[20,24,384]{2,1,0:T(8,128)(2,1)S(1)}, u32[]{:S(2)}, u32[]{:S(2)}) collective-permute-start(bf16[20,24,384]{2,1,0:T(8,128)(2,1)S(1)} %get-tuple-element.21.own), channel_id=1, source_target_pairs={{0,3},{1,0},{2,1},{3,2},{4,5},{5,6},{6,7},{7,4},{8,11},{9,8},{10,9... | collective-permute-start | bytes 1105928 | tf_op jit(solution)/shard_map/ppermute | solution.py:396
  57.2 8.4 %collective-permute-start.6 = (bf16[20,24,384]{2,1,0:T(8,128)(2,1)S(1)}, bf16[20,24,384]{2,1,0:T(8,128)(2,1)S(1)}, u32[]{:S(2)}, u32[]{:S(2)}) collective-permute-start(bf16[20,24,384]{2,1,0:T(8,128)(2,1)S(1)} %collective-permute-done.4.n1), channel_id=1, source_target_pairs={{0,1},{1,2},{2,3},{3,0},{4,7},{5,4},{6,5},{7,6},{8,9},{9,10},{10,1... | collective-permute-start | bytes 1105928 | tf_op jit(solution)/shard_map/ppermute | solution.py:396
  136.6 6.6 %collective-permute-start.7 = (bf16[64,16,128]{2,1,0:T(8,128)(2,1)S(1)}, bf16[64,16,128]{2,1,0:T(8,128)(2,1)S(1)}, u32[]{:S(2)}, u32[]{:S(2)}) collective-permute-start(bf16[64,16,128]{2,1,0:T(8,128)(2,1)S(1)} %all_to_all.23.mine), channel_id=1, source_target_pairs={{0,4},{4,0},{1,5},{5,1},{2,6},{6,2},{3,7},{7,3},{8,12},{12,8},{9,1... | collective-permute-start | bytes 786440 | tf_op jit(solution)/shard_map/ppermute | solution.py:390

commit v3 on v2

--- a/solution.py
+++ b/solution.py
@@ -1,5 +1,6 @@
 import jax
 import jax.numpy as jnp
+import numpy as np
 from jax import lax
 from jax.experimental import pallas as pl
 from jax.experimental.pallas import tpu as pltpu
@@ -17,6 +18,7 @@
 ROWS = 304
 HALF = 160
 SIDE = 51
+SPREAD = 64
 SPAN = 96
 BLOCK = 1088
 FRAME = 1152
@@ -136,97 +138,135 @@
     )(scores, parts)
 
 
-def gram_kernel(place, targets, loc, precision, innov, own, n1, n2, p2, out, every, rows, acc):
-    group, core = place[0], place[1]
+def lay(rows, stride, at, block):
+    for g in range(OBS // 8):
+        for lane in range(WIDE // 128):
+            rows[lane, pl.ds(g * 8 * stride + at, 8, stride=stride), :] = block[
+                g * 8 : g * 8 + 8, lane * 128 : lane * 128 + 128
+            ]
+
+
+def lay_kernel(place, own, n1, n2, rows):
+    core = place[1]
     for o in range(OBS):
         for lane in range(WIDE // 128):
-            rows[lane, o * SPAN + 80 : (o + 1) * SPAN, :] = jnp.zeros((SPAN - 80, 128), F32)
-    acc[...] = jnp.zeros_like(acc)
-    after, before = MEM, 3 * MEM + 1
+            rows[lane, o * SPREAD + 56 : (o + 1) * SPREAD, :] = jnp.zeros((8, 128), F32)
+    after, before = MEM, 2 * MEM
     at1 = before + core * (after - before)
     at2 = after + core * (before - after)
-    for at, block in ((0, own), (at1, n1), (at2, n2), (2 * MEM, p2)):
+    for at, block in ((0, own), (at1, n1), (at2, n2)):
         for m in range(MEM):
-            wide = block[m].astype(F32)
-            for g in range(OBS // 8):
-                for lane in range(WIDE // 128):
-                    rows[lane, pl.ds(g * 8 * SPAN + at + m, 8, stride=SPAN), :] = wide[
-                        g * 8 : g * 8 + 8, lane * 128 : lane * 128 + 128
-                    ]
-    wide = innov[...].astype(F32)
-    for g in range(OBS // 8):
+            lay(rows, SPREAD, at + m, block[m].astype(F32))
+
+
+def lay_call(place, own, n1, n2):
+    return pl.pallas_call(
+        lay_kernel,
+        out_shape=jax.ShapeDtypeStruct((WIDE // 128, OBS * SPREAD, 128), F32),
+        in_specs=[SMEM] + [VMEM] * 3,
+        out_specs=VMEM,
+        compiler_params=params(),
+        cost_estimate=pl.CostEstimate(flops=1000000, bytes_accessed=6000000, transcendentals=0),
+        name="lay",
+    )(place, own, n1, n2)
+
+
+def pack_maps():
+    variants = []
+    for first_half in (0, 1):
+        kept = [
+            list(range(40)) + list(range(40 + 10 * half, 50 + 10 * half)) + [60]
+            for half in (first_half, 1 - first_half)
+        ]
+        maps = np.zeros((6, 128, 128), np.float32)
+        for at, source in enumerate(kept[0]):
+            if at != 19:
+                maps[0:2, source, at] = 1
+                maps[2, source, SIDE + at] = 1
+        for at, source in enumerate(kept[1]):
+            maps[at // 26, 64 + source, 102 + at % 26] = 1
+            if at != 19:
+                maps[3, source, SIDE + at] = 1
+        maps[4, 60, 19] = maps[4, 124, 127] = maps[5, 60, SIDE + 19] = 1
+        variants.append(maps.reshape(6 * 128, 128))
+    return variants
+
+
+def gram_kernel(targets, loc, precision, maps, innov, rows, p2, out, every, far, acc):
+    acc[...] = jnp.zeros_like(acc)
+    for o in range(OBS):
         for lane in range(WIDE // 128):
-            rows[lane, pl.ds(g * 8 * SPAN + 3 * MEM, 8, stride=SPAN), :] = wide[
-                g * 8 : g * 8 + 8, lane * 128 : lane * 128 + 128
-            ]
-    live = lax.broadcasted_iota(jnp.int32, (24, 128), 0) < MEM
-    fade = [
-        jnp.where(live, precision[0:1, lane * 128 : lane * 128 + 128], 0.0)
-        for lane in range(WIDE // 128)
-    ]
+            far[lane, o * 24 + 16 : (o + 1) * 24, :] = jnp.zeros((8, 128), F32)
+    for m in range(MEM):
+        lay(far, 24, m, p2[m].astype(F32))
+    lay(far, 24, MEM, innov[...].astype(F32))
+    row = lax.broadcasted_iota(jnp.int32, (8, 128), 0)
+    lane = lax.broadcasted_iota(jnp.int32, (8, 128), 1)
 
     def footprint(o, carry):
-        start = pl.multiple_of(o * SPAN, SPAN)
+        start = pl.multiple_of(o * SPREAD, SPREAD)
+        far_start = pl.multiple_of(o * 24, 24)
         result = None
-        for lane in range(WIDE // 128):
-            whole = rows[lane, pl.ds(start, SPAN), :]
-            every[o, :, lane * 128 : lane * 128 + 128] = whole.astype(BF16)
-            mine = whole[:24]
+        for at in range(WIDE // 128):
+            span = slice(at * 128, at * 128 + 128)
+            near = rows[at, pl.ds(start, SPREAD), :]
+            whole = jnp.concatenate(
+                [
+                    near[:40],
+                    far[at, pl.ds(far_start, 24), :],
+                    near[40:],
+                    jnp.zeros((SPAN - 24 - SPREAD, 128), F32),
+                ],
+                axis=0,
+            )
+            every[o, :, span] = whole.astype(BF16)
+            last = jnp.where(row < 4, whole[16:24], pltpu.roll(whole[16:24], 4, 0))
+            mine = jnp.concatenate([whole[:16], last], axis=0)
             weighted = jnp.concatenate(
-                [mine * (loc[o * TOP + r] * fade[lane]) for r in range(TOP)], axis=0
+                [mine * (loc[o * TOP + r] * precision[0:1, span]) for r in range(TOP)], axis=0
             ).astype(BF16)
-            right = jnp.concatenate([whole[:64], jnp.zeros((64, 128), F32)], axis=0).astype(BF16)
+            right = jnp.concatenate([whole[:64], whole[:64]], axis=0).astype(BF16)
             term = lax.dot_general(weighted, right, NT, preferred_element_type=F32)
             result = term if result is None else result + term
         for r in range(TOP):
             index = targets[o * TOP + r]
             part = result[24 * r : 24 * r + 24]
-            acc[index, 0:8, :] += part[0:8] + pltpu.roll(part[16:24], 64, 1)
+            acc[index, 0:8, :] += jnp.where(lane < 64, part[0:8], part[16:24])
             acc[index, 8:16, :] += part[8:16]
         return carry
 
     lax.fori_loop(0, OBS, footprint, 0, unroll=4)
-    lane = lax.broadcasted_iota(jnp.int32, (8, 128), 1)
-    row = lax.broadcasted_iota(jnp.int32, (8, 128), 0)
-    column = lane % 64
-    second = jnp.where(lane < 64, row * 0, 1)
-    as_is = []
-    for half in (second, jnp.where(row + 8 >= MEM // 2, 1, 0)):
-        near = half == jnp.where(group >= GROUPS // 2, 1, 0)
-        as_is.append((column < 40) | ((column < 50) & near))
-
-    def pack(t, carry):
-        top, middle = acc[t, 0:8, :], acc[t, 8:16, :]
-        top = jnp.where(as_is[0], top, pltpu.roll(top, 118, 1))
-        middle = jnp.where(as_is[1], middle, pltpu.roll(middle, 118, 1))
-        low = top - top.astype(BF16).astype(F32)
-        top = jnp.where(lane == 19, pltpu.roll(low, 97, 1), top)
-        top = jnp.where(lane == 115, pltpu.roll(low, 1, 1), top)
-        low = middle - middle.astype(BF16).astype(F32)
-        middle = jnp.where(lane == 19, pltpu.roll(low, 97, 1), middle)
-        tail = jnp.where(row < 4, pltpu.roll(top, 38, 1), pltpu.roll(pltpu.roll(top, 12, 1), 4, 0))
-        out[t, :, :] = jnp.where(
-            lane < SIDE, top, jnp.where(lane < 2 * SIDE, pltpu.roll(middle, SIDE, 1), tail)
+    for t in range(0, 2 * CHIPS, 16):
+        top, middle = acc[t : t + 16, 0:8, :], acc[t : t + 16, 8:16, :]
+        low_top = top - top.astype(BF16).astype(F32)
+        low_middle = middle - middle.astype(BF16).astype(F32)
+        pieces = (
+            jnp.where(row < 4, top, 0.0),
+            jnp.where(row < 4, 0.0, top),
+            jnp.where(row < 2, middle, 0.0),
+            jnp.where(row < 2, 0.0, middle),
+            jnp.where((row < 4) & (lane >= 64), 0.0, low_top),
+            low_middle,
         )
-        return carry
-
-    lax.fori_loop(0, 2 * CHIPS, pack, 0, unroll=8)
-
-
-def gram_call(place, targets, loc, precision, innov, own, n1, n2, p2):
+        left = jnp.concatenate([p.reshape(128, 128).astype(BF16) for p in pieces], axis=1)
+        packed = jnp.dot(left, maps[...], preferred_element_type=F32)
+        out[t : t + 16, :, :] = packed.reshape(16, 8, 128)
+
+
+def gram_call(targets, loc, precision, maps, innov, rows, p2):
     packed = jax.ShapeDtypeStruct((2 * CHIPS, 8, 128), F32)
     return pl.pallas_call(
         gram_kernel,
         out_shape=(packed, jax.ShapeDtypeStruct((OBS, SPAN, WIDE), BF16)),
-        in_specs=[SMEM] * 3 + [VMEM] * 6,
+        in_specs=[SMEM] * 2 + [VMEM] * 5,
         out_specs=(VMEM,) * 2,
         scratch_shapes=[
-            pltpu.VMEM((WIDE // 128, OBS * SPAN, 128), F32),
+            pltpu.VMEM((WIDE // 128, OBS * 24, 128), F32),
             pltpu.VMEM((2 * CHIPS, 16, 128), F32),
         ],
         compiler_params=params(),
         name="gram",
-    )(place, targets, loc, precision, innov, own, n1, n2, p2)
+    )(targets, loc, precision, maps, innov, rows, p2)
 
 
 def root_kernel(place, gathered, out, upper):
@@ -352,7 +392,7 @@
             jnp.where(lane8[0:1] < 80, right[2:3] + right[4:5], 0.0),
         )
         whole = whole + offset + jnp.where(own & (lane24 < MEM), left[0:1], 0.0)
-        moved = jnp.where((lane24 > 60) & (lane24 < 81), pltpu.roll(whole, 1, 1), 0.0)
+        moved = jnp.where((lane24 >= 64) & (lane24 < 84), pltpu.roll(whole, 4, 1), 0.0)
         whole = jnp.where(lane24 < 60, whole, moved)
         high = whole.astype(BF16).astype(F32)
         both = jnp.concatenate([high, whole - high], axis=0).astype(BF16)
@@ -436,15 +476,14 @@
     rounded_loc = lax.reduce_precision(weights_loc, 8, 7).reshape(OBS * TOP)
     coef = (weights_loc / jnp.sum(weights_loc, axis=1, keepdims=True)).reshape(OBS * TOP)
     targets = tile_lists.reshape(OBS * TOP)
+    maps = jnp.where(group < GROUPS // 2, *(jnp.asarray(each, BF16) for each in pack_maps()))
     packed, every = gram_call(
-        place,
         targets,
         rounded_loc,
         pad_lanes(precision_pc[None], WIDE),
+        maps,
         innovation,
-        perturbed,
-        next1,
-        next2,
+        lay_call(place, perturbed, next1, next2),
         across,
     )
     arrived = lax.all_to_all(

time: 147 us -> 141 us (0.959)
  Pallas kernels: 20.4 us -> 17.1 us
  waiting for transfers between devices: 12.7 us -> 10.9 us
    pallas_call x1, Pallas kernels: 9.86 us -> 3.8 us  [gram_call(): pl.pallas_call(gram_kernel, out_shape=(packed, jax.ShapeDtypeStruct((OBS,...]
    pallas_call x0 -> x1, Pallas kernels: none -> 2.78 us  [lay_call(): pl.pallas_call(lay_kernel, out_shape=jax.ShapeDtypeStruct((WIDE // 128, O...]
    ppermute x5, waiting for transfers between devices: 10.5 us -> 8.68 us  [turn(): return lax.ppermute(value, ('core', 'mem'), pairs)]
  transfers between devices with their start and end apart: 8 -> 8, of which waited for: 6 -> 5; matrix products, arithmetic and copies ran while one was open for 1% -> 1% of each run, Pallas kernels for 1% -> 3%
where the time goes in v3:
time: 141 us
  blocking collectives  65.8 us (47%)
  starting transfers between devices  40.1 us (28%)
  Pallas kernels  17.1 us (12%)
  waiting for transfers between devices  10.9 us (8%)
  local copies, waits for them, and re-layouts  2.88 us (2%)
  other arithmetic  2.06 us (1%)
    all_to_all x1, blocking collectives, body(): lax.all_to_all(packed.astype(BF16), ('y', 'z', 'core'), split_axis=0, con...  33.1 us
    ppermute x3, starting transfers between devices, swap(): return lax.ppermute(value, 'core', [(0, 1), (1, 0)])  20.8 us
    ppermute x5, starting transfers between devices, turn(): return lax.ppermute(value, ('core', 'mem'), pairs)  19.3 us
    all_to_all x1, blocking collectives, body(): lax.all_to_all(jnp.broadcast_to(weights[None], (CHIPS, 16, 128)), ('y', '...  17.2 us
    all_to_all x2, blocking collectives, to_groups(): lax.all_to_all(copies, 'mem', split_axis=0, concat_axis=0, tiled=True)  15.6 us
    ppermute x5, waiting for transfers between devices, turn(): return lax.ppermute(value, ('core', 'mem'), pairs)  8.68 us
    pallas_call x1, Pallas kernels, gram_call(): pl.pallas_call(gram_kernel, out_shape=(packed, jax.ShapeDtypeStruct((OBS,...  3.8 us
    pallas_call x1, Pallas kernels, mix_call(): pl.pallas_call(mix_kernel, out_shape=jax.ShapeDtypeStruct((MEM, OBS, COMP...  3.51 us
  transfers between devices with their start and end apart: 8, of which 5 were waited for; matrix products, arithmetic and copies ran while one was open for 1% of the time, Pallas kernels for 3%

profile of v3, /device:TPU:1, one launch (start us, length us, event | category | flops | bytes accessed | tf_op | source)
XLA Modules:
  0.0 140.6 jit_solution(699637250724048416)
XLA Ops:
  0.0 1.8 %pad_select_fusion.own = bf16[304,1152]{1,0:T(8,128)(2,1)S(1)} fusion(bf16[300,1088]{1,0:T(8,128)(2,1)} %bitcast.14, pred[]{:T(512)S(6)} %eq.3), kind=kLoop, calls=%fused_computation | loop fusion | flops 350208 | bytes 1353217 | tf_op jit(solution)/shard_map/jit(_where)/select_n | solution.py:456
  1.8 5.2 %collective-permute-start = (bf16[304,1152]{1,0:T(8,128)(2,1)S(1)}, bf16[304,1152]{1,0:T(8,128)(2,1)S(1)}, u32[]{:S(2)}, u32[]{:S(2)}) collective-permute-start(bf16[304,1152]{1,0:T(8,128)(2,1)S(1)} %pad_select_fusion.own), channel_id=1, source_target_pairs={{0,1},{1,2},{2,3},{3,0},{4,7},{5,4},{6,5},{7,6},{8,9},{9,10},{10,1... | collective-permute-start | bytes 2101256 | tf_op jit(solution)/shard_map/ppermute | solution.py:436
  7.0 1.4 fusion.2
  8.5 2.2 %copy-done.1 = bf16[24,20,4352]{2,0,1:T(8,128)(2,1)S(1)} copy-done((bf16[24,20,4352]{2,0,1:T(8,128)(2,1)S(1)}, bf16[24,20,4352]{2,0,1:T(8,128)(2,1)}, u32[]{:S(2)}) %copy-start.1) | copy-done | bytes 4177944
  10.7 1.3 scores_own.1.first
  12.0 3.0 %collective-permute-done.beside1 = bf16[304,1152]{1,0:T(8,128)(2,1)S(1)} collective-permute-done((bf16[304,1152]{1,0:T(8,128)(2,1)S(1)}, bf16[304,1152]{1,0:T(8,128)(2,1)S(1)}, u32[]{:S(2)}, u32[]{:S(2)}) %collective-permute-start) | collective-permute-done | bytes 700448 | tf_op jit(solution)/shard_map/ppermute | solution.py:436
  15.1 5.2 %collective-permute-start.2 = (bf16[160,1152]{1,0:T(8,128)(2,1)S(1)}, bf16[160,1152]{1,0:T(8,128)(2,1)S(1)}, u32[]{:S(2)}, u32[]{:S(2)}) collective-permute-start(bf16[160,1152]{1,0:T(8,128)(2,1)S(1)} %constant_dynamic-slice_fusion), channel_id=1, source_target_pairs={{0,1},{1,2},{2,3},{3,0},{4,7},{5,4},{6,5},{7,6},{8,9},{9,10},{10,1... | collective-permute-start | bytes 1105928 | tf_op jit(solution)/shard_map/ppermute | solution.py:436
  20.2 6.6 %collective-permute-start.1 = (bf16[304,1152]{1,0:T(8,128)(2,1)S(1)}, bf16[304,1152]{1,0:T(8,128)(2,1)S(1)}, u32[]{:S(2)}, u32[]{:S(2)}) collective-permute-start(bf16[304,1152]{1,0:T(8,128)(2,1)S(1)} %collective-permute-done.beside1), channel_id=1, source_target_pairs={{0,4},{4,0},{1,5},{5,1},{2,6},{6,2},{3,7},{7,3},{8,12},{12,8},{9,1... | collective-permute-start | bytes 2101256 | tf_op jit(solution)/shard_map/ppermute | solution.py:430
  26.9 8.7 %collective-permute-start.3 = (bf16[160,1152]{1,0:T(8,128)(2,1)S(1)}, bf16[160,1152]{1,0:T(8,128)(2,1)S(1)}, u32[]{:S(2)}, u32[]{:S(2)}) collective-permute-start(bf16[160,1152]{1,0:T(8,128)(2,1)S(1)} %collective-permute-done.2.far1), channel_id=1, source_target_pairs={{0,4},{4,0},{1,5},{5,1},{2,6},{6,2},{3,7},{7,3},{8,12},{12,8},{9,1... | collective-permute-start | bytes 1105928 | tf_op jit(solution)/shard_map/ppermute | solution.py:430
  35.6 1.3 collective-permute-done.3.far2
  36.8 2.7 %scores.1 = (f32[20,24,304]{2,1,0:T(8,128)S(1)}, f32[24,304]{1,0:T(8,128)S(1)}) custom-call(s32[2]{0:T(128)S(1)} %pad_add_fusion.place, bf16[480,4352]{1,0:T(8,128)(2,1)S(1)} %bitcast.12, f32[480,304]{1,0:T(8,128)S(1)} %scores_own.1.first, bf16[304,1152]{1,0:T(8,128)(2,1)S(1)} %collective-permute-done.beside1, ...), custom_call_target="tpu_custom_call" | custom-call | tf_op jit(solution)/shard_map/scores/pallas_call | solution.py:99
  39.6 9.0 %all_to_all.20.parts = f32[4,2,24,304]{3,2,1,0:T(8,128)S(1)} all-to-all(f32[4,2,24,304]{3,2,1,0:T(8,128)S(1)} %broadcast_in_dim.9), channel_id=1, replica_groups=mesh['y'=8,'z'=8,'core'=2,'mem'=4] {'mem'}, dimensions={0} | all-to-all | bytes 466944 | tf_op jit(solution)/shard_map/all_to_all | solution.py:441
  48.6 2.8 %collective-permute-start.4 = (bf16[20,24,384]{2,1,0:T(8,128)(2,1)S(1)}, bf16[20,24,384]{2,1,0:T(8,128)(2,1)S(1)}, u32[]{:S(2)}, u32[]{:S(2)}) collective-permute-start(bf16[20,24,384]{2,1,0:T(8,128)(2,1)S(1)} %get-tuple-element.21.own), channel_id=1, source_target_pairs={{0,1},{1,2},{2,3},{3,0},{4,7},{5,4},{6,5},{7,6},{8,9},{9,10},{10,1... | collective-permute-start | bytes 1105928 | tf_op jit(solution)/shard_map/ppermute | solution.py:436
  51.5 2.5 %collective-permute-start.5 = (bf16[20,24,384]{2,1,0:T(8,128)(2,1)S(1)}, bf16[20,24,384]{2,1,0:T(8,128)(2,1)S(1)}, u32[]{:S(2)}, u32[]{:S(2)}) collective-permute-start(bf16[20,24,384]{2,1,0:T(8,128)(2,1)S(1)} %get-tuple-element.21.own), channel_id=1, source_target_pairs={{0,3},{1,0},{2,1},{3,2},{4,5},{5,6},{6,7},{7,4},{8,11},{9,8},{10,9... | collective-permute-start | bytes 1105928 | tf_op jit(solution)/shard_map/ppermute | solution.py:436
  54.0 3.2 %collective-permute-done.4.n1 = bf16[20,24,384]{2,1,0:T(8,128)(2,1)S(1)} collective-permute-done((bf16[20,24,384]{2,1,0:T(8,128)(2,1)S(1)}, bf16[20,24,384]{2,1,0:T(8,128)(2,1)S(1)}, u32[]{:S(2)}, u32[]{:S(2)}) %collective-permute-start.4) | collective-permute-done | bytes 368672 | tf_op jit(solution)/shard_map/ppermute | solution.py:436
  57.2 3.7 %collective-permute-start.6 = (bf16[20,24,384]{2,1,0:T(8,128)(2,1)S(1)}, bf16[20,24,384]{2,1,0:T(8,128)(2,1)S(1)}, u32[]{:S(2)}, u32[]{:S(2)}) collective-permute-start(bf16[20,24,384]{2,1,0:T(8,128)(2,1)S(1)} %collective-permute-done.4.n1), channel_id=1, source_target_pairs={{0,1},{1,2},{2,3},{3,0},{4,7},{5,4},{6,5},{7,6},{8,9},{9,10},{10,1... | collective-permute-start | bytes 1105928 | tf_op jit(solution)/shard_map/ppermute | solution.py:436
  61.0 0.1 reshape.18.loc
  61.1 0.1 copy.12
  61.2 0.1 reshape.16.targets
  61.3 2.5 %collective-permute-done.5.n2 = bf16[20,24,384]{2,1,0:T(8,128)(2,1)S(1)} collective-permute-done((bf16[20,24,384]{2,1,0:T(8,128)(2,1)S(1)}, bf16[20,24,384]{2,1,0:T(8,128)(2,1)S(1)}, u32[]{:S(2)}, u32[]{:S(2)}) %collective-permute-start.5) | collective-permute-done | bytes 368672 | tf_op jit(solution)/shard_map/ppermute | solution.py:436
  63.9 2.8 %lay.1.rows = f32[3,1536,128]{2,1,0:T(8,128)S(1)} custom-call(s32[2]{0:T(128)S(1)} %pad_add_fusion.place, bf16[20,24,384]{2,1,0:T(8,128)(2,1)S(1)} %get-tuple-element.21.own, bf16[20,24,384]{2,1,0:T(8,128)(2,1)S(1)} %collective-permute-done.4.n1, bf16[20,24,384]{2,1,0:T(8,128)(2,1)S(1)} %collective-permute-done.5.n2), custom_call_target="tpu_custom_call" | custom-call | flops 1000000 | bytes 6000000 | tf_op jit(solution)/shard_map/lay/pallas_call | solution.py:163
  66.7 3.8 %gram.1 = (f32[128,8,128]{2,1,0:T(8,128)S(1)}, bf16[24,96,384]{2,1,0:T(8,128)(2,1)S(1)}) custom-call(s32[72]{0:T(128)S(1)} %reshape.16.targets, f32[72]{0:T(128)S(1)} %reshape.18.loc, f32[1,384]{1,0:T(1,128)S(1)} %pad.16.precision, bf16[768,128]{1,0:T(8,128)(2,1)S(1)} %broadcast_select_fusion.maps, bf16[24,384]{1,0:T(8,128)(2,1)S(1)} %get-tuple-element.20.innov, ...), custom_call_target="tpu_custom_call" | custom-call | tf_op jit(solution)/shard_map/gram/pallas_call | solution.py:258
  70.5 33.1 %all_to_all.21 = bf16[128,8,128]{2,1,0:T(8,128)(2,1)S(1)} all-to-all(bf16[128,8,128]{2,1,0:T(8,128)(2,1)S(1)} %convert_element_type.18), channel_id=1, replica_groups=mesh['y'=8,'z'=8,'core'=2,'mem'=4] {'y','z','core'}, dimensions={0} | all-to-all | bytes 524288 | tf_op jit(solution)/shard_map/all_to_all | solution.py:489
  103.5 0.1 convert_reduce_fusion
  103.7 6.6 %all_to_all.22.gathered = f32[4,8,128]{2,1,0:T(8,128)S(1)} all-to-all(f32[4,8,128]{2,1,0:T(8,128)S(1)} %broadcast_in_dim.10), channel_id=1, replica_groups=mesh['y'=8,'z'=8,'core'=2,'mem'=4] {'mem'}, dimensions={0} | all-to-all | bytes 32768 | tf_op jit(solution)/shard_map/all_to_all | solution.py:441
  110.2 3.0 %root.1 = bf16[16,128]{1,0:T(8,128)(2,1)S(1)} custom-call(s32[2]{0:T(128)S(1)} %pad_add_fusion.place, f32[4,8,128]{2,1,0:T(8,128)S(1)} %all_to_all.22.gathered), custom_call_target="tpu_custom_call" | custom-call | tf_op jit(solution)/shard_map/root/pallas_call | solution.py:355
  113.3 17.2 %all_to_all.23.mine = bf16[64,16,128]{2,1,0:T(8,128)(2,1)S(1)} all-to-all(bf16[64,16,128]{2,1,0:T(8,128)(2,1)S(1)} %broadcast_in_dim.11), channel_id=1, replica_groups=mesh['y'=8,'z'=8,'core'=2,'mem'=4] {'y','z'}, dimensions={0} | all-to-all | bytes 524288 | tf_op jit(solution)/shard_map/all_to_all | solution.py:494
  130.5 5.5 %collective-permute-start.7 = (bf16[64,16,128]{2,1,0:T(8,128)(2,1)S(1)}, bf16[64,16,128]{2,1,0:T(8,128)(2,1)S(1)}, u32[]{:S(2)}, u32[]{:S(2)}) collective-permute-start(bf16[64,16,128]{2,1,0:T(8,128)(2,1)S(1)} %all_to_all.23.mine), channel_id=1, source_target_pairs={{0,4},{4,0},{1,5},{5,1},{2,6},{6,2},{3,7},{7,3},{8,12},{12,8},{9,1... | collective-permute-start | bytes 786440 | tf_op jit(solution)/shard_map/ppermute | solution.py:430
  136.0 0.1 copy.13
  136.0 0.1 reshape.17.coef
  136.1 1.0 collective-permute-done.7.other
  137.1 3.5 %mix.1 = bf16[20,24,300]{2,1,0:T(8,128)(2,1)} custom-call(s32[2]{0:T(128)S(1)} %pad_add_fusion.place, s32[72]{0:T(128)S(1)} %reshape.16.targets, f32[72]{0:T(128)S(1)} %reshape.17.coef, bf16[64,16,128]{2,1,0:T(8,128)(2,1)S(1)} %all_to_all.23.mine, bf16[64,16,128]{2,1,0:T(8,128)(2,1)S(1)} %collective-permute-done.7.other, ...), custom_call_target="tpu_custom_call" | custom-call | tf_op jit(solution)/shard_map/mix/pallas_call | solution.py:418
  (31 shorter events, 0.5 us)
Async XLA Ops:
  0.0 7.0 %copy-start = (bf16[24,1088]{1,0:T(8,128)(2,1)S(1)}, bf16[24,1088]{1,0:T(8,128)(2,1)}, u32[]{:S(2)}) copy-start(bf16[24,1088]{1,0:T(8,128)(2,1)} %param.9) | copy-start | bytes 156676
  1.8 13.2 %collective-permute-start = (bf16[304,1152]{1,0:T(8,128)(2,1)S(1)}, bf16[304,1152]{1,0:T(8,128)(2,1)S(1)}, u32[]{:S(2)}, u32[]{:S(2)}) collective-permute-start(bf16[304,1152]{1,0:T(8,128)(2,1)S(1)} %pad_select_fusion.own), channel_id=1, source_target_pairs={{0,1},{1,2},{2,3},{3,0},{4,7},{5,4},{6,5},{7,6},{8,9},{9,10},{10,1... | collective-permute-start | bytes 2101256 | tf_op jit(solution)/shard_map/ppermute | solution.py:436
  8.5 2.2 %copy-start.1 = (bf16[24,20,4352]{2,0,1:T(8,128)(2,1)S(1)}, bf16[24,20,4352]{2,0,1:T(8,128)(2,1)}, u32[]{:S(2)}) copy-start(bf16[24,20,4352]{2,0,1:T(8,128)(2,1)} %param.8) | copy-start | bytes 12533764
  15.0 36.4 %copy-start.6 = (f32[300]{0:T(512)S(1)}, f32[300]{0:T(512)}, u32[]{:S(2)}) copy-start(f32[300]{0:T(512)} %param.11) | copy-start | bytes 3604
  15.0 36.5 %copy-start.4 = (s32[24,3]{0,1:T(4,128)S(1)}, s32[24,3]{0,1:T(4,128)}, u32[]{:S(2)}) copy-start(s32[24,3]{0,1:T(4,128)} %param.13) | copy-start | bytes 868
  15.0 46.1 %copy-start.5 = (s32[24,3]{0,1:T(4,128)S(1)}, s32[24,3]{0,1:T(4,128)}, u32[]{:S(2)}) copy-start(s32[24,3]{0,1:T(4,128)} %param.12) | copy-start | bytes 868
  15.0 46.2 %copy-start.2 = (bf16[768,128]{1,0:T(8,128)(2,1)S(1)}, bf16[768,128]{1,0:T(8,128)(2,1)}, u32[]{:S(2)}) copy-start(bf16[768,128]{1,0:T(8,128)(2,1)} %constant.37.clone) | copy-start | bytes 589828
  15.1 46.2 %copy-start.3 = (bf16[768,128]{1,0:T(8,128)(2,1)S(1)}, bf16[768,128]{1,0:T(8,128)(2,1)}, u32[]{:S(2)}) copy-start(bf16[768,128]{1,0:T(8,128)(2,1)} %constant.36.clone) | copy-start | bytes 589828
  15.1 11.8 %collective-permute-start.2 = (bf16[160,1152]{1,0:T(8,128)(2,1)S(1)}, bf16[160,1152]{1,0:T(8,128)(2,1)S(1)}, u32[]{:S(2)}, u32[]{:S(2)}) collective-permute-start(bf16[160,1152]{1,0:T(8,128)(2,1)S(1)} %constant_dynamic-slice_fusion), channel_id=1, source_target_pairs={{0,1},{1,2},{2,3},{3,0},{4,7},{5,4},{6,5},{7,6},{8,9},{9,10},{10,1... | collective-permute-start | bytes 1105928 | tf_op jit(solution)/shard_map/ppermute | solution.py:436
  20.2 15.3 %collective-permute-start.1 = (bf16[304,1152]{1,0:T(8,128)(2,1)S(1)}, bf16[304,1152]{1,0:T(8,128)(2,1)S(1)}, u32[]{:S(2)}, u32[]{:S(2)}) collective-permute-start(bf16[304,1152]{1,0:T(8,128)(2,1)S(1)} %collective-permute-done.beside1), channel_id=1, source_target_pairs={{0,4},{4,0},{1,5},{5,1},{2,6},{6,2},{3,7},{7,3},{8,12},{12,8},{9,1... | collective-permute-start | bytes 2101256 | tf_op jit(solution)/shard_map/ppermute | solution.py:430
  26.9 10.0 %collective-permute-start.3 = (bf16[160,1152]{1,0:T(8,128)(2,1)S(1)}, bf16[160,1152]{1,0:T(8,128)(2,1)S(1)}, u32[]{:S(2)}, u32[]{:S(2)}) collective-permute-start(bf16[160,1152]{1,0:T(8,128)(2,1)S(1)} %collective-permute-done.2.far1), channel_id=1, source_target_pairs={{0,4},{4,0},{1,5},{5,1},{2,6},{6,2},{3,7},{7,3},{8,12},{12,8},{9,1... | collective-permute-start | bytes 1105928 | tf_op jit(solution)/shard_map/ppermute | solution.py:430
  48.6 8.6 %collective-permute-start.4 = (bf16[20,24,384]{2,1,0:T(8,128)(2,1)S(1)}, bf16[20,24,384]{2,1,0:T(8,128)(2,1)S(1)}, u32[]{:S(2)}, u32[]{:S(2)}) collective-permute-start(bf16[20,24,384]{2,1,0:T(8,128)(2,1)S(1)} %get-tuple-element.21.own), channel_id=1, source_target_pairs={{0,1},{1,2},{2,3},{3,0},{4,7},{5,4},{6,5},{7,6},{8,9},{9,10},{10,1... | collective-permute-start | bytes 1105928 | tf_op jit(solution)/shard_map/ppermute | solution.py:436
  51.5 12.3 %collective-permute-start.5 = (bf16[20,24,384]{2,1,0:T(8,128)(2,1)S(1)}, bf16[20,24,384]{2,1,0:T(8,128)(2,1)S(1)}, u32[]{:S(2)}, u32[]{:S(2)}) collective-permute-start(bf16[20,24,384]{2,1,0:T(8,128)(2,1)S(1)} %get-tuple-element.21.own), channel_id=1, source_target_pairs={{0,3},{1,0},{2,1},{3,2},{4,5},{5,6},{6,7},{7,4},{8,11},{9,8},{10,9... | collective-permute-start | bytes 1105928 | tf_op jit(solution)/shard_map/ppermute | solution.py:436
  57.2 9.5 %collective-permute-start.6 = (bf16[20,24,384]{2,1,0:T(8,128)(2,1)S(1)}, bf16[20,24,384]{2,1,0:T(8,128)(2,1)S(1)}, u32[]{:S(2)}, u32[]{:S(2)}) collective-permute-start(bf16[20,24,384]{2,1,0:T(8,128)(2,1)S(1)} %collective-permute-done.4.n1), channel_id=1, source_target_pairs={{0,1},{1,2},{2,3},{3,0},{4,7},{5,4},{6,5},{7,6},{8,9},{9,10},{10,1... | collective-permute-start | bytes 1105928 | tf_op jit(solution)/shard_map/ppermute | solution.py:436
  130.5 6.6 %collective-permute-start.7 = (bf16[64,16,128]{2,1,0:T(8,128)(2,1)S(1)}, bf16[64,16,128]{2,1,0:T(8,128)(2,1)S(1)}, u32[]{:S(2)}, u32[]{:S(2)}) collective-permute-start(bf16[64,16,128]{2,1,0:T(8,128)(2,1)S(1)} %all_to_all.23.mine), channel_id=1, source_target_pairs={{0,4},{4,0},{1,5},{5,1},{2,6},{6,2},{3,7},{7,3},{8,12},{12,8},{9,1... | collective-permute-start | bytes 786440 | tf_op jit(solution)/shard_map/ppermute | solution.py:430

commit v4 on v3

--- a/solution.py
+++ b/solution.py
@@ -235,7 +235,7 @@
             acc[index, 8:16, :] += part[8:16]
         return carry
 
-    lax.fori_loop(0, OBS, footprint, 0, unroll=4)
+    lax.fori_loop(0, OBS, footprint, 0, unroll=8)
     for t in range(0, 2 * CHIPS, 16):
         top, middle = acc[t : t + 16, 0:8, :], acc[t : t + 16, 8:16, :]
         low_top = top - top.astype(BF16).astype(F32)
@@ -406,7 +406,7 @@
                 ]
         return carry
 
-    lax.fori_loop(0, OBS, footprint, 0, unroll=4)
+    lax.fori_loop(0, OBS, footprint, 0, unroll=12)
     for m in range(MEM):
         wide = jnp.concatenate(
             [rows[lane, m * OBS : (m + 1) * OBS, :] for lane in range(WIDE // 128)], axis=1

time: 141 us -> 140 us (level)
  transfers between devices with their start and end apart: 8 -> 8, of which waited for: 5 -> 5; matrix products, arithmetic and copies ran while one was open for 1% -> 2% of each run, Pallas kernels for 3% -> 3%
where the time goes in v4:
time: 140 us; the launch traced here: 139 us
  blocking collectives  65.8 us (47%)
  starting transfers between devices  40.1 us (29%)
  Pallas kernels  15.7 us (11%)
  waiting for transfers between devices  10.9 us (8%)
  local copies, waits for them, and re-layouts  2.88 us (2%)
  other arithmetic  2.06 us (1%)
    all_to_all x1, blocking collectives, body(): lax.all_to_all(packed.astype(BF16), ('y', 'z', 'core'), split_axis=0, con...  33.1 us
    ppermute x3, starting transfers between devices, swap(): return lax.ppermute(value, 'core', [(0, 1), (1, 0)])  20.8 us
    ppermute x5, starting transfers between devices, turn(): return lax.ppermute(value, ('core', 'mem'), pairs)  19.3 us
    all_to_all x1, blocking collectives, body(): lax.all_to_all(jnp.broadcast_to(weights[None], (CHIPS, 16, 128)), ('y', '...  17.2 us
    all_to_all x2, blocking collectives, to_groups(): lax.all_to_all(copies, 'mem', split_axis=0, concat_axis=0, tiled=True)  15.6 us
    ppermute x5, waiting for transfers between devices, turn(): return lax.ppermute(value, ('core', 'mem'), pairs)  8.68 us
    pallas_call x1, Pallas kernels, gram_call(): pl.pallas_call(gram_kernel, out_shape=(packed, jax.ShapeDtypeStruct((OBS,...  3.36 us
    pallas_call x1, Pallas kernels, root_call(): pl.pallas_call(root_kernel, out_shape=jax.ShapeDtypeStruct((16, 128), BF1...  2.96 us
  transfers between devices with their start and end apart: 8, of which 5 were waited for; matrix products, arithmetic and copies ran while one was open for 2% of the time, Pallas kernels for 3%

profile of v4, /device:TPU:1, one launch (start us, length us, event | category | flops | bytes accessed | tf_op | source)
XLA Modules:
  0.0 139.2 jit_solution(5818512212593004201)
XLA Ops:
  0.0 1.8 %pad_select_fusion.own = bf16[304,1152]{1,0:T(8,128)(2,1)S(1)} fusion(bf16[300,1088]{1,0:T(8,128)(2,1)} %bitcast.14, pred[]{:T(512)S(6)} %eq.3), kind=kLoop, calls=%fused_computation | loop fusion | flops 350208 | bytes 1353217 | tf_op jit(solution)/shard_map/jit(_where)/select_n | solution.py:456
  1.8 5.2 %collective-permute-start = (bf16[304,1152]{1,0:T(8,128)(2,1)S(1)}, bf16[304,1152]{1,0:T(8,128)(2,1)S(1)}, u32[]{:S(2)}, u32[]{:S(2)}) collective-permute-start(bf16[304,1152]{1,0:T(8,128)(2,1)S(1)} %pad_select_fusion.own), channel_id=1, source_target_pairs={{0,1},{1,2},{2,3},{3,0},{4,7},{5,4},{6,5},{7,6},{8,9},{9,10},{10,1... | collective-permute-start | bytes 2101256 | tf_op jit(solution)/shard_map/ppermute | solution.py:436
  7.0 1.4 %fusion.2 = f32[24,300]{1,0:T(8,128)S(1)} fusion(bf16[24,1088]{1,0:T(8,128)(2,1)S(1)} %copy-done, bf16[1088,300]{0,1:T(8,128)(2,1)} %param.10), kind=kOutput, calls=%fused_computation.10 | convolution fusion | flops 15667200 | bytes 733824 | tf_op jit(solution)/shard_map/dot_general | solution.py:463
  8.5 2.2 %copy-done.1 = bf16[24,20,4352]{2,0,1:T(8,128)(2,1)S(1)} copy-done((bf16[24,20,4352]{2,0,1:T(8,128)(2,1)S(1)}, bf16[24,20,4352]{2,0,1:T(8,128)(2,1)}, u32[]{:S(2)}) %copy-start.1) | copy-done | bytes 4177944
  10.7 1.3 scores_own.1.first
  12.0 3.0 %collective-permute-done.beside1 = bf16[304,1152]{1,0:T(8,128)(2,1)S(1)} collective-permute-done((bf16[304,1152]{1,0:T(8,128)(2,1)S(1)}, bf16[304,1152]{1,0:T(8,128)(2,1)S(1)}, u32[]{:S(2)}, u32[]{:S(2)}) %collective-permute-start) | collective-permute-done | bytes 700448 | tf_op jit(solution)/shard_map/ppermute | solution.py:436
  15.1 5.2 %collective-permute-start.2 = (bf16[160,1152]{1,0:T(8,128)(2,1)S(1)}, bf16[160,1152]{1,0:T(8,128)(2,1)S(1)}, u32[]{:S(2)}, u32[]{:S(2)}) collective-permute-start(bf16[160,1152]{1,0:T(8,128)(2,1)S(1)} %constant_dynamic-slice_fusion), channel_id=1, source_target_pairs={{0,1},{1,2},{2,3},{3,0},{4,7},{5,4},{6,5},{7,6},{8,9},{9,10},{10,1... | collective-permute-start | bytes 1105928 | tf_op jit(solution)/shard_map/ppermute | solution.py:436
  20.2 6.6 %collective-permute-start.1 = (bf16[304,1152]{1,0:T(8,128)(2,1)S(1)}, bf16[304,1152]{1,0:T(8,128)(2,1)S(1)}, u32[]{:S(2)}, u32[]{:S(2)}) collective-permute-start(bf16[304,1152]{1,0:T(8,128)(2,1)S(1)} %collective-permute-done.beside1), channel_id=1, source_target_pairs={{0,4},{4,0},{1,5},{5,1},{2,6},{6,2},{3,7},{7,3},{8,12},{12,8},{9,1... | collective-permute-start | bytes 2101256 | tf_op jit(solution)/shard_map/ppermute | solution.py:430
  26.9 8.7 %collective-permute-start.3 = (bf16[160,1152]{1,0:T(8,128)(2,1)S(1)}, bf16[160,1152]{1,0:T(8,128)(2,1)S(1)}, u32[]{:S(2)}, u32[]{:S(2)}) collective-permute-start(bf16[160,1152]{1,0:T(8,128)(2,1)S(1)} %collective-permute-done.2.far1), channel_id=1, source_target_pairs={{0,4},{4,0},{1,5},{5,1},{2,6},{6,2},{3,7},{7,3},{8,12},{12,8},{9,1... | collective-permute-start | bytes 1105928 | tf_op jit(solution)/shard_map/ppermute | solution.py:430
  35.6 1.3 collective-permute-done.3.far2
  36.8 2.7 %scores.1 = (f32[20,24,304]{2,1,0:T(8,128)S(1)}, f32[24,304]{1,0:T(8,128)S(1)}) custom-call(s32[2]{0:T(128)S(1)} %pad_add_fusion.place, bf16[480,4352]{1,0:T(8,128)(2,1)S(1)} %bitcast.12, f32[480,304]{1,0:T(8,128)S(1)} %scores_own.1.first, bf16[304,1152]{1,0:T(8,128)(2,1)S(1)} %collective-permute-done.beside1, ...), custom_call_target="tpu_custom_call" | custom-call | tf_op jit(solution)/shard_map/scores/pallas_call | solution.py:99
  39.6 9.0 %all_to_all.20.parts = f32[4,2,24,304]{3,2,1,0:T(8,128)S(1)} all-to-all(f32[4,2,24,304]{3,2,1,0:T(8,128)S(1)} %broadcast_in_dim.9), channel_id=1, replica_groups=mesh['y'=8,'z'=8,'core'=2,'mem'=4] {'mem'}, dimensions={0} | all-to-all | bytes 466944 | tf_op jit(solution)/shard_map/all_to_all | solution.py:441
  48.6 2.8 %collective-permute-start.4 = (bf16[20,24,384]{2,1,0:T(8,128)(2,1)S(1)}, bf16[20,24,384]{2,1,0:T(8,128)(2,1)S(1)}, u32[]{:S(2)}, u32[]{:S(2)}) collective-permute-start(bf16[20,24,384]{2,1,0:T(8,128)(2,1)S(1)} %get-tuple-element.21.own), channel_id=1, source_target_pairs={{0,1},{1,2},{2,3},{3,0},{4,7},{5,4},{6,5},{7,6},{8,9},{9,10},{10,1... | collective-permute-start | bytes 1105928 | tf_op jit(solution)/shard_map/ppermute | solution.py:436
  51.5 2.5 %collective-permute-start.5 = (bf16[20,24,384]{2,1,0:T(8,128)(2,1)S(1)}, bf16[20,24,384]{2,1,0:T(8,128)(2,1)S(1)}, u32[]{:S(2)}, u32[]{:S(2)}) collective-permute-start(bf16[20,24,384]{2,1,0:T(8,128)(2,1)S(1)} %get-tuple-element.21.own), channel_id=1, source_target_pairs={{0,3},{1,0},{2,1},{3,2},{4,5},{5,6},{6,7},{7,4},{8,11},{9,8},{10,9... | collective-permute-start | bytes 1105928 | tf_op jit(solution)/shard_map/ppermute | solution.py:436
  54.0 3.2 %collective-permute-done.4.n1 = bf16[20,24,384]{2,1,0:T(8,128)(2,1)S(1)} collective-permute-done((bf16[20,24,384]{2,1,0:T(8,128)(2,1)S(1)}, bf16[20,24,384]{2,1,0:T(8,128)(2,1)S(1)}, u32[]{:S(2)}, u32[]{:S(2)}) %collective-permute-start.4) | collective-permute-done | bytes 368672 | tf_op jit(solution)/shard_map/ppermute | solution.py:436
  57.2 3.7 %collective-permute-start.6 = (bf16[20,24,384]{2,1,0:T(8,128)(2,1)S(1)}, bf16[20,24,384]{2,1,0:T(8,128)(2,1)S(1)}, u32[]{:S(2)}, u32[]{:S(2)}) collective-permute-start(bf16[20,24,384]{2,1,0:T(8,128)(2,1)S(1)} %collective-permute-done.4.n1), channel_id=1, source_target_pairs={{0,1},{1,2},{2,3},{3,0},{4,7},{5,4},{6,5},{7,6},{8,9},{9,10},{10,1... | collective-permute-start | bytes 1105928 | tf_op jit(solution)/shard_map/ppermute | solution.py:436
  60.9 0.1 copy.14
  61.0 0.1 reshape.18.loc
  61.1 0.1 copy.12
  61.2 0.1 reshape.16.targets
  61.3 2.5 %collective-permute-done.5.n2 = bf16[20,24,384]{2,1,0:T(8,128)(2,1)S(1)} collective-permute-done((bf16[20,24,384]{2,1,0:T(8,128)(2,1)S(1)}, bf16[20,24,384]{2,1,0:T(8,128)(2,1)S(1)}, u32[]{:S(2)}, u32[]{:S(2)}) %collective-permute-start.5) | collective-permute-done | bytes 368672 | tf_op jit(solution)/shard_map/ppermute | solution.py:436
  63.9 2.8 %lay.1.rows = f32[3,1536,128]{2,1,0:T(8,128)S(1)} custom-call(s32[2]{0:T(128)S(1)} %pad_add_fusion.place, bf16[20,24,384]{2,1,0:T(8,128)(2,1)S(1)} %get-tuple-element.21.own, bf16[20,24,384]{2,1,0:T(8,128)(2,1)S(1)} %collective-permute-done.4.n1, bf16[20,24,384]{2,1,0:T(8,128)(2,1)S(1)} %collective-permute-done.5.n2), custom_call_target="tpu_custom_call" | custom-call | flops 1000000 | bytes 6000000 | tf_op jit(solution)/shard_map/lay/pallas_call | solution.py:163
  66.7 3.4 %gram.1 = (f32[128,8,128]{2,1,0:T(8,128)S(1)}, bf16[24,96,384]{2,1,0:T(8,128)(2,1)S(1)}) custom-call(s32[72]{0:T(128)S(1)} %reshape.16.targets, f32[72]{0:T(128)S(1)} %reshape.18.loc, f32[1,384]{1,0:T(1,128)S(1)} %pad.16.precision, bf16[768,128]{1,0:T(8,128)(2,1)S(1)} %broadcast_select_fusion.maps, bf16[24,384]{1,0:T(8,128)(2,1)S(1)} %get-tuple-element.20.innov, ...), custom_call_target="tpu_custom_call" | custom-call | tf_op jit(solution)/shard_map/gram/pallas_call | solution.py:258
  70.1 33.1 %all_to_all.21 = bf16[128,8,128]{2,1,0:T(8,128)(2,1)S(1)} all-to-all(bf16[128,8,128]{2,1,0:T(8,128)(2,1)S(1)} %convert_element_type.18), channel_id=1, replica_groups=mesh['y'=8,'z'=8,'core'=2,'mem'=4] {'y','z','core'}, dimensions={0} | all-to-all | bytes 524288 | tf_op jit(solution)/shard_map/all_to_all | solution.py:489
  103.1 0.1 convert_reduce_fusion
  103.2 6.6 %all_to_all.22.gathered = f32[4,8,128]{2,1,0:T(8,128)S(1)} all-to-all(f32[4,8,128]{2,1,0:T(8,128)S(1)} %broadcast_in_dim.10), channel_id=1, replica_groups=mesh['y'=8,'z'=8,'core'=2,'mem'=4] {'mem'}, dimensions={0} | all-to-all | bytes 32768 | tf_op jit(solution)/shard_map/all_to_all | solution.py:441
  109.8 3.0 %root.1 = bf16[16,128]{1,0:T(8,128)(2,1)S(1)} custom-call(s32[2]{0:T(128)S(1)} %pad_add_fusion.place, f32[4,8,128]{2,1,0:T(8,128)S(1)} %all_to_all.22.gathered), custom_call_target="tpu_custom_call" | custom-call | tf_op jit(solution)/shard_map/root/pallas_call | solution.py:355
  112.8 17.2 %all_to_all.23.mine = bf16[64,16,128]{2,1,0:T(8,128)(2,1)S(1)} all-to-all(bf16[64,16,128]{2,1,0:T(8,128)(2,1)S(1)} %broadcast_in_dim.11), channel_id=1, replica_groups=mesh['y'=8,'z'=8,'core'=2,'mem'=4] {'y','z'}, dimensions={0} | all-to-all | bytes 524288 | tf_op jit(solution)/shard_map/all_to_all | solution.py:494
  130.0 5.5 %collective-permute-start.7 = (bf16[64,16,128]{2,1,0:T(8,128)(2,1)S(1)}, bf16[64,16,128]{2,1,0:T(8,128)(2,1)S(1)}, u32[]{:S(2)}, u32[]{:S(2)}) collective-permute-start(bf16[64,16,128]{2,1,0:T(8,128)(2,1)S(1)} %all_to_all.23.mine), channel_id=1, source_target_pairs={{0,4},{4,0},{1,5},{5,1},{2,6},{6,2},{3,7},{7,3},{8,12},{12,8},{9,1... | collective-permute-start | bytes 786440 | tf_op jit(solution)/shard_map/ppermute | solution.py:430
  135.6 0.1 reshape.17.coef
  135.7 1.0 collective-permute-done.7.other
  136.7 2.5 %mix.1 = bf16[20,24,300]{2,1,0:T(8,128)(2,1)} custom-call(s32[2]{0:T(128)S(1)} %pad_add_fusion.place, s32[72]{0:T(128)S(1)} %reshape.16.targets, f32[72]{0:T(128)S(1)} %reshape.17.coef, bf16[64,16,128]{2,1,0:T(8,128)(2,1)S(1)} %all_to_all.23.mine, bf16[64,16,128]{2,1,0:T(8,128)(2,1)S(1)} %collective-permute-done.7.other, ...), custom_call_target="tpu_custom_call" | custom-call | tf_op jit(solution)/shard_map/mix/pallas_call | solution.py:418
  (31 shorter events, 0.5 us)
Async XLA Ops:
  0.0 7.0 %copy-start = (bf16[24,1088]{1,0:T(8,128)(2,1)S(1)}, bf16[24,1088]{1,0:T(8,128)(2,1)}, u32[]{:S(2)}) copy-start(bf16[24,1088]{1,0:T(8,128)(2,1)} %param.9) | copy-start | bytes 156676
  1.8 13.2 %collective-permute-start = (bf16[304,1152]{1,0:T(8,128)(2,1)S(1)}, bf16[304,1152]{1,0:T(8,128)(2,1)S(1)}, u32[]{:S(2)}, u32[]{:S(2)}) collective-permute-start(bf16[304,1152]{1,0:T(8,128)(2,1)S(1)} %pad_select_fusion.own), channel_id=1, source_target_pairs={{0,1},{1,2},{2,3},{3,0},{4,7},{5,4},{6,5},{7,6},{8,9},{9,10},{10,1... | collective-permute-start | bytes 2101256 | tf_op jit(solution)/shard_map/ppermute | solution.py:436
  8.5 2.2 %copy-start.1 = (bf16[24,20,4352]{2,0,1:T(8,128)(2,1)S(1)}, bf16[24,20,4352]{2,0,1:T(8,128)(2,1)}, u32[]{:S(2)}) copy-start(bf16[24,20,4352]{2,0,1:T(8,128)(2,1)} %param.8) | copy-start | bytes 12533764
  15.0 36.4 %copy-start.6 = (f32[300]{0:T(512)S(1)}, f32[300]{0:T(512)}, u32[]{:S(2)}) copy-start(f32[300]{0:T(512)} %param.11) | copy-start | bytes 3604
  15.0 36.5 %copy-start.4 = (s32[24,3]{0,1:T(4,128)S(1)}, s32[24,3]{0,1:T(4,128)}, u32[]{:S(2)}) copy-start(s32[24,3]{0,1:T(4,128)} %param.13) | copy-start | bytes 868
  15.0 46.1 %copy-start.5 = (s32[24,3]{0,1:T(4,128)S(1)}, s32[24,3]{0,1:T(4,128)}, u32[]{:S(2)}) copy-start(s32[24,3]{0,1:T(4,128)} %param.12) | copy-start | bytes 868
  15.0 46.2 %copy-start.2 = (bf16[768,128]{1,0:T(8,128)(2,1)S(1)}, bf16[768,128]{1,0:T(8,128)(2,1)}, u32[]{:S(2)}) copy-start(bf16[768,128]{1,0:T(8,128)(2,1)} %constant.37.clone) | copy-start | bytes 589828
  15.1 46.2 %copy-start.3 = (bf16[768,128]{1,0:T(8,128)(2,1)S(1)}, bf16[768,128]{1,0:T(8,128)(2,1)}, u32[]{:S(2)}) copy-start(bf16[768,128]{1,0:T(8,128)(2,1)} %constant.36.clone) | copy-start | bytes 589828
  15.1 11.8 %collective-permute-start.2 = (bf16[160,1152]{1,0:T(8,128)(2,1)S(1)}, bf16[160,1152]{1,0:T(8,128)(2,1)S(1)}, u32[]{:S(2)}, u32[]{:S(2)}) collective-permute-start(bf16[160,1152]{1,0:T(8,128)(2,1)S(1)} %constant_dynamic-slice_fusion), channel_id=1, source_target_pairs={{0,1},{1,2},{2,3},{3,0},{4,7},{5,4},{6,5},{7,6},{8,9},{9,10},{10,1... | collective-permute-start | bytes 1105928 | tf_op jit(solution)/shard_map/ppermute | solution.py:436
  20.2 15.3 %collective-permute-start.1 = (bf16[304,1152]{1,0:T(8,128)(2,1)S(1)}, bf16[304,1152]{1,0:T(8,128)(2,1)S(1)}, u32[]{:S(2)}, u32[]{:S(2)}) collective-permute-start(bf16[304,1152]{1,0:T(8,128)(2,1)S(1)} %collective-permute-done.beside1), channel_id=1, source_target_pairs={{0,4},{4,0},{1,5},{5,1},{2,6},{6,2},{3,7},{7,3},{8,12},{12,8},{9,1... | collective-permute-start | bytes 2101256 | tf_op jit(solution)/shard_map/ppermute | solution.py:430
  26.9 10.0 %collective-permute-start.3 = (bf16[160,1152]{1,0:T(8,128)(2,1)S(1)}, bf16[160,1152]{1,0:T(8,128)(2,1)S(1)}, u32[]{:S(2)}, u32[]{:S(2)}) collective-permute-start(bf16[160,1152]{1,0:T(8,128)(2,1)S(1)} %collective-permute-done.2.far1), channel_id=1, source_target_pairs={{0,4},{4,0},{1,5},{5,1},{2,6},{6,2},{3,7},{7,3},{8,12},{12,8},{9,1... | collective-permute-start | bytes 1105928 | tf_op jit(solution)/shard_map/ppermute | solution.py:430
  48.6 8.6 %collective-permute-start.4 = (bf16[20,24,384]{2,1,0:T(8,128)(2,1)S(1)}, bf16[20,24,384]{2,1,0:T(8,128)(2,1)S(1)}, u32[]{:S(2)}, u32[]{:S(2)}) collective-permute-start(bf16[20,24,384]{2,1,0:T(8,128)(2,1)S(1)} %get-tuple-element.21.own), channel_id=1, source_target_pairs={{0,1},{1,2},{2,3},{3,0},{4,7},{5,4},{6,5},{7,6},{8,9},{9,10},{10,1... | collective-permute-start | bytes 1105928 | tf_op jit(solution)/shard_map/ppermute | solution.py:436
  51.5 12.3 %collective-permute-start.5 = (bf16[20,24,384]{2,1,0:T(8,128)(2,1)S(1)}, bf16[20,24,384]{2,1,0:T(8,128)(2,1)S(1)}, u32[]{:S(2)}, u32[]{:S(2)}) collective-permute-start(bf16[20,24,384]{2,1,0:T(8,128)(2,1)S(1)} %get-tuple-element.21.own), channel_id=1, source_target_pairs={{0,3},{1,0},{2,1},{3,2},{4,5},{5,6},{6,7},{7,4},{8,11},{9,8},{10,9... | collective-permute-start | bytes 1105928 | tf_op jit(solution)/shard_map/ppermute | solution.py:436
  57.2 9.5 %collective-permute-start.6 = (bf16[20,24,384]{2,1,0:T(8,128)(2,1)S(1)}, bf16[20,24,384]{2,1,0:T(8,128)(2,1)S(1)}, u32[]{:S(2)}, u32[]{:S(2)}) collective-permute-start(bf16[20,24,384]{2,1,0:T(8,128)(2,1)S(1)} %collective-permute-done.4.n1), channel_id=1, source_target_pairs={{0,1},{1,2},{2,3},{3,0},{4,7},{5,4},{6,5},{7,6},{8,9},{9,10},{10,1... | collective-permute-start | bytes 1105928 | tf_op jit(solution)/shard_map/ppermute | solution.py:436
  130.0 6.6 %collective-permute-start.7 = (bf16[64,16,128]{2,1,0:T(8,128)(2,1)S(1)}, bf16[64,16,128]{2,1,0:T(8,128)(2,1)S(1)}, u32[]{:S(2)}, u32[]{:S(2)}) collective-permute-start(bf16[64,16,128]{2,1,0:T(8,128)(2,1)S(1)} %all_to_all.23.mine), channel_id=1, source_target_pairs={{0,4},{4,0},{1,5},{5,1},{2,6},{6,2},{3,7},{7,3},{8,12},{12,8},{9,1... | collective-permute-start | bytes 786440 | tf_op jit(solution)/shard_map/ppermute | solution.py:430

commit v5 on v4

--- a/solution.py
+++ b/solution.py
@@ -235,7 +235,7 @@
             acc[index, 8:16, :] += part[8:16]
         return carry
 
-    lax.fori_loop(0, OBS, footprint, 0, unroll=8)
+    lax.fori_loop(0, OBS, footprint, 0, unroll=12)
     for t in range(0, 2 * CHIPS, 16):
         top, middle = acc[t : t + 16, 0:8, :], acc[t : t + 16, 8:16, :]
         low_top = top - top.astype(BF16).astype(F32)
@@ -406,7 +406,7 @@
                 ]
         return carry
 
-    lax.fori_loop(0, OBS, footprint, 0, unroll=12)
+    lax.fori_loop(0, OBS, footprint, 0, unroll=24)
     for m in range(MEM):
         wide = jnp.concatenate(
             [rows[lane, m * OBS : (m + 1) * OBS, :] for lane in range(WIDE // 128)], axis=1
@@ -453,11 +453,9 @@
 
     turned = basis.T
     spare = ROWS - COMPS
-    own = jnp.where(
-        lax.rem(group, 2) == 1,
-        jnp.pad(turned, ((0, spare), (FRAME - BLOCK, 0))),
-        jnp.pad(turned, ((0, spare), (0, FRAME - BLOCK))),
-    )
+    edge = FRAME - BLOCK
+    framed = jnp.pad(turned, ((0, spare), (edge, edge)))
+    own = lax.dynamic_slice_in_dim(framed, edge * (1 - lax.rem(group, 2)), FRAME, 1)
     beside1 = turn(own)
     first = own_call(place, rad, own)
     obs_partial = pad_lanes(jnp.dot(observed, basis, preferred_element_type=F32), ROWS)

time: 140 us -> 139 us (level)
  other arithmetic: 2.06 us -> 0.31 us
  local copies, waits for them, and re-layouts: 2.88 us -> 4.33 us
    select_n x1 -> x0, other arithmetic: 1.75 us -> none  [body(): jnp.where(lax.rem(group, 2) == 1, jnp.pad(turned, ((0, spare), (FRAME - B...]
    dynamic_slice x0 -> x1, local copies, waits for them, and re-layouts: none -> 1.45 us  [body(): lax.dynamic_slice_in_dim(framed, edge * (1 - lax.rem(group, 2)), FRAME, 1)]
where the time goes in v5:
time: 139 us; the launch traced here: 138 us
  blocking collectives  65.8 us (47%)
  starting transfers between devices  40.1 us (29%)
  Pallas kernels  15.3 us (11%)
  waiting for transfers between devices  10.9 us (8%)
  local copies, waits for them, and re-layouts  4.33 us (3%)
  matrix products  1.4 us (1%)
    all_to_all x1, blocking collectives, body(): lax.all_to_all(packed.astype(BF16), ('y', 'z', 'core'), split_axis=0, con...  33 us
    ppermute x3, starting transfers between devices, swap(): return lax.ppermute(value, 'core', [(0, 1), (1, 0)])  20.8 us
    ppermute x5, starting transfers between devices, turn(): return lax.ppermute(value, ('core', 'mem'), pairs)  19.3 us
    all_to_all x1, blocking collectives, body(): lax.all_to_all(jnp.broadcast_to(weights[None], (CHIPS, 16, 128)), ('y', '...  17.2 us
    all_to_all x2, blocking collectives, to_groups(): lax.all_to_all(copies, 'mem', split_axis=0, concat_axis=0, tiled=True)  15.6 us
    ppermute x5, waiting for transfers between devices, turn(): return lax.ppermute(value, ('core', 'mem'), pairs)  8.68 us
    pallas_call x1, Pallas kernels, gram_call(): pl.pallas_call(gram_kernel, out_shape=(packed, jax.ShapeDtypeStruct((OBS,...  3.26 us
    pallas_call x1, Pallas kernels, root_call(): pl.pallas_call(root_kernel, out_shape=jax.ShapeDtypeStruct((16, 128), BF1...  2.96 us
  transfers between devices with their start and end apart: 8, of which 5 were waited for; matrix products, arithmetic and copies ran while one was open for 2% of the time, Pallas kernels for 3%

profile of v5, /device:TPU:1, one launch (start us, length us, event | category | flops | bytes accessed | tf_op | source)
XLA Modules:
  0.0 138.5 jit_solution(17345773777313660271)
XLA Ops:
  0.0 1.4 %pad_dynamic-slice_fusion.own = bf16[304,1152]{1,0:T(8,128)(2,1)S(1)} fusion(s32[]{:T(128)S(6)} %select_n.16, bf16[300,1088]{1,0:T(8,128)(2,1)} %bitcast.14), kind=kLoop, calls=%fused_computation | loop fusion | bytes 1353220 | tf_op jit(solution)/shard_map/dynamic_slice | solution.py:458
  1.5 5.2 %collective-permute-start = (bf16[304,1152]{1,0:T(8,128)(2,1)S(1)}, bf16[304,1152]{1,0:T(8,128)(2,1)S(1)}, u32[]{:S(2)}, u32[]{:S(2)}) collective-permute-start(bf16[304,1152]{1,0:T(8,128)(2,1)S(1)} %pad_dynamic-slice_fusion.own), channel_id=1, source_target_pairs={{0,1},{1,2},{2,3},{3,0},{4,7},{5,4},{6,5},{7,6},{8,9},{9,10},{10,1... | collective-permute-start | bytes 2101256 | tf_op jit(solution)/shard_map/ppermute | solution.py:436
  6.7 1.4 %fusion.2 = f32[24,300]{1,0:T(8,128)S(1)} fusion(bf16[24,1088]{1,0:T(8,128)(2,1)S(1)} %copy-done, bf16[1088,300]{0,1:T(8,128)(2,1)} %param.10), kind=kOutput, calls=%fused_computation.10 | convolution fusion | flops 15667200 | bytes 733824 | tf_op jit(solution)/shard_map/dot_general | solution.py:461
  8.2 2.2 %copy-done.1 = bf16[24,20,4352]{2,0,1:T(8,128)(2,1)S(1)} copy-done((bf16[24,20,4352]{2,0,1:T(8,128)(2,1)S(1)}, bf16[24,20,4352]{2,0,1:T(8,128)(2,1)}, u32[]{:S(2)}) %copy-start.1) | copy-done | bytes 4177944
  10.4 1.3 scores_own.1.first
  11.7 3.0 %collective-permute-done.beside1 = bf16[304,1152]{1,0:T(8,128)(2,1)S(1)} collective-permute-done((bf16[304,1152]{1,0:T(8,128)(2,1)S(1)}, bf16[304,1152]{1,0:T(8,128)(2,1)S(1)}, u32[]{:S(2)}, u32[]{:S(2)}) %collective-permute-start) | collective-permute-done | bytes 700448 | tf_op jit(solution)/shard_map/ppermute | solution.py:436
  14.8 5.2 %collective-permute-start.2 = (bf16[160,1152]{1,0:T(8,128)(2,1)S(1)}, bf16[160,1152]{1,0:T(8,128)(2,1)S(1)}, u32[]{:S(2)}, u32[]{:S(2)}) collective-permute-start(bf16[160,1152]{1,0:T(8,128)(2,1)S(1)} %constant_dynamic-slice_fusion), channel_id=1, source_target_pairs={{0,1},{1,2},{2,3},{3,0},{4,7},{5,4},{6,5},{7,6},{8,9},{9,10},{10,1... | collective-permute-start | bytes 1105928 | tf_op jit(solution)/shard_map/ppermute | solution.py:436
  19.9 6.6 %collective-permute-start.1 = (bf16[304,1152]{1,0:T(8,128)(2,1)S(1)}, bf16[304,1152]{1,0:T(8,128)(2,1)S(1)}, u32[]{:S(2)}, u32[]{:S(2)}) collective-permute-start(bf16[304,1152]{1,0:T(8,128)(2,1)S(1)} %collective-permute-done.beside1), channel_id=1, source_target_pairs={{0,4},{4,0},{1,5},{5,1},{2,6},{6,2},{3,7},{7,3},{8,12},{12,8},{9,1... | collective-permute-start | bytes 2101256 | tf_op jit(solution)/shard_map/ppermute | solution.py:430
  26.6 8.7 %collective-permute-start.3 = (bf16[160,1152]{1,0:T(8,128)(2,1)S(1)}, bf16[160,1152]{1,0:T(8,128)(2,1)S(1)}, u32[]{:S(2)}, u32[]{:S(2)}) collective-permute-start(bf16[160,1152]{1,0:T(8,128)(2,1)S(1)} %collective-permute-done.2.far1), channel_id=1, source_target_pairs={{0,4},{4,0},{1,5},{5,1},{2,6},{6,2},{3,7},{7,3},{8,12},{12,8},{9,1... | collective-permute-start | bytes 1105928 | tf_op jit(solution)/shard_map/ppermute | solution.py:430
  35.3 1.3 collective-permute-done.3.far2
  36.5 2.7 %scores.1 = (f32[20,24,304]{2,1,0:T(8,128)S(1)}, f32[24,304]{1,0:T(8,128)S(1)}) custom-call(s32[2]{0:T(128)S(1)} %pad_add_fusion.place, bf16[480,4352]{1,0:T(8,128)(2,1)S(1)} %bitcast.12, f32[480,304]{1,0:T(8,128)S(1)} %scores_own.1.first, bf16[304,1152]{1,0:T(8,128)(2,1)S(1)} %collective-permute-done.beside1, ...), custom_call_target="tpu_custom_call" | custom-call | tf_op jit(solution)/shard_map/scores/pallas_call | solution.py:99
  39.3 9.0 %all_to_all.20.parts = f32[4,2,24,304]{3,2,1,0:T(8,128)S(1)} all-to-all(f32[4,2,24,304]{3,2,1,0:T(8,128)S(1)} %broadcast_in_dim.9), channel_id=1, replica_groups=mesh['y'=8,'z'=8,'core'=2,'mem'=4] {'mem'}, dimensions={0} | all-to-all | bytes 466944 | tf_op jit(solution)/shard_map/all_to_all | solution.py:441
  48.3 2.8 %collective-permute-start.4 = (bf16[20,24,384]{2,1,0:T(8,128)(2,1)S(1)}, bf16[20,24,384]{2,1,0:T(8,128)(2,1)S(1)}, u32[]{:S(2)}, u32[]{:S(2)}) collective-permute-start(bf16[20,24,384]{2,1,0:T(8,128)(2,1)S(1)} %get-tuple-element.21.own), channel_id=1, source_target_pairs={{0,1},{1,2},{2,3},{3,0},{4,7},{5,4},{6,5},{7,6},{8,9},{9,10},{10,1... | collective-permute-start | bytes 1105928 | tf_op jit(solution)/shard_map/ppermute | solution.py:436
  51.2 2.5 %collective-permute-start.5 = (bf16[20,24,384]{2,1,0:T(8,128)(2,1)S(1)}, bf16[20,24,384]{2,1,0:T(8,128)(2,1)S(1)}, u32[]{:S(2)}, u32[]{:S(2)}) collective-permute-start(bf16[20,24,384]{2,1,0:T(8,128)(2,1)S(1)} %get-tuple-element.21.own), channel_id=1, source_target_pairs={{0,3},{1,0},{2,1},{3,2},{4,5},{5,6},{6,7},{7,4},{8,11},{9,8},{10,9... | collective-permute-start | bytes 1105928 | tf_op jit(solution)/shard_map/ppermute | solution.py:436
  53.7 3.2 %collective-permute-done.4.n1 = bf16[20,24,384]{2,1,0:T(8,128)(2,1)S(1)} collective-permute-done((bf16[20,24,384]{2,1,0:T(8,128)(2,1)S(1)}, bf16[20,24,384]{2,1,0:T(8,128)(2,1)S(1)}, u32[]{:S(2)}, u32[]{:S(2)}) %collective-permute-start.4) | collective-permute-done | bytes 368672 | tf_op jit(solution)/shard_map/ppermute | solution.py:436
  56.9 3.7 %collective-permute-start.6 = (bf16[20,24,384]{2,1,0:T(8,128)(2,1)S(1)}, bf16[20,24,384]{2,1,0:T(8,128)(2,1)S(1)}, u32[]{:S(2)}, u32[]{:S(2)}) collective-permute-start(bf16[20,24,384]{2,1,0:T(8,128)(2,1)S(1)} %collective-permute-done.4.n1), channel_id=1, source_target_pairs={{0,1},{1,2},{2,3},{3,0},{4,7},{5,4},{6,5},{7,6},{8,9},{9,10},{10,1... | collective-permute-start | bytes 1105928 | tf_op jit(solution)/shard_map/ppermute | solution.py:436
  60.6 0.1 copy.14
  60.7 0.1 reshape.18.loc
  60.8 0.1 copy.12
  60.9 0.1 reshape.16.targets
  61.0 2.5 %collective-permute-done.5.n2 = bf16[20,24,384]{2,1,0:T(8,128)(2,1)S(1)} collective-permute-done((bf16[20,24,384]{2,1,0:T(8,128)(2,1)S(1)}, bf16[20,24,384]{2,1,0:T(8,128)(2,1)S(1)}, u32[]{:S(2)}, u32[]{:S(2)}) %collective-permute-start.5) | collective-permute-done | bytes 368672 | tf_op jit(solution)/shard_map/ppermute | solution.py:436
  63.5 2.8 %lay.1.rows = f32[3,1536,128]{2,1,0:T(8,128)S(1)} custom-call(s32[2]{0:T(128)S(1)} %pad_add_fusion.place, bf16[20,24,384]{2,1,0:T(8,128)(2,1)S(1)} %get-tuple-element.21.own, bf16[20,24,384]{2,1,0:T(8,128)(2,1)S(1)} %collective-permute-done.4.n1, bf16[20,24,384]{2,1,0:T(8,128)(2,1)S(1)} %collective-permute-done.5.n2), custom_call_target="tpu_custom_call" | custom-call | flops 1000000 | bytes 6000000 | tf_op jit(solution)/shard_map/lay/pallas_call | solution.py:163
  66.3 3.3 %gram.1 = (f32[128,8,128]{2,1,0:T(8,128)S(1)}, bf16[24,96,384]{2,1,0:T(8,128)(2,1)S(1)}) custom-call(s32[72]{0:T(128)S(1)} %reshape.16.targets, f32[72]{0:T(128)S(1)} %reshape.18.loc, f32[1,384]{1,0:T(1,128)S(1)} %pad.12.precision, bf16[768,128]{1,0:T(8,128)(2,1)S(1)} %broadcast_select_fusion.maps, bf16[24,384]{1,0:T(8,128)(2,1)S(1)} %get-tuple-element.20.innov, ...), custom_call_target="tpu_custom_call" | custom-call | tf_op jit(solution)/shard_map/gram/pallas_call | solution.py:258
  69.7 33.0 %all_to_all.21 = bf16[128,8,128]{2,1,0:T(8,128)(2,1)S(1)} all-to-all(bf16[128,8,128]{2,1,0:T(8,128)(2,1)S(1)} %convert_element_type.16), channel_id=1, replica_groups=mesh['y'=8,'z'=8,'core'=2,'mem'=4] {'y','z','core'}, dimensions={0} | all-to-all | bytes 524288 | tf_op jit(solution)/shard_map/all_to_all | solution.py:487
  102.7 0.1 convert_reduce_fusion
  102.8 6.6 %all_to_all.22.gathered = f32[4,8,128]{2,1,0:T(8,128)S(1)} all-to-all(f32[4,8,128]{2,1,0:T(8,128)S(1)} %broadcast_in_dim.10), channel_id=1, replica_groups=mesh['y'=8,'z'=8,'core'=2,'mem'=4] {'mem'}, dimensions={0} | all-to-all | bytes 32768 | tf_op jit(solution)/shard_map/all_to_all | solution.py:441
  109.4 3.0 %root.1 = bf16[16,128]{1,0:T(8,128)(2,1)S(1)} custom-call(s32[2]{0:T(128)S(1)} %pad_add_fusion.place, f32[4,8,128]{2,1,0:T(8,128)S(1)} %all_to_all.22.gathered), custom_call_target="tpu_custom_call" | custom-call | tf_op jit(solution)/shard_map/root/pallas_call | solution.py:355
  112.4 17.2 %all_to_all.23.mine = bf16[64,16,128]{2,1,0:T(8,128)(2,1)S(1)} all-to-all(bf16[64,16,128]{2,1,0:T(8,128)(2,1)S(1)} %broadcast_in_dim.11), channel_id=1, replica_groups=mesh['y'=8,'z'=8,'core'=2,'mem'=4] {'y','z'}, dimensions={0} | all-to-all | bytes 524288 | tf_op jit(solution)/shard_map/all_to_all | solution.py:492
  129.6 5.5 %collective-permute-start.7 = (bf16[64,16,128]{2,1,0:T(8,128)(2,1)S(1)}, bf16[64,16,128]{2,1,0:T(8,128)(2,1)S(1)}, u32[]{:S(2)}, u32[]{:S(2)}) collective-permute-start(bf16[64,16,128]{2,1,0:T(8,128)(2,1)S(1)} %all_to_all.23.mine), channel_id=1, source_target_pairs={{0,4},{4,0},{1,5},{5,1},{2,6},{6,2},{3,7},{7,3},{8,12},{12,8},{9,1... | collective-permute-start | bytes 786440 | tf_op jit(solution)/shard_map/ppermute | solution.py:430
  135.2 0.1 reshape.17.coef
  135.3 1.0 collective-permute-done.7.other
  136.3 2.2 %mix.1 = bf16[20,24,300]{2,1,0:T(8,128)(2,1)} custom-call(s32[2]{0:T(128)S(1)} %pad_add_fusion.place, s32[72]{0:T(128)S(1)} %reshape.16.targets, f32[72]{0:T(128)S(1)} %reshape.17.coef, bf16[64,16,128]{2,1,0:T(8,128)(2,1)S(1)} %all_to_all.23.mine, bf16[64,16,128]{2,1,0:T(8,128)(2,1)S(1)} %collective-permute-done.7.other, ...), custom_call_target="tpu_custom_call" | custom-call | tf_op jit(solution)/shard_map/mix/pallas_call | solution.py:418
  (31 shorter events, 0.5 us)
Async XLA Ops:
  0.0 6.7 %copy-start = (bf16[24,1088]{1,0:T(8,128)(2,1)S(1)}, bf16[24,1088]{1,0:T(8,128)(2,1)}, u32[]{:S(2)}) copy-start(bf16[24,1088]{1,0:T(8,128)(2,1)} %param.9) | copy-start | bytes 156676
  1.5 13.2 %collective-permute-start = (bf16[304,1152]{1,0:T(8,128)(2,1)S(1)}, bf16[304,1152]{1,0:T(8,128)(2,1)S(1)}, u32[]{:S(2)}, u32[]{:S(2)}) collective-permute-start(bf16[304,1152]{1,0:T(8,128)(2,1)S(1)} %pad_dynamic-slice_fusion.own), channel_id=1, source_target_pairs={{0,1},{1,2},{2,3},{3,0},{4,7},{5,4},{6,5},{7,6},{8,9},{9,10},{10,1... | collective-permute-start | bytes 2101256 | tf_op jit(solution)/shard_map/ppermute | solution.py:436
  8.2 2.2 %copy-start.1 = (bf16[24,20,4352]{2,0,1:T(8,128)(2,1)S(1)}, bf16[24,20,4352]{2,0,1:T(8,128)(2,1)}, u32[]{:S(2)}) copy-start(bf16[24,20,4352]{2,0,1:T(8,128)(2,1)} %param.8) | copy-start | bytes 12533764
  14.7 36.4 %copy-start.6 = (f32[300]{0:T(512)S(1)}, f32[300]{0:T(512)}, u32[]{:S(2)}) copy-start(f32[300]{0:T(512)} %param.11) | copy-start | bytes 3604
  14.7 36.5 %copy-start.4 = (s32[24,3]{0,1:T(4,128)S(1)}, s32[24,3]{0,1:T(4,128)}, u32[]{:S(2)}) copy-start(s32[24,3]{0,1:T(4,128)} %param.13) | copy-start | bytes 868
  14.7 46.1 %copy-start.5 = (s32[24,3]{0,1:T(4,128)S(1)}, s32[24,3]{0,1:T(4,128)}, u32[]{:S(2)}) copy-start(s32[24,3]{0,1:T(4,128)} %param.12) | copy-start | bytes 868
  14.7 46.2 %copy-start.2 = (bf16[768,128]{1,0:T(8,128)(2,1)S(1)}, bf16[768,128]{1,0:T(8,128)(2,1)}, u32[]{:S(2)}) copy-start(bf16[768,128]{1,0:T(8,128)(2,1)} %constant.41.clone) | copy-start | bytes 589828
  14.8 46.2 %copy-start.3 = (bf16[768,128]{1,0:T(8,128)(2,1)S(1)}, bf16[768,128]{1,0:T(8,128)(2,1)}, u32[]{:S(2)}) copy-start(bf16[768,128]{1,0:T(8,128)(2,1)} %constant.40.clone) | copy-start | bytes 589828
  14.8 11.8 %collective-permute-start.2 = (bf16[160,1152]{1,0:T(8,128)(2,1)S(1)}, bf16[160,1152]{1,0:T(8,128)(2,1)S(1)}, u32[]{:S(2)}, u32[]{:S(2)}) collective-permute-start(bf16[160,1152]{1,0:T(8,128)(2,1)S(1)} %constant_dynamic-slice_fusion), channel_id=1, source_target_pairs={{0,1},{1,2},{2,3},{3,0},{4,7},{5,4},{6,5},{7,6},{8,9},{9,10},{10,1... | collective-permute-start | bytes 1105928 | tf_op jit(solution)/shard_map/ppermute | solution.py:436
  19.9 15.3 %collective-permute-start.1 = (bf16[304,1152]{1,0:T(8,128)(2,1)S(1)}, bf16[304,1152]{1,0:T(8,128)(2,1)S(1)}, u32[]{:S(2)}, u32[]{:S(2)}) collective-permute-start(bf16[304,1152]{1,0:T(8,128)(2,1)S(1)} %collective-permute-done.beside1), channel_id=1, source_target_pairs={{0,4},{4,0},{1,5},{5,1},{2,6},{6,2},{3,7},{7,3},{8,12},{12,8},{9,1... | collective-permute-start | bytes 2101256 | tf_op jit(solution)/shard_map/ppermute | solution.py:430
  26.6 10.0 %collective-permute-start.3 = (bf16[160,1152]{1,0:T(8,128)(2,1)S(1)}, bf16[160,1152]{1,0:T(8,128)(2,1)S(1)}, u32[]{:S(2)}, u32[]{:S(2)}) collective-permute-start(bf16[160,1152]{1,0:T(8,128)(2,1)S(1)} %collective-permute-done.2.far1), channel_id=1, source_target_pairs={{0,4},{4,0},{1,5},{5,1},{2,6},{6,2},{3,7},{7,3},{8,12},{12,8},{9,1... | collective-permute-start | bytes 1105928 | tf_op jit(solution)/shard_map/ppermute | solution.py:430
  48.3 8.6 %collective-permute-start.4 = (bf16[20,24,384]{2,1,0:T(8,128)(2,1)S(1)}, bf16[20,24,384]{2,1,0:T(8,128)(2,1)S(1)}, u32[]{:S(2)}, u32[]{:S(2)}) collective-permute-start(bf16[20,24,384]{2,1,0:T(8,128)(2,1)S(1)} %get-tuple-element.21.own), channel_id=1, source_target_pairs={{0,1},{1,2},{2,3},{3,0},{4,7},{5,4},{6,5},{7,6},{8,9},{9,10},{10,1... | collective-permute-start | bytes 1105928 | tf_op jit(solution)/shard_map/ppermute | solution.py:436
  51.2 12.3 %collective-permute-start.5 = (bf16[20,24,384]{2,1,0:T(8,128)(2,1)S(1)}, bf16[20,24,384]{2,1,0:T(8,128)(2,1)S(1)}, u32[]{:S(2)}, u32[]{:S(2)}) collective-permute-start(bf16[20,24,384]{2,1,0:T(8,128)(2,1)S(1)} %get-tuple-element.21.own), channel_id=1, source_target_pairs={{0,3},{1,0},{2,1},{3,2},{4,5},{5,6},{6,7},{7,4},{8,11},{9,8},{10,9... | collective-permute-start | bytes 1105928 | tf_op jit(solution)/shard_map/ppermute | solution.py:436
  56.9 9.5 %collective-permute-start.6 = (bf16[20,24,384]{2,1,0:T(8,128)(2,1)S(1)}, bf16[20,24,384]{2,1,0:T(8,128)(2,1)S(1)}, u32[]{:S(2)}, u32[]{:S(2)}) collective-permute-start(bf16[20,24,384]{2,1,0:T(8,128)(2,1)S(1)} %collective-permute-done.4.n1), channel_id=1, source_target_pairs={{0,1},{1,2},{2,3},{3,0},{4,7},{5,4},{6,5},{7,6},{8,9},{9,10},{10,1... | collective-permute-start | bytes 1105928 | tf_op jit(solution)/shard_map/ppermute | solution.py:436
  129.6 6.6 %collective-permute-start.7 = (bf16[64,16,128]{2,1,0:T(8,128)(2,1)S(1)}, bf16[64,16,128]{2,1,0:T(8,128)(2,1)S(1)}, u32[]{:S(2)}, u32[]{:S(2)}) collective-permute-start(bf16[64,16,128]{2,1,0:T(8,128)(2,1)S(1)} %all_to_all.23.mine), channel_id=1, source_target_pairs={{0,4},{4,0},{1,5},{5,1},{2,6},{6,2},{3,7},{7,3},{8,12},{12,8},{9,1... | collective-permute-start | bytes 786440 | tf_op jit(solution)/shard_map/ppermute | solution.py:430

commit v6 on v5

--- a/solution.py
+++ b/solution.py
@@ -250,11 +250,11 @@
         )
         left = jnp.concatenate([p.reshape(128, 128).astype(BF16) for p in pieces], axis=1)
         packed = jnp.dot(left, maps[...], preferred_element_type=F32)
-        out[t : t + 16, :, :] = packed.reshape(16, 8, 128)
+        out[t : t + 16, :, :] = packed.reshape(16, 8, 128).astype(BF16)
 
 
 def gram_call(targets, loc, precision, maps, innov, rows, p2):
-    packed = jax.ShapeDtypeStruct((2 * CHIPS, 8, 128), F32)
+    packed = jax.ShapeDtypeStruct((2 * CHIPS, 8, 128), BF16)
     return pl.pallas_call(
         gram_kernel,
         out_shape=(packed, jax.ShapeDtypeStruct((OBS, SPAN, WIDE), BF16)),
@@ -485,7 +485,7 @@
         across,
     )
     arrived = lax.all_to_all(
-        packed.astype(BF16), ("y", "z", "core"), split_axis=0, concat_axis=0, tiled=True
+        packed, ("y", "z", "core"), split_axis=0, concat_axis=0, tiled=True
     )
     gathered = to_groups(jnp.sum(arrived.astype(F32), axis=0))
     weights = root_call(place, gathered)

time: 139 us -> 139 us (level)
  no operation moved by 1% of the time
where the time goes in v6:
time: 139 us; the launch traced here: 138 us
  blocking collectives  65.8 us (47%)
  starting transfers between devices  40.1 us (29%)
  Pallas kernels  15.3 us (11%)
  waiting for transfers between devices  10.9 us (8%)
  local copies, waits for them, and re-layouts  4.33 us (3%)
  matrix products  1.4 us (1%)
    all_to_all x1, blocking collectives, body(): lax.all_to_all(packed, ('y', 'z', 'core'), split_axis=0, concat_axis=0, t...  33 us
    ppermute x3, starting transfers between devices, swap(): return lax.ppermute(value, 'core', [(0, 1), (1, 0)])  20.8 us
    ppermute x5, starting transfers between devices, turn(): return lax.ppermute(value, ('core', 'mem'), pairs)  19.3 us
    all_to_all x1, blocking collectives, body(): lax.all_to_all(jnp.broadcast_to(weights[None], (CHIPS, 16, 128)), ('y', '...  17.2 us
    all_to_all x2, blocking collectives, to_groups(): lax.all_to_all(copies, 'mem', split_axis=0, concat_axis=0, tiled=True)  15.6 us
    ppermute x5, waiting for transfers between devices, turn(): return lax.ppermute(value, ('core', 'mem'), pairs)  8.68 us
    pallas_call x1, Pallas kernels, gram_call(): pl.pallas_call(gram_kernel, out_shape=(packed, jax.ShapeDtypeStruct((OBS,...  3.26 us
    pallas_call x1, Pallas kernels, root_call(): pl.pallas_call(root_kernel, out_shape=jax.ShapeDtypeStruct((16, 128), BF1...  2.96 us
  transfers between devices with their start and end apart: 8, of which 5 were waited for; matrix products, arithmetic and copies ran while one was open for 2% of the time, Pallas kernels for 3%

profile of v6, /device:TPU:1, one launch (start us, length us, event | category | flops | bytes accessed | tf_op | source)
XLA Modules:
  0.0 138.4 jit_solution(1524714281937508569)
XLA Ops:
  0.0 1.4 %pad_dynamic-slice_fusion.own = bf16[304,1152]{1,0:T(8,128)(2,1)S(1)} fusion(s32[]{:T(128)S(6)} %select_n.16, bf16[300,1088]{1,0:T(8,128)(2,1)} %bitcast.14), kind=kLoop, calls=%fused_computation | loop fusion | bytes 1353220 | tf_op jit(solution)/shard_map/dynamic_slice | solution.py:458
  1.5 5.2 %collective-permute-start = (bf16[304,1152]{1,0:T(8,128)(2,1)S(1)}, bf16[304,1152]{1,0:T(8,128)(2,1)S(1)}, u32[]{:S(2)}, u32[]{:S(2)}) collective-permute-start(bf16[304,1152]{1,0:T(8,128)(2,1)S(1)} %pad_dynamic-slice_fusion.own), channel_id=1, source_target_pairs={{0,1},{1,2},{2,3},{3,0},{4,7},{5,4},{6,5},{7,6},{8,9},{9,10},{10,1... | collective-permute-start | bytes 2101256 | tf_op jit(solution)/shard_map/ppermute | solution.py:436
  6.7 1.4 %fusion.2 = f32[24,300]{1,0:T(8,128)S(1)} fusion(bf16[24,1088]{1,0:T(8,128)(2,1)S(1)} %copy-done, bf16[1088,300]{0,1:T(8,128)(2,1)} %param.10), kind=kOutput, calls=%fused_computation.10 | convolution fusion | flops 15667200 | bytes 733824 | tf_op jit(solution)/shard_map/dot_general | solution.py:461
  8.2 2.2 %copy-done.1 = bf16[24,20,4352]{2,0,1:T(8,128)(2,1)S(1)} copy-done((bf16[24,20,4352]{2,0,1:T(8,128)(2,1)S(1)}, bf16[24,20,4352]{2,0,1:T(8,128)(2,1)}, u32[]{:S(2)}) %copy-start.1) | copy-done | bytes 4177944
  10.4 1.3 scores_own.1.first
  11.7 3.0 %collective-permute-done.beside1 = bf16[304,1152]{1,0:T(8,128)(2,1)S(1)} collective-permute-done((bf16[304,1152]{1,0:T(8,128)(2,1)S(1)}, bf16[304,1152]{1,0:T(8,128)(2,1)S(1)}, u32[]{:S(2)}, u32[]{:S(2)}) %collective-permute-start) | collective-permute-done | bytes 700448 | tf_op jit(solution)/shard_map/ppermute | solution.py:436
  14.8 5.2 %collective-permute-start.2 = (bf16[160,1152]{1,0:T(8,128)(2,1)S(1)}, bf16[160,1152]{1,0:T(8,128)(2,1)S(1)}, u32[]{:S(2)}, u32[]{:S(2)}) collective-permute-start(bf16[160,1152]{1,0:T(8,128)(2,1)S(1)} %constant_dynamic-slice_fusion), channel_id=1, source_target_pairs={{0,1},{1,2},{2,3},{3,0},{4,7},{5,4},{6,5},{7,6},{8,9},{9,10},{10,1... | collective-permute-start | bytes 1105928 | tf_op jit(solution)/shard_map/ppermute | solution.py:436
  19.9 6.6 %collective-permute-start.1 = (bf16[304,1152]{1,0:T(8,128)(2,1)S(1)}, bf16[304,1152]{1,0:T(8,128)(2,1)S(1)}, u32[]{:S(2)}, u32[]{:S(2)}) collective-permute-start(bf16[304,1152]{1,0:T(8,128)(2,1)S(1)} %collective-permute-done.beside1), channel_id=1, source_target_pairs={{0,4},{4,0},{1,5},{5,1},{2,6},{6,2},{3,7},{7,3},{8,12},{12,8},{9,1... | collective-permute-start | bytes 2101256 | tf_op jit(solution)/shard_map/ppermute | solution.py:430
  26.6 8.7 %collective-permute-start.3 = (bf16[160,1152]{1,0:T(8,128)(2,1)S(1)}, bf16[160,1152]{1,0:T(8,128)(2,1)S(1)}, u32[]{:S(2)}, u32[]{:S(2)}) collective-permute-start(bf16[160,1152]{1,0:T(8,128)(2,1)S(1)} %collective-permute-done.2.far1), channel_id=1, source_target_pairs={{0,4},{4,0},{1,5},{5,1},{2,6},{6,2},{3,7},{7,3},{8,12},{12,8},{9,1... | collective-permute-start | bytes 1105928 | tf_op jit(solution)/shard_map/ppermute | solution.py:430
  35.3 1.3 collective-permute-done.3.far2
  36.5 2.7 %scores.1 = (f32[20,24,304]{2,1,0:T(8,128)S(1)}, f32[24,304]{1,0:T(8,128)S(1)}) custom-call(s32[2]{0:T(128)S(1)} %pad_add_fusion.place, bf16[480,4352]{1,0:T(8,128)(2,1)S(1)} %bitcast.12, f32[480,304]{1,0:T(8,128)S(1)} %scores_own.1.first, bf16[304,1152]{1,0:T(8,128)(2,1)S(1)} %collective-permute-done.beside1, ...), custom_call_target="tpu_custom_call" | custom-call | tf_op jit(solution)/shard_map/scores/pallas_call | solution.py:99
  39.3 9.0 %all_to_all.20.parts = f32[4,2,24,304]{3,2,1,0:T(8,128)S(1)} all-to-all(f32[4,2,24,304]{3,2,1,0:T(8,128)S(1)} %broadcast_in_dim.9), channel_id=1, replica_groups=mesh['y'=8,'z'=8,'core'=2,'mem'=4] {'mem'}, dimensions={0} | all-to-all | bytes 466944 | tf_op jit(solution)/shard_map/all_to_all | solution.py:441
  48.3 2.8 %collective-permute-start.4 = (bf16[20,24,384]{2,1,0:T(8,128)(2,1)S(1)}, bf16[20,24,384]{2,1,0:T(8,128)(2,1)S(1)}, u32[]{:S(2)}, u32[]{:S(2)}) collective-permute-start(bf16[20,24,384]{2,1,0:T(8,128)(2,1)S(1)} %get-tuple-element.21.own), channel_id=1, source_target_pairs={{0,1},{1,2},{2,3},{3,0},{4,7},{5,4},{6,5},{7,6},{8,9},{9,10},{10,1... | collective-permute-start | bytes 1105928 | tf_op jit(solution)/shard_map/ppermute | solution.py:436
  51.2 2.5 %collective-permute-start.5 = (bf16[20,24,384]{2,1,0:T(8,128)(2,1)S(1)}, bf16[20,24,384]{2,1,0:T(8,128)(2,1)S(1)}, u32[]{:S(2)}, u32[]{:S(2)}) collective-permute-start(bf16[20,24,384]{2,1,0:T(8,128)(2,1)S(1)} %get-tuple-element.21.own), channel_id=1, source_target_pairs={{0,3},{1,0},{2,1},{3,2},{4,5},{5,6},{6,7},{7,4},{8,11},{9,8},{10,9... | collective-permute-start | bytes 1105928 | tf_op jit(solution)/shard_map/ppermute | solution.py:436
  53.7 3.2 %collective-permute-done.4.n1 = bf16[20,24,384]{2,1,0:T(8,128)(2,1)S(1)} collective-permute-done((bf16[20,24,384]{2,1,0:T(8,128)(2,1)S(1)}, bf16[20,24,384]{2,1,0:T(8,128)(2,1)S(1)}, u32[]{:S(2)}, u32[]{:S(2)}) %collective-permute-start.4) | collective-permute-done | bytes 368672 | tf_op jit(solution)/shard_map/ppermute | solution.py:436
  56.9 3.7 %collective-permute-start.6 = (bf16[20,24,384]{2,1,0:T(8,128)(2,1)S(1)}, bf16[20,24,384]{2,1,0:T(8,128)(2,1)S(1)}, u32[]{:S(2)}, u32[]{:S(2)}) collective-permute-start(bf16[20,24,384]{2,1,0:T(8,128)(2,1)S(1)} %collective-permute-done.4.n1), channel_id=1, source_target_pairs={{0,1},{1,2},{2,3},{3,0},{4,7},{5,4},{6,5},{7,6},{8,9},{9,10},{10,1... | collective-permute-start | bytes 1105928 | tf_op jit(solution)/shard_map/ppermute | solution.py:436
  60.7 0.1 reshape.18.loc
  60.8 0.1 copy.12
  60.9 0.1 reshape.16.targets
  61.0 2.5 %collective-permute-done.5.n2 = bf16[20,24,384]{2,1,0:T(8,128)(2,1)S(1)} collective-permute-done((bf16[20,24,384]{2,1,0:T(8,128)(2,1)S(1)}, bf16[20,24,384]{2,1,0:T(8,128)(2,1)S(1)}, u32[]{:S(2)}, u32[]{:S(2)}) %collective-permute-start.5) | collective-permute-done | bytes 368672 | tf_op jit(solution)/shard_map/ppermute | solution.py:436
  63.5 2.8 %lay.1.rows = f32[3,1536,128]{2,1,0:T(8,128)S(1)} custom-call(s32[2]{0:T(128)S(1)} %pad_add_fusion.place, bf16[20,24,384]{2,1,0:T(8,128)(2,1)S(1)} %get-tuple-element.21.own, bf16[20,24,384]{2,1,0:T(8,128)(2,1)S(1)} %collective-permute-done.4.n1, bf16[20,24,384]{2,1,0:T(8,128)(2,1)S(1)} %collective-permute-done.5.n2), custom_call_target="tpu_custom_call" | custom-call | flops 1000000 | bytes 6000000 | tf_op jit(solution)/shard_map/lay/pallas_call | solution.py:163
  66.3 3.3 %gram.1 = (bf16[128,8,128]{2,1,0:T(8,128)(2,1)S(1)}, bf16[24,96,384]{2,1,0:T(8,128)(2,1)S(1)}) custom-call(s32[72]{0:T(128)S(1)} %reshape.16.targets, f32[72]{0:T(128)S(1)} %reshape.18.loc, f32[1,384]{1,0:T(1,128)S(1)} %pad.12.precision, bf16[768,128]{1,0:T(8,128)(2,1)S(1)} %broadcast_select_fusion.maps, bf16[24,384]{1,0:T(8,128)(2,1)S(1)} %get-tuple-element.20.innov, ...), custom_call_target="tpu_custom_call" | custom-call | tf_op jit(solution)/shard_map/gram/pallas_call | solution.py:258
  69.6 33.0 %all_to_all.21 = bf16[128,8,128]{2,1,0:T(8,128)(2,1)S(1)} all-to-all(bf16[128,8,128]{2,1,0:T(8,128)(2,1)S(1)} %get-tuple-element.22), channel_id=1, replica_groups=mesh['y'=8,'z'=8,'core'=2,'mem'=4] {'y','z','core'}, dimensions={0} | all-to-all | bytes 524288 | tf_op jit(solution)/shard_map/all_to_all | solution.py:487
  102.7 0.1 convert_reduce_fusion
  102.8 6.6 %all_to_all.22.gathered = f32[4,8,128]{2,1,0:T(8,128)S(1)} all-to-all(f32[4,8,128]{2,1,0:T(8,128)S(1)} %broadcast_in_dim.10), channel_id=1, replica_groups=mesh['y'=8,'z'=8,'core'=2,'mem'=4] {'mem'}, dimensions={0} | all-to-all | bytes 32768 | tf_op jit(solution)/shard_map/all_to_all | solution.py:441
  109.4 3.0 %root.1 = bf16[16,128]{1,0:T(8,128)(2,1)S(1)} custom-call(s32[2]{0:T(128)S(1)} %pad_add_fusion.place, f32[4,8,128]{2,1,0:T(8,128)S(1)} %all_to_all.22.gathered), custom_call_target="tpu_custom_call" | custom-call | tf_op jit(solution)/shard_map/root/pallas_call | solution.py:355
  112.4 17.2 %all_to_all.23.mine = bf16[64,16,128]{2,1,0:T(8,128)(2,1)S(1)} all-to-all(bf16[64,16,128]{2,1,0:T(8,128)(2,1)S(1)} %broadcast_in_dim.11), channel_id=1, replica_groups=mesh['y'=8,'z'=8,'core'=2,'mem'=4] {'y','z'}, dimensions={0} | all-to-all | bytes 524288 | tf_op jit(solution)/shard_map/all_to_all | solution.py:492
  129.6 5.5 %collective-permute-start.7 = (bf16[64,16,128]{2,1,0:T(8,128)(2,1)S(1)}, bf16[64,16,128]{2,1,0:T(8,128)(2,1)S(1)}, u32[]{:S(2)}, u32[]{:S(2)}) collective-permute-start(bf16[64,16,128]{2,1,0:T(8,128)(2,1)S(1)} %all_to_all.23.mine), channel_id=1, source_target_pairs={{0,4},{4,0},{1,5},{5,1},{2,6},{6,2},{3,7},{7,3},{8,12},{12,8},{9,1... | collective-permute-start | bytes 786440 | tf_op jit(solution)/shard_map/ppermute | solution.py:430
  135.1 0.1 copy.13
  135.2 0.1 reshape.17.coef
  135.3 1.0 collective-permute-done.7.other
  136.2 2.2 %mix.1 = bf16[20,24,300]{2,1,0:T(8,128)(2,1)} custom-call(s32[2]{0:T(128)S(1)} %pad_add_fusion.place, s32[72]{0:T(128)S(1)} %reshape.16.targets, f32[72]{0:T(128)S(1)} %reshape.17.coef, bf16[64,16,128]{2,1,0:T(8,128)(2,1)S(1)} %all_to_all.23.mine, bf16[64,16,128]{2,1,0:T(8,128)(2,1)S(1)} %collective-permute-done.7.other, ...), custom_call_target="tpu_custom_call" | custom-call | tf_op jit(solution)/shard_map/mix/pallas_call | solution.py:418
  (30 shorter events, 0.5 us)
Async XLA Ops:
  0.0 6.7 %copy-start = (bf16[24,1088]{1,0:T(8,128)(2,1)S(1)}, bf16[24,1088]{1,0:T(8,128)(2,1)}, u32[]{:S(2)}) copy-start(bf16[24,1088]{1,0:T(8,128)(2,1)} %param.9) | copy-start | bytes 156676
  1.5 13.2 %collective-permute-start = (bf16[304,1152]{1,0:T(8,128)(2,1)S(1)}, bf16[304,1152]{1,0:T(8,128)(2,1)S(1)}, u32[]{:S(2)}, u32[]{:S(2)}) collective-permute-start(bf16[304,1152]{1,0:T(8,128)(2,1)S(1)} %pad_dynamic-slice_fusion.own), channel_id=1, source_target_pairs={{0,1},{1,2},{2,3},{3,0},{4,7},{5,4},{6,5},{7,6},{8,9},{9,10},{10,1... | collective-permute-start | bytes 2101256 | tf_op jit(solution)/shard_map/ppermute | solution.py:436
  8.2 2.2 %copy-start.1 = (bf16[24,20,4352]{2,0,1:T(8,128)(2,1)S(1)}, bf16[24,20,4352]{2,0,1:T(8,128)(2,1)}, u32[]{:S(2)}) copy-start(bf16[24,20,4352]{2,0,1:T(8,128)(2,1)} %param.8) | copy-start | bytes 12533764
  14.7 36.4 %copy-start.6 = (f32[300]{0:T(512)S(1)}, f32[300]{0:T(512)}, u32[]{:S(2)}) copy-start(f32[300]{0:T(512)} %param.11) | copy-start | bytes 3604
  14.7 36.5 %copy-start.4 = (s32[24,3]{0,1:T(4,128)S(1)}, s32[24,3]{0,1:T(4,128)}, u32[]{:S(2)}) copy-start(s32[24,3]{0,1:T(4,128)} %param.13) | copy-start | bytes 868
  14.7 46.1 %copy-start.5 = (s32[24,3]{0,1:T(4,128)S(1)}, s32[24,3]{0,1:T(4,128)}, u32[]{:S(2)}) copy-start(s32[24,3]{0,1:T(4,128)} %param.12) | copy-start | bytes 868
  14.7 46.2 %copy-start.2 = (bf16[768,128]{1,0:T(8,128)(2,1)S(1)}, bf16[768,128]{1,0:T(8,128)(2,1)}, u32[]{:S(2)}) copy-start(bf16[768,128]{1,0:T(8,128)(2,1)} %constant.41.clone) | copy-start | bytes 589828
  14.8 46.2 %copy-start.3 = (bf16[768,128]{1,0:T(8,128)(2,1)S(1)}, bf16[768,128]{1,0:T(8,128)(2,1)}, u32[]{:S(2)}) copy-start(bf16[768,128]{1,0:T(8,128)(2,1)} %constant.40.clone) | copy-start | bytes 589828
  14.8 11.8 %collective-permute-start.2 = (bf16[160,1152]{1,0:T(8,128)(2,1)S(1)}, bf16[160,1152]{1,0:T(8,128)(2,1)S(1)}, u32[]{:S(2)}, u32[]{:S(2)}) collective-permute-start(bf16[160,1152]{1,0:T(8,128)(2,1)S(1)} %constant_dynamic-slice_fusion), channel_id=1, source_target_pairs={{0,1},{1,2},{2,3},{3,0},{4,7},{5,4},{6,5},{7,6},{8,9},{9,10},{10,1... | collective-permute-start | bytes 1105928 | tf_op jit(solution)/shard_map/ppermute | solution.py:436
  19.9 15.3 %collective-permute-start.1 = (bf16[304,1152]{1,0:T(8,128)(2,1)S(1)}, bf16[304,1152]{1,0:T(8,128)(2,1)S(1)}, u32[]{:S(2)}, u32[]{:S(2)}) collective-permute-start(bf16[304,1152]{1,0:T(8,128)(2,1)S(1)} %collective-permute-done.beside1), channel_id=1, source_target_pairs={{0,4},{4,0},{1,5},{5,1},{2,6},{6,2},{3,7},{7,3},{8,12},{12,8},{9,1... | collective-permute-start | bytes 2101256 | tf_op jit(solution)/shard_map/ppermute | solution.py:430
  26.6 10.0 %collective-permute-start.3 = (bf16[160,1152]{1,0:T(8,128)(2,1)S(1)}, bf16[160,1152]{1,0:T(8,128)(2,1)S(1)}, u32[]{:S(2)}, u32[]{:S(2)}) collective-permute-start(bf16[160,1152]{1,0:T(8,128)(2,1)S(1)} %collective-permute-done.2.far1), channel_id=1, source_target_pairs={{0,4},{4,0},{1,5},{5,1},{2,6},{6,2},{3,7},{7,3},{8,12},{12,8},{9,1... | collective-permute-start | bytes 1105928 | tf_op jit(solution)/shard_map/ppermute | solution.py:430
  48.3 8.6 %collective-permute-start.4 = (bf16[20,24,384]{2,1,0:T(8,128)(2,1)S(1)}, bf16[20,24,384]{2,1,0:T(8,128)(2,1)S(1)}, u32[]{:S(2)}, u32[]{:S(2)}) collective-permute-start(bf16[20,24,384]{2,1,0:T(8,128)(2,1)S(1)} %get-tuple-element.21.own), channel_id=1, source_target_pairs={{0,1},{1,2},{2,3},{3,0},{4,7},{5,4},{6,5},{7,6},{8,9},{9,10},{10,1... | collective-permute-start | bytes 1105928 | tf_op jit(solution)/shard_map/ppermute | solution.py:436
  51.2 12.3 %collective-permute-start.5 = (bf16[20,24,384]{2,1,0:T(8,128)(2,1)S(1)}, bf16[20,24,384]{2,1,0:T(8,128)(2,1)S(1)}, u32[]{:S(2)}, u32[]{:S(2)}) collective-permute-start(bf16[20,24,384]{2,1,0:T(8,128)(2,1)S(1)} %get-tuple-element.21.own), channel_id=1, source_target_pairs={{0,3},{1,0},{2,1},{3,2},{4,5},{5,6},{6,7},{7,4},{8,11},{9,8},{10,9... | collective-permute-start | bytes 1105928 | tf_op jit(solution)/shard_map/ppermute | solution.py:436
  56.9 9.5 %collective-permute-start.6 = (bf16[20,24,384]{2,1,0:T(8,128)(2,1)S(1)}, bf16[20,24,384]{2,1,0:T(8,128)(2,1)S(1)}, u32[]{:S(2)}, u32[]{:S(2)}) collective-permute-start(bf16[20,24,384]{2,1,0:T(8,128)(2,1)S(1)} %collective-permute-done.4.n1), channel_id=1, source_target_pairs={{0,1},{1,2},{2,3},{3,0},{4,7},{5,4},{6,5},{7,6},{8,9},{9,10},{10,1... | collective-permute-start | bytes 1105928 | tf_op jit(solution)/shard_map/ppermute | solution.py:436
  129.6 6.6 %collective-permute-start.7 = (bf16[64,16,128]{2,1,0:T(8,128)(2,1)S(1)}, bf16[64,16,128]{2,1,0:T(8,128)(2,1)S(1)}, u32[]{:S(2)}, u32[]{:S(2)}) collective-permute-start(bf16[64,16,128]{2,1,0:T(8,128)(2,1)S(1)} %all_to_all.23.mine), channel_id=1, source_target_pairs={{0,4},{4,0},{1,5},{5,1},{2,6},{6,2},{3,7},{7,3},{8,12},{12,8},{9,1... | collective-permute-start | bytes 786440 | tf_op jit(solution)/shard_map/ppermute | solution.py:430
